TPU v7x, 32 devices: a whole 2x2x4 slice. The times are simulated.
32 devices in a mesh: gx: 4 (over z), gy: 8 (over y, x, core).
Axes of the slice: x: 2, y: 2, z: 4, core: 2. Of those that a mesh axis runs over, the one named last changes fastest.
Arguments:
- initial_guess: float32 [128, 128, 128], P('gx', 'gy'), may hold values from -6 to 6
- source: float32 [128, 128, 128], P('gx', 'gy'), may hold values from -12 to 12
- leaf_density: float32 [128, 128, 16], P('gx', 'gy'), may hold values from 0 to 4
- absorption: float32 [128, 128, 16], P('gx', 'gy'), may hold values from 0.5 to 2.5
Outputs:
- solution: float32 [128, 128, 128], P('gx', 'gy')
- residual: float32 [128, 128, 128], P('gx', 'gy')
All inputs are finite; a program needn't handle non-finite values.
Results may differ from a plain program's by a relative error of at most 0.0003.
Values sent between devices are 32-bit elements; how exact they have to be, the bound alone decides.
No kernel may reach another device: no remote copies, remote signals or barrier semaphores. Data moves between devices by JAX's collectives and lax.ppermute only.
A program may use at most 128 MiB of HBM per device.

v0:
```python
import functools

import jax
import jax.numpy as jnp
import numpy as np
from jax import lax
from jax.experimental import pallas as pl
from jax.experimental.pallas import tpu as pltpu
from jax.sharding import PartitionSpec as P

NRHS = 8
S = 8
DEEP = S
LANES = 128

PEAK_COND = 0.6
CENTRE = 10.3
HALF_WIDTH = 9.8
RIDGE = 0.05
HIGHEST = lax.Precision.HIGHEST
VMEM_BYTES = 48 * 1024 * 1024


def lanes_of(shape):
    return lax.broadcasted_iota(jnp.int32, shape, len(shape) - 1)


def rows_at(shape):
    return lax.broadcasted_iota(jnp.int32, shape, len(shape) - 2)


def z_sum(f):
    lane = lanes_of(f.shape)
    ax = f.ndim - 1
    up = jnp.where(lane >= NRHS, pltpu.roll(f, NRHS, ax), 0.0)
    down = jnp.where(lane < LANES - NRHS, pltpu.roll(f, LANES - NRHS, ax), 0.0)
    return up + down


def row_sum(f):
    n = f.shape[-2]
    ax = f.ndim - 2
    return pltpu.roll(f, 1, ax) + pltpu.roll(f, n - 1, ax)


def row_sum_zero(f):
    n = f.shape[-2]
    ax = f.ndim - 2
    row = rows_at(f.shape)
    up = jnp.where(row >= 1, pltpu.roll(f, 1, ax), 0.0)
    down = jnp.where(row < n - 1, pltpu.roll(f, n - 1, ax), 0.0)
    return up + down


def slab_sum(before, here, after, rows):
    ux = before[0] + after[0]
    px = before[1] + after[1]
    s = here[1] + ux
    q = here[0] + 0.5 * s + (1.0 / 3.0) * px
    return s + 0.5 * px + rows(q)


def cross_sum(f, rows):
    p = z_sum(f)
    return f + 0.5 * p + rows(0.5 * f + (1.0 / 3.0) * p)


def select(shape, rule):
    row = lax.broadcasted_iota(jnp.int32, shape, 0)
    col = lax.broadcasted_iota(jnp.int32, shape, 1)
    return jnp.where(rule(row, col), 1.0, 0.0).astype(jnp.float32)


def exact(a, b):
    return jnp.dot(a, b, precision=HIGHEST, preferred_element_type=jnp.float32)


def unpack_matrix(quarter, part, depth):
    base = quarter * 2 * depth + part * depth
    return select((LANES, LANES), lambda r, c: r == base + c // NRHS)


def pack_matrix(quarter, part, depth):
    base = quarter * 2 * depth + part * depth
    return select((LANES, LANES), lambda r, c: (r % NRHS == 0) & (c == base + r // NRHS))


def begin_kernel(px, guess, source, ra, root_o, abs_o, b0_o, send_a, send_b):
    nx, ny, _ = guess.shape
    depth = ra.shape[2] // 2
    flat = ra[...].reshape(nx * ny, 2 * depth)
    for part, out in ((0, root_o), (1, abs_o)):
        spread = select((2 * depth, LANES), lambda r, c: r == part * depth + c // NRHS)
        out[...] = exact(flat, spread).reshape(nx, ny, LANES)
    zero = jnp.zeros((ny, LANES), jnp.float32)

    def pair(x, field):
        if x < 0 or x >= nx:
            return (zero, zero)
        u = root_o[x] if field is None else root_o[x] * field[x]
        return (u, z_sum(u))

    moving = [pair(-1, guess), pair(0, guess)]
    still = [pair(-1, None), pair(0, None)]
    for x in range(nx):
        moving.append(pair(x + 1, guess))
        still.append(pair(x + 1, None))
        wu = slab_sum(*moving, row_sum_zero)
        wr = slab_sum(*still, row_sum_zero)
        moving, still = moving[1:], still[1:]
        v = guess[x]
        b0_o[x] = source[x] - abs_o[x] * v + root_o[x] * (wu - v * wr)

    def write(out, x0, face, beyond):
        n = DEEP * ny
        out[0:n] = b0_o[x0 : x0 + DEEP].reshape(n, LANES)
        out[n : n + ny] = guess[face]
        n += ny
        for col in (0, ny - 1):
            out[n : n + DEEP] = guess[x0 : x0 + DEEP, col, :]
            n += DEEP
        out[n : n + 8] = jnp.zeros((8, LANES), jnp.float32)
        for at, col in ((0, 0), (1, ny - 1)):
            out[n + at : n + at + 1] = guess[beyond, col : col + 1, :]
            out[n + 2 + at : n + 3 + at] = root_o[beyond, col : col + 1, :]
        n += 8
        group = DEEP // 4
        packed = jnp.zeros((group * ny, LANES), jnp.float32)
        for q in range(4):
            place = select((2 * depth, LANES), lambda r, c: c == q * 2 * depth + r)
            part = ra[x0 + q * group : x0 + (q + 1) * group].reshape(group * ny, 2 * depth)
            packed = packed + exact(part, place)
        out[n : n + group * ny] = packed

    @pl.when(px[0] == 0)
    def _():
        write(send_a, nx - DEEP, nx - 1, nx - DEEP - 1)
        write(send_b, 0, 0, DEEP)

    @pl.when(px[0] == 1)
    def _():
        write(send_b, nx - DEEP, nx - 1, nx - DEEP - 1)
        write(send_a, 0, 0, DEEP)


def widen_kernel(
    px, py, recv_a, recv_b, guess, root, absb, b0, rootx, absx, b0x, edge, send_a, send_b, face
):
    nx, ny, _ = guess.shape
    wide = nx + 2 * DEEP
    depth = LANES // NRHS
    rootx[DEEP : DEEP + nx] = root[...]
    absx[DEEP : DEEP + nx] = absb[...]
    b0x[DEEP : DEEP + nx] = b0[...]
    for at, col in ((0, 0), (1, ny - 1)):
        edge[at, DEEP : DEEP + nx] = guess[:, col, :]
        edge[at, wide : wide + 8] = jnp.zeros((8, LANES), jnp.float32)

    def read(msg, x0, side):
        n = DEEP * ny
        b0x[x0 : x0 + DEEP] = msg[0:n].reshape(DEEP, ny, LANES)
        face[side] = msg[n : n + ny]
        n += ny
        for at in (0, 1):
            edge[at, x0 : x0 + DEEP] = msg[n : n + DEEP]
            n += DEEP
        for at in (0, 1):
            edge[at, wide + side : wide + side + 1] = msg[n + at : n + at + 1]
            edge[at, wide + 2 + side : wide + 3 + side] = msg[n + 2 + at : n + 3 + at]
        n += 8
        group = DEEP // 4
        packed = msg[n : n + group * ny]
        for q in range(4):
            for part, out in ((0, rootx), (1, absx)):
                got = exact(packed, unpack_matrix(q, part, depth))
                out[x0 + q * group : x0 + (q + 1) * group] = got.reshape(group, ny, LANES)

    @pl.when(px[0] == 0)
    def _():
        read(recv_b, 0, 0)
        read(recv_a, DEEP + nx, 1)

    @pl.when(px[0] == 1)
    def _():
        read(recv_a, 0, 0)
        read(recv_b, DEEP + nx, 1)

    for side, out_x, in_x, own in ((0, DEEP - 1, DEEP, 0), (1, DEEP + nx, DEEP + nx - 1, nx - 1)):
        va, ra = face[side], rootx[out_x]
        vb, rb = guess[own], rootx[in_x]
        fix_a = ra * (cross_sum(rb * vb, row_sum_zero) - va * cross_sum(rb, row_sum_zero))
        fix_b = rb * (cross_sum(ra * va, row_sum_zero) - vb * cross_sum(ra, row_sum_zero))
        b0x[out_x] = b0x[out_x] + fix_a
        b0x[in_x] = b0x[in_x] + fix_b

    def write(out, y0, at):
        n = wide * DEEP
        out[0:n] = b0x[:, y0 : y0 + DEEP, :].reshape(n, LANES)
        out[n : n + wide + 8] = edge[at]
        n += wide + 8
        group = wide // 4
        packed = jnp.zeros((group * DEEP, LANES), jnp.float32)
        for q in range(4):
            for part, field in ((0, rootx), (1, absx)):
                some = field[q * group : (q + 1) * group, y0 : y0 + DEEP, :]
                packed = packed + exact(
                    some.reshape(group * DEEP, LANES), pack_matrix(q, part, depth)
                )
        out[n : n + group * DEEP] = packed

    @pl.when(py[0] == 0)
    def _():
        write(send_a, ny - DEEP, 1)
        write(send_b, 0, 0)

    @pl.when(py[0] == 1)
    def _():
        write(send_b, ny - DEEP, 1)
        write(send_a, 0, 0)


def halves(a):
    high = a.astype(jnp.bfloat16)
    return high, (a - high.astype(jnp.float32)).astype(jnp.bfloat16)


def dot_t(a, b):
    return lax.dot_general(a, b, (((0,), (0,)), ((), ())), preferred_element_type=jnp.float32)


def basis_kernel(
    py, recv_a, recv_b, rootx, absx, b0x, edge, basis, moments, root, diag, far, f0, f1, f2
):
    wide, ny, _ = b0x.shape
    nx = wide - 2 * DEEP
    tall = ny + 2 * DEEP
    depth = LANES // NRHS
    root[:, DEEP : DEEP + ny, :] = rootx[...]
    diag[:, DEEP : DEEP + ny, :] = absx[...]
    f0[:, DEEP : DEEP + ny, :] = b0x[...]

    def read(msg, y0, side):
        n = wide * DEEP
        f0[:, y0 : y0 + DEEP, :] = msg[0:n].reshape(wide, DEEP, LANES)
        far[side] = msg[n : n + wide + 8]
        n += wide + 8
        group = wide // 4
        packed = msg[n : n + group * DEEP]
        for q in range(4):
            for part, out in ((0, root), (1, diag)):
                got = exact(packed, unpack_matrix(q, part, depth))
                out[q * group : (q + 1) * group, y0 : y0 + DEEP, :] = got.reshape(
                    group, DEEP, LANES
                )

    @pl.when(py[0] == 0)
    def _():
        read(recv_b, 0, 0)
        read(recv_a, DEEP + ny, 1)

    @pl.when(py[0] == 1)
    def _():
        read(recv_a, 0, 0)
        read(recv_b, DEEP + ny, 1)

    row = lax.broadcasted_iota(jnp.int32, (wide, LANES), 0)

    def across(f, before, after):
        p = z_sum(f)
        ends = jnp.concatenate([before, after], axis=0)
        ends = 0.5 * ends + (1.0 / 3.0) * z_sum(ends)
        g = 0.5 * f + (1.0 / 3.0) * p
        up = jnp.where(row == 0, ends[0:1], pltpu.roll(g, 1, 0))
        down = jnp.where(row == wide - 1, ends[1:2], pltpu.roll(g, wide - 1, 0))
        return f + 0.5 * p + up + down

    def column(ref, at, y):
        v = ref[at, 0:wide]
        ends = ref[at, wide : wide + 8]
        r = root[:, y, :]
        r0, r1 = ends[2:3], ends[3:4]
        return v, r, across(r * v, r0 * ends[0:1], r1 * ends[1:2]), across(r, r0, r1)

    for side, out_y, in_y in ((0, DEEP - 1, DEEP), (1, DEEP + ny, DEEP + ny - 1)):
        va, ra, ua, wa = column(far, side, out_y)
        vb, rb, ub, wb = column(edge, side, in_y)
        f0[:, out_y, :] = f0[:, out_y, :] + ra * (ub - va * wb)
        f0[:, in_y, :] = f0[:, in_y, :] + rb * (ua - vb * wa)

    def pair(src, x):
        u = root[x] if src is None else root[x] * src[x]
        return (u, z_sum(u))

    def sweep(src, lo, hi, put):
        def two(i, carry):
            x = lo + 2 * i
            first, second = carry
            third = pair(src, x + 1)
            put(x, slab_sum(first, second, third, row_sum))
            fourth = pair(src, x + 2)
            put(x + 1, slab_sum(second, third, fourth, row_sum))
            return (third, fourth)

        lax.fori_loop(0, (hi - lo) // 2, two, (pair(src, lo - 1), pair(src, lo)))

    def put_diag(x, total):
        diag[x] = (diag[x] + root[x] * total - CENTRE) * (2.0 / HALF_WIDTH)

    sweep(None, 1, wide - 1, put_diag)

    lane = lanes_of((NRHS, LANES))
    same = select((LANES, LANES), lambda r, c: r // NRHS == c // NRHS)

    def fold(block):
        f = jnp.sum((block * same).reshape(LANES // NRHS, NRHS, LANES), axis=0)
        shift = LANES // 2
        while shift >= NRHS:
            f = f + pltpu.roll(f, shift, 1)
            shift //= 2
        return f

    tile = [jnp.zeros((NRHS, LANES), jnp.float32) for _ in range(2)]

    def note(tile, n, block):
        f = fold(block)
        which, place = divmod(n, LANES // NRHS)
        tile[which] = tile[which] + jnp.where(lane // NRHS == place, f, 0.0)

    frames = [f0, f1, f2]
    old = None
    for j in range(S + 1):
        now = frames[j % 3]
        if j > 0:
            src, prev = frames[(j - 1) % 3], frames[(j - 2) % 3]

            def put(x, total):
                new = diag[x] * src[x] - (2.0 / HALF_WIDTH) * root[x] * total
                now[x] = 0.5 * new if j == 1 else new - prev[x]

            sweep(src, j, wide - j, put)
        own = now[DEEP : DEEP + nx, DEEP : DEEP + ny, :]
        basis[:, :, j * LANES : (j + 1) * LANES] = own
        high, low = halves(own.reshape(nx * ny, LANES))
        note(tile, 2 * j, dot_t(high, high) + dot_t(high, low) + dot_t(low, high))
        if j > 0:
            note(tile, 2 * j - 1, dot_t(high, old[0]) + dot_t(high, old[1]) + dot_t(low, old[0]))
        old = (high, low)
    moments[0:NRHS] = tile[0]
    moments[NRHS : 2 * NRHS] = tile[1]


def combine_kernel(guess, basis, weights, update, rest, wh, wl):
    nx, ny, _ = guess.shape
    spread = select((NRHS, LANES), lambda r, c: r == c % NRHS)
    same = select((LANES, LANES), lambda r, c: r // NRHS == c // NRHS)
    for part in range(2):
        rows = exact(weights[part], spread)
        for j in range(S + 1):
            tile = rows[j * NRHS : (j + 1) * NRHS]
            full = jnp.concatenate([tile] * (LANES // NRHS), axis=0) * same
            high, low = halves(full)
            wh[j * LANES : (j + 1) * LANES, part * LANES : (part + 1) * LANES] = high
            wl[j * LANES : (j + 1) * LANES, part * LANES : (part + 1) * LANES] = low
    chunk = nx // 4
    for i in range(4):
        at = slice(i * chunk, (i + 1) * chunk)
        high, low = halves(basis[at].reshape(chunk * ny, (S + 1) * LANES))
        dot = functools.partial(jnp.dot, preferred_element_type=jnp.float32)
        out = dot(high, wh[...]) + dot(high, wl[...]) + dot(low, wh[...])
        out = out.reshape(chunk, ny, 2 * LANES)
        update[at] = guess[at] + out[:, :, :LANES]
        rest[at] = out[:, :, LANES:]


def call(kernel, ins, outs, scratch=(), scalars=0):
    specs = [pl.BlockSpec(memory_space=pltpu.SMEM)] * scalars
    specs += [pl.BlockSpec(memory_space=pltpu.VMEM)] * (len(ins) - scalars)
    result = pl.pallas_call(
        kernel,
        out_shape=[jax.ShapeDtypeStruct(s, jnp.float32) for s in outs],
        in_specs=specs,
        out_specs=[pl.BlockSpec(memory_space=pltpu.VMEM)] * len(outs),
        scratch_shapes=list(scratch),
        compiler_params=pltpu.CompilerParams(vmem_limit_bytes=VMEM_BYTES),
    )(*ins)
    return result


def exchange(first, second, axis):
    count = lax.axis_size(axis)
    got = []
    for cells, start in ((first, 0), (second, 1)):
        links = []
        for i in range(start, count - 1, 2):
            links += [(i, i + 1), (i + 1, i)]
        got.append(lax.ppermute(cells, axis, links))
    return got


def total_of(x, axis):
    count = lax.axis_size(axis)
    if count & (count - 1):
        return lax.psum(x, axis)
    step = 1
    while step < count:
        x = x + lax.ppermute(x, axis, [(i, i ^ step) for i in range(count)])
        step *= 2
    return x


def krylov_map():
    table = np.zeros((S + 1, S))
    table[0, 0] = CENTRE
    table[1, 0] = HALF_WIDTH
    for column in range(1, S):
        table[column, column] = CENTRE
        table[column - 1, column] = HALF_WIDTH / 2
        table[column + 1, column] = HALF_WIDTH / 2
    return np.kron(table, np.eye(NRHS))


def gram_of(moments):
    raw = [
        moments[(n // 16) * 8 : (n // 16) * 8 + 8, (n % 16) * 8 : (n % 16) * 8 + 8]
        for n in range(2 * S + 1)
    ]
    m = [raw[0], raw[1]] + [2.0 * raw[n] - raw[n % 2] for n in range(2, 2 * S + 1)]
    return jnp.concatenate(
        [
            jnp.concatenate([0.5 * (m[i + j] + m[abs(i - j)]) for j in range(S + 1)], axis=1)
            for i in range(S + 1)
        ],
        axis=0,
    )


def least_squares(gram):
    lift = jnp.asarray(krylov_map(), dtype=gram.dtype)
    normal = jnp.dot(lift.T, jnp.dot(gram, lift, precision=HIGHEST), precision=HIGHEST)
    project = jnp.dot(lift.T, gram[:, :NRHS], precision=HIGHEST)
    scale = 1.0 / jnp.sqrt(jnp.diagonal(normal))
    balanced = scale[:, None] * normal * scale[None, :] + RIDGE * jnp.eye(
        S * NRHS, dtype=gram.dtype
    )
    factor = jnp.linalg.cholesky(balanced)
    coeffs = scale[:, None] * jax.scipy.linalg.cho_solve((factor, True), scale[:, None] * project)
    select_first = jnp.eye((S + 1) * NRHS, dtype=gram.dtype)[:, :NRHS]
    remain = select_first - jnp.dot(lift, coeffs, precision=HIGHEST)
    return (coeffs, remain)


def body(initial_guess, source, leaf_density, absorption):
    nx, ny, lanes = initial_guess.shape
    root = jnp.sqrt(PEAK_COND / (1.0 + leaf_density))
    ra = jnp.concatenate([root, absorption], axis=-1)
    px = lax.rem(lax.axis_index("gx"), 2).astype(jnp.int32).reshape(1)
    py = lax.rem(lax.axis_index("gy"), 2).astype(jnp.int32).reshape(1)
    wide = nx + 2 * DEEP
    tall = ny + 2 * DEEP
    block = (nx, ny, lanes)
    x_rows = DEEP * ny + ny + 2 * DEEP + 8 + DEEP // 4 * ny
    y_rows = wide * DEEP + wide + 8 + wide // 4 * DEEP
    root, absb, b0, xa, xb = call(
        begin_kernel,
        (px, initial_guess, source, ra),
        (block, block, block, (x_rows, lanes), (x_rows, lanes)),
        scalars=1,
    )
    xa, xb = exchange(xa, xb, "gx")
    broad = (wide, ny, lanes)
    rootx, absx, b0x, edge, ya, yb = call(
        widen_kernel,
        (px, py, xa, xb, initial_guess, root, absb, b0),
        (broad, broad, broad, (2, wide + 8, lanes), (y_rows, lanes), (y_rows, lanes)),
        scratch=[pltpu.VMEM((2, ny, lanes), jnp.float32)],
        scalars=2,
    )
    ya, yb = exchange(ya, yb, "gy")
    frame = pltpu.VMEM((wide, tall, lanes), jnp.float32)
    basis, moments = call(
        basis_kernel,
        (py, ya, yb, rootx, absx, b0x, edge),
        ((nx, ny, (S + 1) * lanes), (2 * NRHS, lanes)),
        scratch=[frame, frame, pltpu.VMEM((2, wide + 8, lanes), jnp.float32), frame, frame, frame],
        scalars=1,
    )
    moments = total_of(total_of(moments, "gy"), "gx")
    coeffs, remain = least_squares(gram_of(moments))
    weights = jnp.stack([jnp.pad(coeffs, ((0, NRHS), (0, 0))), remain])
    return call(
        combine_kernel,
        (initial_guess, basis, weights),
        (block, block),
        scratch=[pltpu.VMEM(((S + 1) * lanes, 2 * lanes), jnp.bfloat16)] * 2,
    )


def solution(mesh):
    spec = P("gx", "gy", None)
    return jax.shard_map(
        lambda *arrays: tuple(body(*arrays)),
        mesh=mesh,
        in_specs=(spec,) * 4,
        out_specs=(spec, spec),
        check_vma=False,
    )
```

profile of v0, /device:TPU:0, one launch (start us, length us, event | category | flops | bytes accessed | tf_op | source)
XLA Modules:
  0.0 89.7 jit_solution(9141938479308575367)
XLA Ops:
  0.6 1.1 %copy.21 = f32[32,16,16]{2,1,0:T(8,128)S(1)} copy(f32[32,16,16]{0,2,1:T(8,128)} %param.7) | data formatting | bytes 65536 | tf_op args[2]
  1.8 0.1 divide_sqrt_fusion
  1.9 1.1 %copy.23 = f32[32,16,16]{2,1,0:T(8,128)S(1)} copy(f32[32,16,16]{0,2,1:T(8,128)} %param.8) | data formatting | bytes 65536 | tf_op args[3]
  2.9 0.1 pad_maximum_fusion.ra
  3.1 0.9 %copy-done = f32[32,16,128]{2,1,0:T(8,128)S(1)} copy-done((f32[32,16,128]{2,1,0:T(8,128)S(1)}, f32[32,16,128]{2,1,0:T(8,128)}, u32[]{:S(2)}) %copy-start) | copy-done | bytes 262168
  4.0 0.9 %copy-done.2 = f32[32,16,128]{2,1,0:T(8,128)S(1)} copy-done((f32[32,16,128]{2,1,0:T(8,128)S(1)}, f32[32,16,128]{2,1,0:T(8,128)}, u32[]{:S(2)}) %copy-start.2) | copy-done | bytes 262168
  5.0 1.3 %shard_map.68 = (f32[32,16,128]{2,1,0:T(8,128)S(1)}, f32[32,16,128]{2,1,0:T(8,128)S(1)}, f32[32,16,128]{2,1,0:T(8,128)S(1)}, f32[200,128]{1,0:T(8,128)S(1)}, f32[200,128]{1,0:T(8,128)S(1)}) custom-call(s32[1]{0:T(128)} %bitcast.1.px, f32[32,16,128]{2,1,0:T(8,128)S(1)} %copy-done, f32[32,16,128]{2,1,0:T(8,128)S(1)} %copy-done.2, ...), custom_call_target="tpu_custom_call" | custom-call | tf_op jit(solution)/shard_map/pallas_call | solution.py:378
  6.2 3.0 %collective-permute-start = (f32[200,128]{1,0:T(8,128)S(1)}, f32[200,128]{1,0:T(8,128)S(1)}, u32[]{:S(2)}, u32[]{:S(2)}) collective-permute-start(f32[200,128]{1,0:T(8,128)S(1)} %get-tuple-element.15), channel_id=1, source_target_pairs={{0,8},{8,0},{16,24},{24,16},{1,9},{9,1},{17,25},{25,17},{2,10},{10... | collective-permute-start | bytes 307208 | tf_op jit(solution)/shard_map/ppermute | solution.py:396
  9.3 0.7 collective-permute-start.1
  10.0 2.2 %collective-permute-done.recv_a = f32[200,128]{1,0:T(8,128)S(1)} collective-permute-done((f32[200,128]{1,0:T(8,128)S(1)}, f32[200,128]{1,0:T(8,128)S(1)}, u32[]{:S(2)}, u32[]{:S(2)}) %collective-permute-start) | collective-permute-done | bytes 102432 | tf_op jit(solution)/shard_map/ppermute | solution.py:396
  12.2 2.2 %shard_map.69 = (f32[48,16,128]{2,1,0:T(8,128)S(1)}, f32[48,16,128]{2,1,0:T(8,128)S(1)}, f32[48,16,128]{2,1,0:T(8,128)S(1)}, f32[2,56,128]{2,1,0:T(8,128)S(1)}, ...) custom-call(s32[1]{0:T(128)} %bitcast.1.px, s32[1]{0:T(128)} %bitcast.py, f32[200,128]{1,0:T(8,128)S(1)} %collective-permute-done.recv_a, ...), custom_call_target="tpu_custom_call" | custom-call | tf_op jit(solution)/shard_map/pallas_call | solution.py:378
  14.4 0.7 collective-permute-start.3
  15.1 0.9 collective-permute-done.2.recv_a
  16.0 26.4 %shard_map.70 = (f32[32,16,1152]{2,1,0:T(8,128)S(1)}, f32[16,128]{1,0:T(8,128)S(1)}) custom-call(s32[1]{0:T(128)} %bitcast.py, f32[536,128]{1,0:T(8,128)S(1)} %collective-permute-done.2.recv_a, f32[536,128]{1,0:T(8,128)S(1)} %collective-permute-done.3.recv_b, f32[48,16,128]{2,1,0:T(8,128)S(1)} %get-tuple-element.22.rootx, ...), custom_call_target="tpu_custom_call" | custom-call | tf_op jit(solution)/shard_map/pallas_call | solution.py:378
  42.4 9.3 %collective-permute-start.4 = (f32[16,128]{1,0:T(8,128)S(1)}, f32[16,128]{1,0:T(8,128)S(1)}, u32[]{:S(2)}, u32[]{:S(2)}) collective-permute-start(f32[16,128]{1,0:T(8,128)S(1)} %get-tuple-element.27), channel_id=1, source_target_pairs={{0,1},{1,0},{2,3},{3,2},{4,5},{5,4},{6,7},{7,6},{8,9},{9,8},{10,11... | collective-permute-start | bytes 24584 | tf_op jit(solution)/shard_map/ppermute | solution.py:406
  51.6 0.8 collective-permute-done.4
  52.5 2.4 %collective-permute-start.5 = (f32[16,128]{1,0:T(8,128)S(1)}, f32[16,128]{1,0:T(8,128)S(1)}, u32[]{:S(2)}, u32[]{:S(2)}) collective-permute-start(f32[16,128]{1,0:T(8,128)S(1)} %add.221), channel_id=1, source_target_pairs={{0,2},{1,3},{2,0},{3,1},{4,6},{5,7},{6,4},{7,5},{8,10},{9,11},{10,... | collective-permute-start | bytes 24584 | tf_op jit(solution)/shard_map/ppermute | solution.py:406
  54.9 1.6 %collective-permute-done.5 = f32[16,128]{1,0:T(8,128)S(1)} collective-permute-done((f32[16,128]{1,0:T(8,128)S(1)}, f32[16,128]{1,0:T(8,128)S(1)}, u32[]{:S(2)}, u32[]{:S(2)}) %collective-permute-start.5) | collective-permute-done | bytes 8224 | tf_op jit(solution)/shard_map/ppermute | solution.py:406
  56.5 2.0 %collective-permute-start.6 = (f32[16,128]{1,0:T(8,128)S(1)}, f32[16,128]{1,0:T(8,128)S(1)}, u32[]{:S(2)}, u32[]{:S(2)}) collective-permute-start(f32[16,128]{1,0:T(8,128)S(1)} %add.222), channel_id=1, source_target_pairs={{0,4},{1,5},{2,6},{3,7},{4,0},{5,1},{6,2},{7,3},{8,12},{9,13},{10,... | collective-permute-start | bytes 24584 | tf_op jit(solution)/shard_map/ppermute | solution.py:406
  58.5 1.6 %collective-permute-done.6 = f32[16,128]{1,0:T(8,128)S(1)} collective-permute-done((f32[16,128]{1,0:T(8,128)S(1)}, f32[16,128]{1,0:T(8,128)S(1)}, u32[]{:S(2)}, u32[]{:S(2)}) %collective-permute-start.6) | collective-permute-done | bytes 8224 | tf_op jit(solution)/shard_map/ppermute | solution.py:406
  60.2 4.8 %collective-permute-start.7 = (f32[16,128]{1,0:T(8,128)S(1)}, f32[16,128]{1,0:T(8,128)S(1)}, u32[]{:S(2)}, u32[]{:S(2)}) collective-permute-start(f32[16,128]{1,0:T(8,128)S(1)} %add.223), channel_id=1, source_target_pairs={{0,8},{8,0},{16,24},{24,16},{1,9},{9,1},{17,25},{25,17},{2,10},{10... | collective-permute-start | bytes 24584 | tf_op jit(solution)/shard_map/ppermute | solution.py:406
  65.0 1.6 %collective-permute-done.7 = f32[16,128]{1,0:T(8,128)S(1)} collective-permute-done((f32[16,128]{1,0:T(8,128)S(1)}, f32[16,128]{1,0:T(8,128)S(1)}, u32[]{:S(2)}, u32[]{:S(2)}) %collective-permute-start.7) | collective-permute-done | bytes 8224 | tf_op jit(solution)/shard_map/ppermute | solution.py:406
  66.6 3.5 %collective-permute-start.8 = (f32[16,128]{1,0:T(8,128)S(1)}, f32[16,128]{1,0:T(8,128)S(1)}, u32[]{:S(2)}, u32[]{:S(2)}) collective-permute-start(f32[16,128]{1,0:T(8,128)S(1)} %add.224), channel_id=1, source_target_pairs={{0,16},{8,24},{16,0},{24,8},{1,17},{9,25},{17,1},{25,9},{2,18},{10... | collective-permute-start | bytes 24584 | tf_op jit(solution)/shard_map/ppermute | solution.py:406
  70.1 1.6 %collective-permute-done.8 = f32[16,128]{1,0:T(8,128)S(1)} collective-permute-done((f32[16,128]{1,0:T(8,128)S(1)}, f32[16,128]{1,0:T(8,128)S(1)}, u32[]{:S(2)}, u32[]{:S(2)}) %collective-permute-start.8) | collective-permute-done | bytes 8224 | tf_op jit(solution)/shard_map/ppermute | solution.py:406
  71.8 0.1 fusion.7
  71.9 0.1 add_multiply_fusion.6
  72.0 0.1 add_multiply_fusion.10
  72.1 0.1 concatenate.46
  72.2 0.1 concatenate.44
  72.4 0.1 concatenate.42
  72.5 0.1 concatenate.41
  72.6 0.1 concatenate.40
  72.6 0.1 concatenate.39
  72.7 0.1 concatenate.38
  72.9 0.2 fusion.30
  73.2 0.2 fusion.31
  73.4 0.8 gather_fusion
  74.2 0.1 add_multiply_fusion
  74.3 0.2 convolution_multiply_fusion.1
  74.5 5.9 %cholesky.16 = f32[64,64]{1,0:T(8,128)S(1)} custom-call(f32[64,64]{1,0:T(8,128)S(1)} %add_multiply_fusion), custom_call_target="Cholesky" | custom-call | tf_op jit(solution)/shard_map/jit(cholesky)/cholesky | solution.py:445
  80.4 0.6 compare_reduce_fusion
  81.1 0.7 fusion.2
  81.7 4.9 %custom-call.10 = f32[1,64,64]{1,2,0:T(8,128)S(1)} custom-call(f32[1,64,64]{2,1,0:T(8,128)S(1)} %fusion.2), custom_call_target="InvertDiagBlocksLowerTriangular" | custom-call | tf_op jit(solution)/shard_map/jit(_cho_solve)/triangular_solve | solution.py:446
  86.6 0.2 fusion.4
  86.8 0.2 convolution_multiply_fusion
  86.9 0.2 fusion
  87.2 0.1 copy.25.weights
  87.3 2.4 %shard_map.71 = (f32[32,16,128]{2,1,0:T(8,128)}, f32[32,16,128]{2,1,0:T(8,128)}) custom-call(f32[32,16,128]{2,1,0:T(8,128)S(1)} %copy-done.1, f32[32,16,1152]{2,1,0:T(8,128)S(1)} %get-tuple-element.26.basis, f32[2,72,8]{2,1,0:T(8,128)S(1)} %copy.25.weights), custom_call_target="tpu_custom_call" | custom-call | tf_op jit(solution)/shard_map/pallas_call | solution.py:378
  (32 shorter events, 0.5 us)
Async XLA Ops:
  0.6 11.5 %copy-start.1 = (f32[32,16,128]{2,1,0:T(8,128)S(1)}, f32[32,16,128]{2,1,0:T(8,128)}, u32[]{:S(2)}) copy-start(f32[32,16,128]{2,1,0:T(8,128)} %guess.5) | copy-start | bytes 786436
  3.1 1.0 %copy-start = (f32[32,16,128]{2,1,0:T(8,128)S(1)}, f32[32,16,128]{2,1,0:T(8,128)}, u32[]{:S(2)}) copy-start(f32[32,16,128]{2,1,0:T(8,128)} %guess.5) | copy-start | bytes 786436
  4.0 0.9 %copy-start.2 = (f32[32,16,128]{2,1,0:T(8,128)S(1)}, f32[32,16,128]{2,1,0:T(8,128)}, u32[]{:S(2)}) copy-start(f32[32,16,128]{2,1,0:T(8,128)} %source.1) | copy-start | bytes 786436
  5.0 67.9 %copy-start.3 = (f32[72,64]{1,0:T(8,128)S(1)}, f32[72,64]{1,0:T(8,128)}, u32[]{:S(2)}) copy-start(f32[72,64]{1,0:T(8,128)} %constant.84.clone) | copy-start | bytes 55300
  6.2 5.9 %collective-permute-start = (f32[200,128]{1,0:T(8,128)S(1)}, f32[200,128]{1,0:T(8,128)S(1)}, u32[]{:S(2)}, u32[]{:S(2)}) collective-permute-start(f32[200,128]{1,0:T(8,128)S(1)} %get-tuple-element.15), channel_id=1, source_target_pairs={{0,8},{8,0},{16,24},{24,16},{1,9},{9,1},{17,25},{25,17},{2,10},{10... | collective-permute-start | bytes 307208 | tf_op jit(solution)/shard_map/ppermute | solution.py:396
  9.3 2.9 %collective-permute-start.1 = (f32[200,128]{1,0:T(8,128)S(1)}, f32[200,128]{1,0:T(8,128)S(1)}, u32[]{:S(2)}, u32[]{:S(2)}) collective-permute-start(f32[200,128]{1,0:T(8,128)S(1)} %get-tuple-element.16), channel_id=1, source_target_pairs={{8,16},{16,8},{9,17},{17,9},{10,18},{18,10},{11,19},{19,11},{12,20... | collective-permute-start | bytes 307208 | tf_op jit(solution)/shard_map/ppermute | solution.py:396
  14.3 1.6 %collective-permute-start.2 = (f32[536,128]{1,0:T(8,128)S(1)}, f32[536,128]{1,0:T(8,128)S(1)}, u32[]{:S(2)}, u32[]{:S(2)}) collective-permute-start(f32[536,128]{1,0:T(8,128)S(1)} %get-tuple-element.20), channel_id=1, source_target_pairs={{0,1},{1,0},{2,3},{3,2},{4,5},{5,4},{6,7},{7,6},{8,9},{9,8},{10,11... | collective-permute-start | bytes 823304 | tf_op jit(solution)/shard_map/ppermute | solution.py:396
  14.4 1.5 %collective-permute-start.3 = (f32[536,128]{1,0:T(8,128)S(1)}, f32[536,128]{1,0:T(8,128)S(1)}, u32[]{:S(2)}, u32[]{:S(2)}) collective-permute-start(f32[536,128]{1,0:T(8,128)S(1)} %get-tuple-element.21), channel_id=1, source_target_pairs={{1,2},{2,1},{3,4},{4,3},{5,6},{6,5},{9,10},{10,9},{11,12},{12,11},... | collective-permute-start | bytes 823304 | tf_op jit(solution)/shard_map/ppermute | solution.py:396
  42.4 10.1 %collective-permute-start.4 = (f32[16,128]{1,0:T(8,128)S(1)}, f32[16,128]{1,0:T(8,128)S(1)}, u32[]{:S(2)}, u32[]{:S(2)}) collective-permute-start(f32[16,128]{1,0:T(8,128)S(1)} %get-tuple-element.27), channel_id=1, source_target_pairs={{0,1},{1,0},{2,3},{3,2},{4,5},{5,4},{6,7},{7,6},{8,9},{9,8},{10,11... | collective-permute-start | bytes 24584 | tf_op jit(solution)/shard_map/ppermute | solution.py:406
  52.5 4.0 %collective-permute-start.5 = (f32[16,128]{1,0:T(8,128)S(1)}, f32[16,128]{1,0:T(8,128)S(1)}, u32[]{:S(2)}, u32[]{:S(2)}) collective-permute-start(f32[16,128]{1,0:T(8,128)S(1)} %add.221), channel_id=1, source_target_pairs={{0,2},{1,3},{2,0},{3,1},{4,6},{5,7},{6,4},{7,5},{8,10},{9,11},{10,... | collective-permute-start | bytes 24584 | tf_op jit(solution)/shard_map/ppermute | solution.py:406
  56.5 3.7 %collective-permute-start.6 = (f32[16,128]{1,0:T(8,128)S(1)}, f32[16,128]{1,0:T(8,128)S(1)}, u32[]{:S(2)}, u32[]{:S(2)}) collective-permute-start(f32[16,128]{1,0:T(8,128)S(1)} %add.222), channel_id=1, source_target_pairs={{0,4},{1,5},{2,6},{3,7},{4,0},{5,1},{6,2},{7,3},{8,12},{9,13},{10,... | collective-permute-start | bytes 24584 | tf_op jit(solution)/shard_map/ppermute | solution.py:406
  60.2 6.4 %collective-permute-start.7 = (f32[16,128]{1,0:T(8,128)S(1)}, f32[16,128]{1,0:T(8,128)S(1)}, u32[]{:S(2)}, u32[]{:S(2)}) collective-permute-start(f32[16,128]{1,0:T(8,128)S(1)} %add.223), channel_id=1, source_target_pairs={{0,8},{8,0},{16,24},{24,16},{1,9},{9,1},{17,25},{25,17},{2,10},{10... | collective-permute-start | bytes 24584 | tf_op jit(solution)/shard_map/ppermute | solution.py:406
  66.6 5.1 %collective-permute-start.8 = (f32[16,128]{1,0:T(8,128)S(1)}, f32[16,128]{1,0:T(8,128)S(1)}, u32[]{:S(2)}, u32[]{:S(2)}) collective-permute-start(f32[16,128]{1,0:T(8,128)S(1)} %add.224), channel_id=1, source_target_pairs={{0,16},{8,24},{16,0},{24,8},{1,17},{9,25},{17,1},{25,9},{2,18},{10... | collective-permute-start | bytes 24584 | tf_op jit(solution)/shard_map/ppermute | solution.py:406
where the time goes:
time: 89.9 us; the launch traced here: 89.7 us
  Pallas kernels  32.2 us (36%)
  starting transfers between devices  26.4 us (29%)
  other arithmetic  12.8 us (14%)
  waiting for transfers between devices  10.4 us (12%)
  local copies, waits for them, and re-layouts  5.84 us (6%)
  matrix products  1.1 us (1%)
    pallas_call x4, Pallas kernels, call(): pl.pallas_call(kernel, out_shape=[jax.ShapeDtypeStruct(s, jnp.float32) fo...  32.2 us
    ppermute x5, starting transfers between devices, total_of(): x = x + lax.ppermute(x, axis, [(i, i ^ step) for i in range(count)])  22 us
    ppermute x5, waiting for transfers between devices, total_of(): x = x + lax.ppermute(x, axis, [(i, i ^ step) for i in range(count)])  7.33 us
    another operation x3, other arithmetic, least_squares(): factor = jnp.linalg.cholesky(balanced)  6.55 us
    another operation x2, other arithmetic, least_squares(): jax.scipy.linalg.cho_solve((factor, True), scale[:, None] * project)  5.55 us
    ppermute x4, starting transfers between devices, exchange(): got.append(lax.ppermute(cells, axis, links))  4.45 us
    unnamed x18, local copies, waits for them, and re-layouts  4.11 us
    ppermute x4, waiting for transfers between devices, exchange(): got.append(lax.ppermute(cells, axis, links))  3.07 us
  transfers between devices with their start and end apart: 9, of which 7 were waited for; matrix products, arithmetic and copies ran while one was open for 0% of the time, Pallas kernels for 0%

commit v1 on v0

--- a/solution.py
+++ b/solution.py
@@ -2,7 +2,6 @@
 
 import jax
 import jax.numpy as jnp
-import numpy as np
 from jax import lax
 from jax.experimental import pallas as pl
 from jax.experimental.pallas import tpu as pltpu
@@ -224,12 +223,8 @@
     return high, (a - high.astype(jnp.float32)).astype(jnp.bfloat16)
 
 
-def dot_t(a, b):
-    return lax.dot_general(a, b, (((0,), (0,)), ((), ())), preferred_element_type=jnp.float32)
-
-
 def basis_kernel(
-    py, recv_a, recv_b, rootx, absx, b0x, edge, basis, moments, root, diag, far, f0, f1, f2
+    py, recv_a, recv_b, rootx, absx, b0x, edge, rough, fine, moments, root, diag, far, f0, f1, f2
 ):
     wide, ny, _ = b0x.shape
     nx = wide - 2 * DEEP
@@ -292,39 +287,28 @@
         return (u, z_sum(u))
 
     def sweep(src, lo, hi, put):
-        def two(i, carry):
-            x = lo + 2 * i
-            first, second = carry
+        first, second = pair(src, lo - 1), pair(src, lo)
+        for x in range(lo, hi):
             third = pair(src, x + 1)
             put(x, slab_sum(first, second, third, row_sum))
-            fourth = pair(src, x + 2)
-            put(x + 1, slab_sum(second, third, fourth, row_sum))
-            return (third, fourth)
-
-        lax.fori_loop(0, (hi - lo) // 2, two, (pair(src, lo - 1), pair(src, lo)))
+            first, second = second, third
 
     def put_diag(x, total):
         diag[x] = (diag[x] + root[x] * total - CENTRE) * (2.0 / HALF_WIDTH)
 
     sweep(None, 1, wide - 1, put_diag)
 
-    lane = lanes_of((NRHS, LANES))
-    same = select((LANES, LANES), lambda r, c: r // NRHS == c // NRHS)
-
-    def fold(block):
-        f = jnp.sum((block * same).reshape(LANES // NRHS, NRHS, LANES), axis=0)
-        shift = LANES // 2
-        while shift >= NRHS:
-            f = f + pltpu.roll(f, shift, 1)
-            shift //= 2
-        return f
-
-    tile = [jnp.zeros((NRHS, LANES), jnp.float32) for _ in range(2)]
-
-    def note(tile, n, block):
-        f = fold(block)
-        which, place = divmod(n, LANES // NRHS)
-        tile[which] = tile[which] + jnp.where(lane // NRHS == place, f, 0.0)
+    level = lanes_of((NRHS, LANES)) // NRHS
+    depth = LANES // NRHS
+    folded = [None] * (2 * S + 1)
+
+    def note(n, block):
+        if n in (0, 1, 2 * S):
+            block = 0.5 * (block + block.T)
+        f = block[0:NRHS]
+        for z in range(1, depth):
+            f = jnp.where(level == z, block[z * NRHS : (z + 1) * NRHS], f)
+        folded[n] = f
 
     frames = [f0, f1, f2]
     old = None
@@ -339,45 +323,145 @@
 
             sweep(src, j, wide - j, put)
         own = now[DEEP : DEEP + nx, DEEP : DEEP + ny, :]
-        basis[:, :, j * LANES : (j + 1) * LANES] = own
         high, low = halves(own.reshape(nx * ny, LANES))
-        note(tile, 2 * j, dot_t(high, high) + dot_t(high, low) + dot_t(low, high))
+        rough[:, j * LANES : (j + 1) * LANES] = high
+        fine[:, j * LANES : (j + 1) * LANES] = low
+        turned = high.T
+        both = jnp.concatenate([high, low], axis=1)
+        left = turned if j == 0 else jnp.concatenate([turned, old[0]], axis=0)
+        got = jnp.dot(left, both, preferred_element_type=jnp.float32)
+        note(2 * j, got[:LANES, :LANES] + 2.0 * got[:LANES, LANES:])
         if j > 0:
-            note(tile, 2 * j - 1, dot_t(high, old[0]) + dot_t(high, old[1]) + dot_t(low, old[0]))
-        old = (high, low)
-    moments[0:NRHS] = tile[0]
-    moments[NRHS : 2 * NRHS] = tile[1]
-
-
-def combine_kernel(guess, basis, weights, update, rest, wh, wl):
+            rest = jnp.dot(turned, old[1], preferred_element_type=jnp.float32)
+            note(2 * j - 1, got[LANES:, :LANES] + got[LANES:, LANES:] + rest)
+        old = (turned, low)
+    every = jnp.concatenate(folded, axis=0)
+    shift = LANES // 2
+    while shift >= NRHS:
+        every = every + pltpu.roll(every, shift, 1)
+        shift //= 2
+    blocks = [every[n * NRHS : (n + 1) * NRHS] for n in range(2 * S + 1)]
+    tile = jnp.zeros((NRHS, LANES), jnp.float32)
+    row, col = rows_at((NRHS, LANES)), lanes_of((NRHS, LANES)) % NRHS
+    last = blocks[2 * S]
+    below = jnp.where(row == col + 1, pltpu.roll(last, 1, 0), 0.0)
+    below = jnp.where((row == NRHS - 1) & (col == 0), pltpu.roll(last, 1, 1), below)
+    blocks[0] = jnp.where(row <= col, blocks[0], last)
+    blocks[1] = jnp.where(row <= col, blocks[1], below)
+    for n in range(2 * S):
+        tile = jnp.where(level == n, blocks[n], tile)
+    moments[...] = jnp.broadcast_to(tile[None], moments.shape)
+
+
+def moment_blocks(tile):
+    depth = LANES // NRHS
+    row, lane = rows_at((NRHS, LANES)), lanes_of((NRHS, LANES))
+    raw = [tile] + [pltpu.roll(tile, LANES - NRHS * n, 1) for n in range(1, depth)]
+    square = jnp.concatenate([tile, jnp.zeros((LANES - NRHS, LANES), jnp.float32)], axis=0).T
+    turned = [square[n * NRHS : (n + 1) * NRHS] for n in range(depth)]
+    first, second = raw[0], raw[1]
+    last = jnp.where(row > lane, first, turned[0])
+    last = jnp.where(row == lane, pltpu.roll(second, NRHS - 1, 0), last)
+    last = jnp.where((row == NRHS - 1) & (lane == NRHS - 1), pltpu.roll(second, NRHS - 1, 1), last)
+    even = [0.5 * (r + t) for r, t in zip(raw, turned)] + [last]
+    even[0] = jnp.where(row <= lane, first, turned[0])
+    even[1] = jnp.where(row <= lane, second, turned[1])
+    even = [jnp.where(lane < NRHS, e, 0.0) for e in even]
+    return even[:2] + [2.0 * even[n] - even[n % 2] for n in range(2, 2 * S + 1)]
+
+
+def solve_small(m):
+    lane = lanes_of((NRHS, LANES))
+    half = HALF_WIDTH / 2
+    size = S * NRHS
+
+    def a_on(seq, n):
+        return CENTRE * seq[n] + half * (seq[n + 1] + seq[abs(n - 1)])
+
+    nu = [a_on(m, n) for n in range(2 * S)]
+    mu = [a_on(nu, n) for n in range(2 * S - 1)]
+    up = functools.reduce(jnp.add, [mu[n] if n == 0 else pltpu.roll(mu[n], NRHS * n, 1) for n in range(2 * S - 1)])
+    around = functools.reduce(
+        jnp.add,
+        [mu[abs(n - (S - 1))] if n == 0 else pltpu.roll(mu[abs(n - (S - 1))], NRHS * n, 1) for n in range(2 * S - 1)],
+    )
+
+    def left(f, places):
+        return f if places == 0 else pltpu.roll(f, LANES - places, 1)
+
+    rows = []
+    for c in range(S):
+        both = 0.5 * (left(up, NRHS * c) + left(around, NRHS * (S - 1 - c)))
+        rows.append(jnp.where(lane < size, both, pltpu.roll(nu[c], size, 1)))
+    m = jnp.concatenate(rows, axis=0)
+    row, col = rows_at((size, LANES)), lanes_of((size, LANES))
+    on = row == col
+    kept = jnp.where(on, m, 0.0)
+    scale = 1.0 / jnp.sqrt(jnp.sum(kept, axis=1, keepdims=True))
+    across = jnp.sum(kept, axis=0, keepdims=True)
+    across = jnp.where(lanes_of((1, LANES)) < size, 1.0 / jnp.sqrt(across), 1.0)
+    m = scale * m * across + jnp.where(on, RIDGE, 0.0)
+    for i in range(0, size, 2):
+        c0 = jnp.broadcast_to(m[:, i : i + 1], m.shape)
+        c1 = jnp.broadcast_to(m[:, i + 1 : i + 2], m.shape)
+        r0, r1 = m[i : i + 1], m[i + 1 : i + 2]
+        a, b, d = c0[i : i + 1], c1[i : i + 1], c1[i + 1 : i + 2]
+        inverse = 1.0 / (a * d - b * b)
+        q0 = inverse * (d * r0 - b * r1)
+        q1 = inverse * (a * r1 - b * r0)
+        c0 = jnp.where(row == i, c0 - 1.0, c0)
+        c1 = jnp.where(row == i + 1, c1 - 1.0, c1)
+        m = m - c0 * q0 - c1 * q1
+    x = jnp.where((col >= size) & (col < size + NRHS), scale * m, 0.0)
+    shift = NRHS
+    while shift < LANES:
+        x = x + pltpu.roll(x, shift, 1)
+        shift *= 2
+    c = [x[j * NRHS : (j + 1) * NRHS] for j in range(S)]
+    unit = jnp.where(rows_at((NRHS, LANES)) == lane % NRHS, 1.0, 0.0)
+    remain = []
+    for j in range(S + 1):
+        total = CENTRE * c[j] if j < S else 0.0
+        if j > 0:
+            total = total + (HALF_WIDTH if j == 1 else half) * c[j - 1]
+        if j + 1 < S:
+            total = total + half * c[j + 1]
+        remain.append((unit if j == 0 else 0.0) - total)
+    return c, remain
+
+
+def combine_kernel(guess, rough, fine, parts, update, rest, wh, wl):
     nx, ny, _ = guess.shape
-    spread = select((NRHS, LANES), lambda r, c: r == c % NRHS)
-    same = select((LANES, LANES), lambda r, c: r // NRHS == c // NRHS)
-    for part in range(2):
-        rows = exact(weights[part], spread)
+    level = lanes_of((NRHS, LANES)) // NRHS
+    coeffs, remain = solve_small(moment_blocks(jnp.sum(parts[...], axis=0)))
+    coeffs = coeffs + [jnp.zeros((NRHS, LANES), jnp.float32)]
+    for part, tiles in ((0, coeffs), (1, remain)):
         for j in range(S + 1):
-            tile = rows[j * NRHS : (j + 1) * NRHS]
-            full = jnp.concatenate([tile] * (LANES // NRHS), axis=0) * same
+            full = jnp.concatenate(
+                [jnp.where(level == z, tiles[j], 0.0) for z in range(LANES // NRHS)], axis=0
+            )
             high, low = halves(full)
             wh[j * LANES : (j + 1) * LANES, part * LANES : (part + 1) * LANES] = high
             wl[j * LANES : (j + 1) * LANES, part * LANES : (part + 1) * LANES] = low
     chunk = nx // 4
     for i in range(4):
         at = slice(i * chunk, (i + 1) * chunk)
-        high, low = halves(basis[at].reshape(chunk * ny, (S + 1) * LANES))
+        cells = slice(i * chunk * ny, (i + 1) * chunk * ny)
         dot = functools.partial(jnp.dot, preferred_element_type=jnp.float32)
-        out = dot(high, wh[...]) + dot(high, wl[...]) + dot(low, wh[...])
+        out = dot(rough[cells], wh[...]) + dot(rough[cells], wl[...]) + dot(fine[cells], wh[...])
         out = out.reshape(chunk, ny, 2 * LANES)
         update[at] = guess[at] + out[:, :, :LANES]
         rest[at] = out[:, :, LANES:]
 
 
-def call(kernel, ins, outs, scratch=(), scalars=0):
+def call(kernel, ins, outs, scratch=(), scalars=0, kinds=None):
     specs = [pl.BlockSpec(memory_space=pltpu.SMEM)] * scalars
     specs += [pl.BlockSpec(memory_space=pltpu.VMEM)] * (len(ins) - scalars)
     result = pl.pallas_call(
         kernel,
-        out_shape=[jax.ShapeDtypeStruct(s, jnp.float32) for s in outs],
+        out_shape=[
+            jax.ShapeDtypeStruct(s, k) for s, k in zip(outs, kinds or [jnp.float32] * len(outs))
+        ],
         in_specs=specs,
         out_specs=[pl.BlockSpec(memory_space=pltpu.VMEM)] * len(outs),
         scratch_shapes=list(scratch),
@@ -408,45 +492,11 @@
     return x
 
 
-def krylov_map():
-    table = np.zeros((S + 1, S))
-    table[0, 0] = CENTRE
-    table[1, 0] = HALF_WIDTH
-    for column in range(1, S):
-        table[column, column] = CENTRE
-        table[column - 1, column] = HALF_WIDTH / 2
-        table[column + 1, column] = HALF_WIDTH / 2
-    return np.kron(table, np.eye(NRHS))
-
-
-def gram_of(moments):
-    raw = [
-        moments[(n // 16) * 8 : (n // 16) * 8 + 8, (n % 16) * 8 : (n % 16) * 8 + 8]
-        for n in range(2 * S + 1)
-    ]
-    m = [raw[0], raw[1]] + [2.0 * raw[n] - raw[n % 2] for n in range(2, 2 * S + 1)]
-    return jnp.concatenate(
-        [
-            jnp.concatenate([0.5 * (m[i + j] + m[abs(i - j)]) for j in range(S + 1)], axis=1)
-            for i in range(S + 1)
-        ],
-        axis=0,
-    )
-
-
-def least_squares(gram):
-    lift = jnp.asarray(krylov_map(), dtype=gram.dtype)
-    normal = jnp.dot(lift.T, jnp.dot(gram, lift, precision=HIGHEST), precision=HIGHEST)
-    project = jnp.dot(lift.T, gram[:, :NRHS], precision=HIGHEST)
-    scale = 1.0 / jnp.sqrt(jnp.diagonal(normal))
-    balanced = scale[:, None] * normal * scale[None, :] + RIDGE * jnp.eye(
-        S * NRHS, dtype=gram.dtype
-    )
-    factor = jnp.linalg.cholesky(balanced)
-    coeffs = scale[:, None] * jax.scipy.linalg.cho_solve((factor, True), scale[:, None] * project)
-    select_first = jnp.eye((S + 1) * NRHS, dtype=gram.dtype)[:, :NRHS]
-    remain = select_first - jnp.dot(lift, coeffs, precision=HIGHEST)
-    return (coeffs, remain)
+def totals(parts):
+    count = parts.shape[0]
+    if count > 1:
+        return lax.all_to_all(parts, ("gx", "gy"), 0, 0)
+    return total_of(total_of(parts, "gy"), "gx")
 
 
 def body(initial_guess, source, leaf_density, absorption):
@@ -477,19 +527,20 @@
     )
     ya, yb = exchange(ya, yb, "gy")
     frame = pltpu.VMEM((wide, tall, lanes), jnp.float32)
-    basis, moments = call(
+    count = lax.axis_size("gx") * lax.axis_size("gy")
+    count = count if count <= 64 else 1
+    cells = nx * ny
+    rough, fine, moments = call(
         basis_kernel,
         (py, ya, yb, rootx, absx, b0x, edge),
-        ((nx, ny, (S + 1) * lanes), (2 * NRHS, lanes)),
+        ((cells, (S + 1) * lanes), (cells, (S + 1) * lanes), (count, NRHS, lanes)),
         scratch=[frame, frame, pltpu.VMEM((2, wide + 8, lanes), jnp.float32), frame, frame, frame],
         scalars=1,
+        kinds=(jnp.bfloat16, jnp.bfloat16, jnp.float32),
     )
-    moments = total_of(total_of(moments, "gy"), "gx")
-    coeffs, remain = least_squares(gram_of(moments))
-    weights = jnp.stack([jnp.pad(coeffs, ((0, NRHS), (0, 0))), remain])
     return call(
         combine_kernel,
-        (initial_guess, basis, weights),
+        (initial_guess, rough, fine, totals(moments)),
         (block, block),
         scratch=[pltpu.VMEM(((S + 1) * lanes, 2 * lanes), jnp.bfloat16)] * 2,
     )

time: 89.9 us -> 53.7 us (0.60)
  blocking collectives: 0 us -> 25.4 us
  starting transfers between devices: 26.4 us -> 4.45 us
  Pallas kernels: 32.2 us -> 17.4 us
  other arithmetic: 12.8 us -> 0.23 us
  waiting for transfers between devices: 10.4 us -> 3.07 us
  local copies, waits for them, and re-layouts: 5.84 us -> 2.2 us
  matrix products: 1.1 us -> 0 us
    all_to_all x0 -> x1, blocking collectives: none -> 25.4 us  [totals(): return lax.all_to_all(parts, ('gx', 'gy'), 0, 0)]
    ppermute x5 -> x0, starting transfers between devices: 22 us -> none  [total_of(): x = x + lax.ppermute(x, axis, [(i, i ^ step) for i in range(count)])]
    pallas_call x4, Pallas kernels: 32.2 us -> 17.4 us  [call(): pl.pallas_call(kernel, out_shape=[jax.ShapeDtypeStruct(s, k) for s, k in...]
    another operation x6 -> x0, other arithmetic: 12.1 us -> none  [the longest x3 6.55 us: least_squares(): factor = jnp.linalg.cholesky(balanced)]
    ppermute x5 -> x0, waiting for transfers between devices: 7.33 us -> none  [total_of(): x = x + lax.ppermute(x, axis, [(i, i ^ step) for i in range(count)])]
    unnamed x18 -> x6, local copies, waits for them, and re-layouts: 4.11 us -> 2.2 us
  transfers between devices with their start and end apart: 9 -> 4, of which waited for: 7 -> 2; matrix products, arithmetic and copies ran while one was open for 0% -> 0% of each run, Pallas kernels for 0% -> 0%
where the time goes in v1:
time: 53.7 us; the launch traced here: 53.5 us
  blocking collectives  25.4 us (47%)
  Pallas kernels  17.4 us (32%)
  starting transfers between devices  4.45 us (8%)
  waiting for transfers between devices  3.07 us (6%)
  local copies, waits for them, and re-layouts  2.2 us (4%)
  between operations  0.74 us (1%)
    all_to_all x1, blocking collectives, totals(): return lax.all_to_all(parts, ('gx', 'gy'), 0, 0)  25.4 us
    pallas_call x4, Pallas kernels, call(): pl.pallas_call(kernel, out_shape=[jax.ShapeDtypeStruct(s, k) for s, k in...  17.4 us
    ppermute x4, starting transfers between devices, exchange(): got.append(lax.ppermute(cells, axis, links))  4.45 us
    ppermute x4, waiting for transfers between devices, exchange(): got.append(lax.ppermute(cells, axis, links))  3.07 us
    unnamed x6, local copies, waits for them, and re-layouts  2.2 us
  transfers between devices with their start and end apart: 4, of which 2 were waited for; matrix products, arithmetic and copies ran while one was open for 0% of the time, Pallas kernels for 0%

profile of v1, /device:TPU:0, one launch (start us, length us, event | category | flops | bytes accessed | tf_op | source)
XLA Modules:
  0.0 53.5 jit_solution(9846699735945790425)
XLA Ops:
  0.6 0.0 copy-start
  0.6 0.0 copy-start.1
  0.7 1.1 %copy.8 = f32[32,16,16]{2,1,0:T(8,128)S(1)} copy(f32[32,16,16]{0,2,1:T(8,128)} %param.6) | data formatting | bytes 65536 | tf_op args[2]
  1.8 0.1 divide_sqrt_fusion
  1.9 1.1 %copy.10 = f32[32,16,16]{2,1,0:T(8,128)S(1)} copy(f32[32,16,16]{0,2,1:T(8,128)} %param.7) | data formatting | bytes 65536 | tf_op args[3]
  3.0 0.1 pad_maximum_fusion.ra
  3.1 0.0 copy-done
  3.1 0.0 copy-done.1
  3.1 1.2 %shard_map.59 = (f32[32,16,128]{2,1,0:T(8,128)S(1)}, f32[32,16,128]{2,1,0:T(8,128)S(1)}, f32[32,16,128]{2,1,0:T(8,128)S(1)}, f32[200,128]{1,0:T(8,128)S(1)}, f32[200,128]{1,0:T(8,128)S(1)}) custom-call(s32[1]{0:T(128)} %bitcast.1.px, f32[32,16,128]{2,1,0:T(8,128)S(1)} %copy-done, f32[32,16,128]{2,1,0:T(8,128)S(1)} %copy-done.1, ...), custom_call_target="tpu_custom_call" | custom-call | tf_op jit(solution)/shard_map/pallas_call | solution.py:460
  4.4 3.0 %collective-permute-start = (f32[200,128]{1,0:T(8,128)S(1)}, f32[200,128]{1,0:T(8,128)S(1)}, u32[]{:S(2)}, u32[]{:S(2)}) collective-permute-start(f32[200,128]{1,0:T(8,128)S(1)} %get-tuple-element.16), channel_id=1, source_target_pairs={{0,8},{8,0},{16,24},{24,16},{1,9},{9,1},{17,25},{25,17},{2,10},{10... | collective-permute-start | bytes 307208 | tf_op jit(solution)/shard_map/ppermute | solution.py:480
  7.4 0.7 %collective-permute-start.1 = (f32[200,128]{1,0:T(8,128)S(1)}, f32[200,128]{1,0:T(8,128)S(1)}, u32[]{:S(2)}, u32[]{:S(2)}) collective-permute-start(f32[200,128]{1,0:T(8,128)S(1)} %get-tuple-element.17), channel_id=1, source_target_pairs={{8,16},{16,8},{9,17},{17,9},{10,18},{18,10},{11,19},{19,11},{12,20... | collective-permute-start | bytes 307208 | tf_op jit(solution)/shard_map/ppermute | solution.py:480
  8.1 2.2 %collective-permute-done.recv_a = f32[200,128]{1,0:T(8,128)S(1)} collective-permute-done((f32[200,128]{1,0:T(8,128)S(1)}, f32[200,128]{1,0:T(8,128)S(1)}, u32[]{:S(2)}, u32[]{:S(2)}) %collective-permute-start) | collective-permute-done | bytes 102432 | tf_op jit(solution)/shard_map/ppermute | solution.py:480
  10.3 0.0 collective-permute-done.1.recv_b
  10.3 2.2 %shard_map.60 = (f32[48,16,128]{2,1,0:T(8,128)S(1)}, f32[48,16,128]{2,1,0:T(8,128)S(1)}, f32[48,16,128]{2,1,0:T(8,128)S(1)}, f32[2,56,128]{2,1,0:T(8,128)S(1)}, ...) custom-call(s32[1]{0:T(128)} %bitcast.1.px, s32[1]{0:T(128)} %bitcast.py, f32[200,128]{1,0:T(8,128)S(1)} %collective-permute-done.recv_a, ...), custom_call_target="tpu_custom_call" | custom-call | tf_op jit(solution)/shard_map/pallas_call | solution.py:460
  12.5 0.1 collective-permute-start.2
  12.5 0.7 %collective-permute-start.3 = (f32[536,128]{1,0:T(8,128)S(1)}, f32[536,128]{1,0:T(8,128)S(1)}, u32[]{:S(2)}, u32[]{:S(2)}) collective-permute-start(f32[536,128]{1,0:T(8,128)S(1)} %get-tuple-element.22), channel_id=1, source_target_pairs={{1,2},{2,1},{3,4},{4,3},{5,6},{6,5},{9,10},{10,9},{11,12},{12,11},... | collective-permute-start | bytes 823304 | tf_op jit(solution)/shard_map/ppermute | solution.py:480
  13.2 0.9 %collective-permute-done.2.recv_a = f32[536,128]{1,0:T(8,128)S(1)} collective-permute-done((f32[536,128]{1,0:T(8,128)S(1)}, f32[536,128]{1,0:T(8,128)S(1)}, u32[]{:S(2)}, u32[]{:S(2)}) %collective-permute-start.2) | collective-permute-done | bytes 274464 | tf_op jit(solution)/shard_map/ppermute | solution.py:480
  14.1 0.0 collective-permute-done.3.recv_b
  14.1 8.2 %shard_map.61 = (bf16[512,1152]{1,0:T(8,128)(2,1)S(1)}, bf16[512,1152]{1,0:T(8,128)(2,1)S(1)}, f32[32,8,128]{2,1,0:T(8,128)S(1)}) custom-call(s32[1]{0:T(128)} %bitcast.py, f32[536,128]{1,0:T(8,128)S(1)} %collective-permute-done.2.recv_a, f32[536,128]{1,0:T(8,128)S(1)} %collective-permute-done.3.recv_b, f32[48,16,128]{2,1,0:T(8,128)S(1)} %get-tuple-element.23.rootx, ...), custom_call_target="tpu_custom_call" | custom-call | tf_op jit(solution)/shard_map/pallas_call | solution.py:460
  22.3 25.4 %all_to_all.5.parts = f32[32,8,128]{2,1,0:T(8,128)S(1)} all-to-all(f32[32,8,128]{2,1,0:T(8,128)S(1)} %get-tuple-element.29), channel_id=1, replica_groups=mesh['gx'=4,'gy'=8] {'gx','gy'}, dimensions={0} | all-to-all | bytes 262144 | tf_op jit(solution)/shard_map/all_to_all | solution.py:498
  47.7 5.8 %shard_map.62 = (f32[32,16,128]{2,1,0:T(8,128)}, f32[32,16,128]{2,1,0:T(8,128)}) custom-call(f32[32,16,128]{2,1,0:T(8,128)S(1)} %copy-done, bf16[512,1152]{1,0:T(8,128)(2,1)S(1)} %get-tuple-element.27.rough, bf16[512,1152]{1,0:T(8,128)(2,1)S(1)} %get-tuple-element.28.fine, f32[32,8,128]{2,1,0:T(8,128)S(1)} %all_to_all.5.parts), custom_call_target="tpu_custom_call" | custom-call | tf_op jit(solution)/shard_map/pallas_call | solution.py:460
Async XLA Ops:
  0.6 2.5 %copy-start = (f32[32,16,128]{2,1,0:T(8,128)S(1)}, f32[32,16,128]{2,1,0:T(8,128)}, u32[]{:S(2)}) copy-start(f32[32,16,128]{2,1,0:T(8,128)} %guess.5) | copy-start | bytes 786436
  0.6 2.5 %copy-start.1 = (f32[32,16,128]{2,1,0:T(8,128)S(1)}, f32[32,16,128]{2,1,0:T(8,128)}, u32[]{:S(2)}) copy-start(f32[32,16,128]{2,1,0:T(8,128)} %source.1) | copy-start | bytes 786436
  4.4 5.9 %collective-permute-start = (f32[200,128]{1,0:T(8,128)S(1)}, f32[200,128]{1,0:T(8,128)S(1)}, u32[]{:S(2)}, u32[]{:S(2)}) collective-permute-start(f32[200,128]{1,0:T(8,128)S(1)} %get-tuple-element.16), channel_id=1, source_target_pairs={{0,8},{8,0},{16,24},{24,16},{1,9},{9,1},{17,25},{25,17},{2,10},{10... | collective-permute-start | bytes 307208 | tf_op jit(solution)/shard_map/ppermute | solution.py:480
  7.4 2.9 %collective-permute-start.1 = (f32[200,128]{1,0:T(8,128)S(1)}, f32[200,128]{1,0:T(8,128)S(1)}, u32[]{:S(2)}, u32[]{:S(2)}) collective-permute-start(f32[200,128]{1,0:T(8,128)S(1)} %get-tuple-element.17), channel_id=1, source_target_pairs={{8,16},{16,8},{9,17},{17,9},{10,18},{18,10},{11,19},{19,11},{12,20... | collective-permute-start | bytes 307208 | tf_op jit(solution)/shard_map/ppermute | solution.py:480
  12.5 1.6 %collective-permute-start.2 = (f32[536,128]{1,0:T(8,128)S(1)}, f32[536,128]{1,0:T(8,128)S(1)}, u32[]{:S(2)}, u32[]{:S(2)}) collective-permute-start(f32[536,128]{1,0:T(8,128)S(1)} %get-tuple-element.21), channel_id=1, source_target_pairs={{0,1},{1,0},{2,3},{3,2},{4,5},{5,4},{6,7},{7,6},{8,9},{9,8},{10,11... | collective-permute-start | bytes 823304 | tf_op jit(solution)/shard_map/ppermute | solution.py:480
  12.5 1.5 %collective-permute-start.3 = (f32[536,128]{1,0:T(8,128)S(1)}, f32[536,128]{1,0:T(8,128)S(1)}, u32[]{:S(2)}, u32[]{:S(2)}) collective-permute-start(f32[536,128]{1,0:T(8,128)S(1)} %get-tuple-element.22), channel_id=1, source_target_pairs={{1,2},{2,1},{3,4},{4,3},{5,6},{6,5},{9,10},{10,9},{11,12},{12,11},... | collective-permute-start | bytes 823304 | tf_op jit(solution)/shard_map/ppermute | solution.py:480

commit v2 on v1

--- a/solution.py
+++ b/solution.py
@@ -16,7 +16,7 @@
 CENTRE = 10.3
 HALF_WIDTH = 9.8
 RIDGE = 0.05
-HIGHEST = lax.Precision.HIGHEST
+PANEL = 8
 VMEM_BYTES = 48 * 1024 * 1024
 
 
@@ -64,39 +64,32 @@
     return f + 0.5 * p + rows(0.5 * f + (1.0 / 3.0) * p)
 
 
-def select(shape, rule):
-    row = lax.broadcasted_iota(jnp.int32, shape, 0)
-    col = lax.broadcasted_iota(jnp.int32, shape, 1)
-    return jnp.where(rule(row, col), 1.0, 0.0).astype(jnp.float32)
-
-
-def exact(a, b):
-    return jnp.dot(a, b, precision=HIGHEST, preferred_element_type=jnp.float32)
-
-
-def unpack_matrix(quarter, part, depth):
-    base = quarter * 2 * depth + part * depth
-    return select((LANES, LANES), lambda r, c: r == base + c // NRHS)
-
-
-def pack_matrix(quarter, part, depth):
-    base = quarter * 2 * depth + part * depth
-    return select((LANES, LANES), lambda r, c: (r % NRHS == 0) & (c == base + r // NRHS))
-
-
-def begin_kernel(px, guess, source, ra, root_o, abs_o, b0_o, send_a, send_b):
+def spread(rows):
+    n = rows.shape[0]
+    depth = LANES // NRHS
+    at = rows_at((NRHS, LANES)) * depth + lanes_of((NRHS, LANES)) // NRHS
+    out = []
+    for x in range(n):
+        line = jnp.broadcast_to(rows[x : x + 1], (NRHS, LANES))
+        out.append(jnp.take_along_axis(line, at, axis=1))
+    return jnp.stack(out)
+
+
+def begin_kernel(px, guess, source, leaf, absorb, root_o, abs_o, b0_o, send_a, send_b, root, absb):
     nx, ny, _ = guess.shape
-    depth = ra.shape[2] // 2
-    flat = ra[...].reshape(nx * ny, 2 * depth)
-    for part, out in ((0, root_o), (1, abs_o)):
-        spread = select((2 * depth, LANES), lambda r, c: r == part * depth + c // NRHS)
-        out[...] = exact(flat, spread).reshape(nx, ny, LANES)
+    depth = leaf.shape[1]
+    turned = jnp.transpose(leaf[...].reshape(ny * depth, nx))
+    root_o[...] = jnp.sqrt(PEAK_COND / (1.0 + turned))
+    abs_o[...] = jnp.transpose(absorb[...].reshape(ny * depth, nx))
+    for part, wide in ((root_o, root), (abs_o, absb)):
+        for y in range(0, ny, NRHS):
+            wide[:, y : y + NRHS, :] = spread(part[:, y * depth : (y + NRHS) * depth])
     zero = jnp.zeros((ny, LANES), jnp.float32)
 
     def pair(x, field):
         if x < 0 or x >= nx:
             return (zero, zero)
-        u = root_o[x] if field is None else root_o[x] * field[x]
+        u = root[x] if field is None else root[x] * field[x]
         return (u, z_sum(u))
 
     moving = [pair(-1, guess), pair(0, guess)]
@@ -108,7 +101,7 @@
         wr = slab_sum(*still, row_sum_zero)
         moving, still = moving[1:], still[1:]
         v = guess[x]
-        b0_o[x] = source[x] - abs_o[x] * v + root_o[x] * (wu - v * wr)
+        b0_o[x] = source[x] - absb[x] * v + root[x] * (wu - v * wr)
 
     def write(out, x0, face, beyond):
         n = DEEP * ny
@@ -121,15 +114,12 @@
         out[n : n + 8] = jnp.zeros((8, LANES), jnp.float32)
         for at, col in ((0, 0), (1, ny - 1)):
             out[n + at : n + at + 1] = guess[beyond, col : col + 1, :]
-            out[n + 2 + at : n + 3 + at] = root_o[beyond, col : col + 1, :]
+            out[n + 2 + at : n + 3 + at] = root[beyond, col : col + 1, :]
         n += 8
-        group = DEEP // 4
-        packed = jnp.zeros((group * ny, LANES), jnp.float32)
-        for q in range(4):
-            place = select((2 * depth, LANES), lambda r, c: c == q * 2 * depth + r)
-            part = ra[x0 + q * group : x0 + (q + 1) * group].reshape(group * ny, 2 * depth)
-            packed = packed + exact(part, place)
-        out[n : n + group * ny] = packed
+        for part in (root_o, abs_o):
+            for first in range(0, ny * depth, LANES):
+                out[n : n + DEEP] = part[x0 : x0 + DEEP, first : first + LANES]
+                n += DEEP
 
     @pl.when(px[0] == 0)
     def _():
@@ -147,7 +137,6 @@
 ):
     nx, ny, _ = guess.shape
     wide = nx + 2 * DEEP
-    depth = LANES // NRHS
     rootx[DEEP : DEEP + nx] = root[...]
     absx[DEEP : DEEP + nx] = absb[...]
     b0x[DEEP : DEEP + nx] = b0[...]
@@ -167,12 +156,10 @@
             edge[at, wide + side : wide + side + 1] = msg[n + at : n + at + 1]
             edge[at, wide + 2 + side : wide + 3 + side] = msg[n + 2 + at : n + 3 + at]
         n += 8
-        group = DEEP // 4
-        packed = msg[n : n + group * ny]
-        for q in range(4):
-            for part, out in ((0, rootx), (1, absx)):
-                got = exact(packed, unpack_matrix(q, part, depth))
-                out[x0 + q * group : x0 + (q + 1) * group] = got.reshape(group, ny, LANES)
+        for out in (rootx, absx):
+            for first in range(0, out.shape[1], LANES):
+                out[x0 : x0 + DEEP, first : first + LANES] = msg[n : n + DEEP]
+                n += DEEP
 
     @pl.when(px[0] == 0)
     def _():
@@ -184,9 +171,16 @@
         read(recv_a, 0, 0)
         read(recv_b, DEEP + nx, 1)
 
+    def root_line(x):
+        parts = [
+            spread(rootx[x : x + 1, first : first + LANES])
+            for first in range(0, rootx.shape[1], LANES)
+        ]
+        return jnp.concatenate(parts, axis=1)[0]
+
     for side, out_x, in_x, own in ((0, DEEP - 1, DEEP, 0), (1, DEEP + nx, DEEP + nx - 1, nx - 1)):
-        va, ra = face[side], rootx[out_x]
-        vb, rb = guess[own], rootx[in_x]
+        va, ra = face[side], root_line(out_x)
+        vb, rb = guess[own], root_line(in_x)
         fix_a = ra * (cross_sum(rb * vb, row_sum_zero) - va * cross_sum(rb, row_sum_zero))
         fix_b = rb * (cross_sum(ra * va, row_sum_zero) - vb * cross_sum(ra, row_sum_zero))
         b0x[out_x] = b0x[out_x] + fix_a
@@ -197,15 +191,10 @@
         out[0:n] = b0x[:, y0 : y0 + DEEP, :].reshape(n, LANES)
         out[n : n + wide + 8] = edge[at]
         n += wide + 8
-        group = wide // 4
-        packed = jnp.zeros((group * DEEP, LANES), jnp.float32)
-        for q in range(4):
-            for part, field in ((0, rootx), (1, absx)):
-                some = field[q * group : (q + 1) * group, y0 : y0 + DEEP, :]
-                packed = packed + exact(
-                    some.reshape(group * DEEP, LANES), pack_matrix(q, part, depth)
-                )
-        out[n : n + group * DEEP] = packed
+        first = y0 * (LANES // NRHS)
+        for part in (rootx, absx):
+            out[n : n + wide] = part[:, first : first + LANES]
+            n += wide
 
     @pl.when(py[0] == 0)
     def _():
@@ -230,8 +219,10 @@
     nx = wide - 2 * DEEP
     tall = ny + 2 * DEEP
     depth = LANES // NRHS
-    root[:, DEEP : DEEP + ny, :] = rootx[...]
-    diag[:, DEEP : DEEP + ny, :] = absx[...]
+    for part, out in ((rootx, root), (absx, diag)):
+        for y in range(0, ny, DEEP):
+            first = y * depth
+            out[:, DEEP + y : 2 * DEEP + y, :] = spread(part[:, first : first + LANES])
     f0[:, DEEP : DEEP + ny, :] = b0x[...]
 
     def read(msg, y0, side):
@@ -239,14 +230,9 @@
         f0[:, y0 : y0 + DEEP, :] = msg[0:n].reshape(wide, DEEP, LANES)
         far[side] = msg[n : n + wide + 8]
         n += wide + 8
-        group = wide // 4
-        packed = msg[n : n + group * DEEP]
-        for q in range(4):
-            for part, out in ((0, root), (1, diag)):
-                got = exact(packed, unpack_matrix(q, part, depth))
-                out[q * group : (q + 1) * group, y0 : y0 + DEEP, :] = got.reshape(
-                    group, DEEP, LANES
-                )
+        for out in (root, diag):
+            out[:, y0 : y0 + DEEP, :] = spread(msg[n : n + wide])
+            n += wide
 
     @pl.when(py[0] == 0)
     def _():
@@ -401,17 +387,24 @@
     across = jnp.sum(kept, axis=0, keepdims=True)
     across = jnp.where(lanes_of((1, LANES)) < size, 1.0 / jnp.sqrt(across), 1.0)
     m = scale * m * across + jnp.where(on, RIDGE, 0.0)
-    for i in range(0, size, 2):
-        c0 = jnp.broadcast_to(m[:, i : i + 1], m.shape)
-        c1 = jnp.broadcast_to(m[:, i + 1 : i + 2], m.shape)
-        r0, r1 = m[i : i + 1], m[i + 1 : i + 2]
-        a, b, d = c0[i : i + 1], c1[i : i + 1], c1[i + 1 : i + 2]
-        inverse = 1.0 / (a * d - b * b)
-        q0 = inverse * (d * r0 - b * r1)
-        q1 = inverse * (a * r1 - b * r0)
-        c0 = jnp.where(row == i, c0 - 1.0, c0)
-        c1 = jnp.where(row == i + 1, c1 - 1.0, c1)
-        m = m - c0 * q0 - c1 * q1
+    for first in range(0, size, PANEL):
+        columns = [
+            jnp.broadcast_to(m[:, i : i + 1], m.shape) for i in range(first, first + PANEL)
+        ]
+        for p in range(0, PANEL, 2):
+            i = first + p
+            c0, c1 = columns[p], columns[p + 1]
+            a, b, d = c0[i : i + 1], c1[i : i + 1], c1[i + 1 : i + 2]
+            inverse = 1.0 / (a * d - b * b)
+            a, b, d = inverse * a, inverse * b, inverse * d
+            d0 = jnp.where(row == i, c0 - 1.0, c0)
+            d1 = jnp.where(row == i + 1, c1 - 1.0, c1)
+            for later in range(p + 2, PANEL):
+                r0 = c0[first + later : first + later + 1]
+                r1 = c1[first + later : first + later + 1]
+                columns[later] = columns[later] - d0 * (d * r0 - b * r1) - d1 * (a * r1 - b * r0)
+            r0, r1 = m[i : i + 1], m[i + 1 : i + 2]
+            m = m - d0 * (d * r0 - b * r1) - d1 * (a * r1 - b * r0)
     x = jnp.where((col >= size) & (col < size + NRHS), scale * m, 0.0)
     shift = NRHS
     while shift < LANES:
@@ -501,19 +494,22 @@
 
 def body(initial_guess, source, leaf_density, absorption):
     nx, ny, lanes = initial_guess.shape
-    root = jnp.sqrt(PEAK_COND / (1.0 + leaf_density))
-    ra = jnp.concatenate([root, absorption], axis=-1)
+    leaf = jnp.transpose(leaf_density, (1, 2, 0))
+    absorb = jnp.transpose(absorption, (1, 2, 0))
+    depth = leaf.shape[1]
     px = lax.rem(lax.axis_index("gx"), 2).astype(jnp.int32).reshape(1)
     py = lax.rem(lax.axis_index("gy"), 2).astype(jnp.int32).reshape(1)
     wide = nx + 2 * DEEP
     tall = ny + 2 * DEEP
     block = (nx, ny, lanes)
-    x_rows = DEEP * ny + ny + 2 * DEEP + 8 + DEEP // 4 * ny
-    y_rows = wide * DEEP + wide + 8 + wide // 4 * DEEP
+    across = ny * depth
+    x_rows = DEEP * ny + ny + 2 * DEEP + 8 + 2 * DEEP * (across // lanes)
+    y_rows = wide * DEEP + wide + 8 + 2 * wide
     root, absb, b0, xa, xb = call(
         begin_kernel,
-        (px, initial_guess, source, ra),
-        (block, block, block, (x_rows, lanes), (x_rows, lanes)),
+        (px, initial_guess, source, leaf, absorb),
+        ((nx, across), (nx, across), block, (x_rows, lanes), (x_rows, lanes)),
+        scratch=[pltpu.VMEM(block, jnp.float32)] * 2,
         scalars=1,
     )
     xa, xb = exchange(xa, xb, "gx")
@@ -521,7 +517,7 @@
     rootx, absx, b0x, edge, ya, yb = call(
         widen_kernel,
         (px, py, xa, xb, initial_guess, root, absb, b0),
-        (broad, broad, broad, (2, wide + 8, lanes), (y_rows, lanes), (y_rows, lanes)),
+        ((wide, across), (wide, across), broad, (2, wide + 8, lanes), (y_rows, lanes), (y_rows, lanes)),
         scratch=[pltpu.VMEM((2, ny, lanes), jnp.float32)],
         scalars=2,
     )

time: 53.7 us -> 51.7 us (0.963)
  Pallas kernels: 17.4 us -> 13.1 us
  local copies, waits for them, and re-layouts: 2.2 us -> 4.66 us
    pallas_call x4, Pallas kernels: 17.4 us -> 13.1 us  [call(): pl.pallas_call(kernel, out_shape=[jax.ShapeDtypeStruct(s, k) for s, k in...]
    unnamed x6 -> x12, local copies, waits for them, and re-layouts: 2.2 us -> 4.66 us
where the time goes in v2:
time: 51.7 us; the launch traced here: 51.4 us
  blocking collectives  25.4 us (49%)
  Pallas kernels  13.1 us (25%)
  local copies, waits for them, and re-layouts  4.66 us (9%)
  starting transfers between devices  4.49 us (9%)
  waiting for transfers between devices  3.07 us (6%)
  between operations  0.71 us (1%)
    all_to_all x1, blocking collectives, totals(): return lax.all_to_all(parts, ('gx', 'gy'), 0, 0)  25.4 us
    pallas_call x4, Pallas kernels, call(): pl.pallas_call(kernel, out_shape=[jax.ShapeDtypeStruct(s, k) for s, k in...  13.1 us
    unnamed x12, local copies, waits for them, and re-layouts  4.66 us
    ppermute x4, starting transfers between devices, exchange(): got.append(lax.ppermute(cells, axis, links))  4.49 us
    ppermute x4, waiting for transfers between devices, exchange(): got.append(lax.ppermute(cells, axis, links))  3.07 us
  transfers between devices with their start and end apart: 4, of which 2 were waited for; matrix products, arithmetic and copies ran while one was open for 0% of the time, Pallas kernels for 0%

profile of v2, /device:TPU:0, one launch (start us, length us, event | category | flops | bytes accessed | tf_op | source)
XLA Modules:
  0.0 51.4 jit_solution(5889756062363693103)
XLA Ops:
  0.6 0.0 copy-start
  0.6 0.9 %copy-done = f32[32,16,128]{2,1,0:T(8,128)S(1)} copy-done((f32[32,16,128]{2,1,0:T(8,128)S(1)}, f32[32,16,128]{2,1,0:T(8,128)}, u32[]{:S(2)}) %copy-start) | copy-done | bytes 262168
  1.6 0.0 copy-start.3
  1.6 0.9 %copy-done.3 = f32[32,16,128]{2,1,0:T(8,128)S(1)} copy-done((f32[32,16,128]{2,1,0:T(8,128)S(1)}, f32[32,16,128]{2,1,0:T(8,128)}, u32[]{:S(2)}) %copy-start.3) | copy-done | bytes 262168
  2.5 0.0 copy-start.4
  2.5 0.9 %copy-done.4 = f32[32,16,16]{0,2,1:T(8,128)S(1)} copy-done((f32[32,16,16]{0,2,1:T(8,128)S(1)}, f32[32,16,16]{0,2,1:T(8,128)}, u32[]{:S(2)}) %copy-start.4) | copy-done | bytes 32792
  3.4 0.0 copy-start.5
  3.4 0.9 %copy-done.5 = f32[32,16,16]{0,2,1:T(8,128)S(1)} copy-done((f32[32,16,16]{0,2,1:T(8,128)S(1)}, f32[32,16,16]{0,2,1:T(8,128)}, u32[]{:S(2)}) %copy-start.5) | copy-done | bytes 32792
  4.3 0.0 copy-start.2
  4.4 0.7 %shard_map.59 = (f32[32,256]{1,0:T(8,128)S(1)}, f32[32,256]{1,0:T(8,128)S(1)}, f32[32,16,128]{2,1,0:T(8,128)S(1)}, f32[200,128]{1,0:T(8,128)S(1)}, f32[200,128]{1,0:T(8,128)S(1)}) custom-call(s32[1]{0:T(128)} %bitcast.1.px, f32[32,16,128]{2,1,0:T(8,128)S(1)} %copy-done, f32[32,16,128]{2,1,0:T(8,128)S(1)} %copy-done.3, f32[16,16,32]{2,1,0:T(8,128)S(1)} %bitcast.4, ...), custom_call_target="tpu_custom_call" | custom-call | tf_op jit(solution)/shard_map/pallas_call | solution.py:453
  5.1 3.1 %collective-permute-start = (f32[200,128]{1,0:T(8,128)S(1)}, f32[200,128]{1,0:T(8,128)S(1)}, u32[]{:S(2)}, u32[]{:S(2)}) collective-permute-start(f32[200,128]{1,0:T(8,128)S(1)} %get-tuple-element.16), channel_id=1, source_target_pairs={{0,8},{8,0},{16,24},{24,16},{1,9},{9,1},{17,25},{25,17},{2,10},{10... | collective-permute-start | bytes 307208 | tf_op jit(solution)/shard_map/ppermute | solution.py:473
  8.2 0.7 %collective-permute-start.1 = (f32[200,128]{1,0:T(8,128)S(1)}, f32[200,128]{1,0:T(8,128)S(1)}, u32[]{:S(2)}, u32[]{:S(2)}) collective-permute-start(f32[200,128]{1,0:T(8,128)S(1)} %get-tuple-element.17), channel_id=1, source_target_pairs={{8,16},{16,8},{9,17},{17,9},{10,18},{18,10},{11,19},{19,11},{12,20... | collective-permute-start | bytes 307208 | tf_op jit(solution)/shard_map/ppermute | solution.py:473
  8.8 2.2 %collective-permute-done.recv_a = f32[200,128]{1,0:T(8,128)S(1)} collective-permute-done((f32[200,128]{1,0:T(8,128)S(1)}, f32[200,128]{1,0:T(8,128)S(1)}, u32[]{:S(2)}, u32[]{:S(2)}) %collective-permute-start) | collective-permute-done | bytes 102432 | tf_op jit(solution)/shard_map/ppermute | solution.py:473
  11.1 0.0 collective-permute-done.1.recv_b
  11.1 0.0 copy-start.1
  11.1 0.9 %copy-done.1 = f32[32,16,128]{2,1,0:T(8,128)S(1)} copy-done((f32[32,16,128]{2,1,0:T(8,128)S(1)}, f32[32,16,128]{2,1,0:T(8,128)}, u32[]{:S(2)}) %copy-start.1) | copy-done | bytes 262168
  12.0 0.3 shard_map.60
  12.3 0.1 collective-permute-start.2
  12.4 0.7 %collective-permute-start.3 = (f32[536,128]{1,0:T(8,128)S(1)}, f32[536,128]{1,0:T(8,128)S(1)}, u32[]{:S(2)}, u32[]{:S(2)}) collective-permute-start(f32[536,128]{1,0:T(8,128)S(1)} %get-tuple-element.22), channel_id=1, source_target_pairs={{1,2},{2,1},{3,4},{4,3},{5,6},{6,5},{9,10},{10,9},{11,12},{12,11},... | collective-permute-start | bytes 823304 | tf_op jit(solution)/shard_map/ppermute | solution.py:473
  13.1 0.9 %collective-permute-done.2.recv_a = f32[536,128]{1,0:T(8,128)S(1)} collective-permute-done((f32[536,128]{1,0:T(8,128)S(1)}, f32[536,128]{1,0:T(8,128)S(1)}, u32[]{:S(2)}, u32[]{:S(2)}) %collective-permute-start.2) | collective-permute-done | bytes 274464 | tf_op jit(solution)/shard_map/ppermute | solution.py:473
  13.9 0.0 collective-permute-done.3.recv_b
  13.9 7.4 %shard_map.61 = (bf16[512,1152]{1,0:T(8,128)(2,1)S(1)}, bf16[512,1152]{1,0:T(8,128)(2,1)S(1)}, f32[32,8,128]{2,1,0:T(8,128)S(1)}) custom-call(s32[1]{0:T(128)} %bitcast.py, f32[536,128]{1,0:T(8,128)S(1)} %collective-permute-done.2.recv_a, f32[536,128]{1,0:T(8,128)S(1)} %collective-permute-done.3.recv_b, f32[48,256]{1,0:T(8,128)S(1)} %get-tuple-element.23.rootx, ...), custom_call_target="tpu_custom_call" | custom-call | tf_op jit(solution)/shard_map/pallas_call | solution.py:453
  21.3 25.4 %all_to_all.5.parts = f32[32,8,128]{2,1,0:T(8,128)S(1)} all-to-all(f32[32,8,128]{2,1,0:T(8,128)S(1)} %get-tuple-element.29), channel_id=1, replica_groups=mesh['gx'=4,'gy'=8] {'gx','gy'}, dimensions={0} | all-to-all | bytes 262144 | tf_op jit(solution)/shard_map/all_to_all | solution.py:491
  46.8 0.0 copy-done.2
  46.8 4.7 %shard_map.62 = (f32[32,16,128]{2,1,0:T(8,128)}, f32[32,16,128]{2,1,0:T(8,128)}) custom-call(f32[32,16,128]{2,1,0:T(8,128)S(1)} %copy-done.2, bf16[512,1152]{1,0:T(8,128)(2,1)S(1)} %get-tuple-element.27.rough, bf16[512,1152]{1,0:T(8,128)(2,1)S(1)} %get-tuple-element.28.fine, f32[32,8,128]{2,1,0:T(8,128)S(1)} %all_to_all.5.parts), custom_call_target="tpu_custom_call" | custom-call | tf_op jit(solution)/shard_map/pallas_call | solution.py:453
Async XLA Ops:
  0.6 1.0 %copy-start = (f32[32,16,128]{2,1,0:T(8,128)S(1)}, f32[32,16,128]{2,1,0:T(8,128)}, u32[]{:S(2)}) copy-start(f32[32,16,128]{2,1,0:T(8,128)} %guess.5) | copy-start | bytes 786436
  1.6 0.9 %copy-start.3 = (f32[32,16,128]{2,1,0:T(8,128)S(1)}, f32[32,16,128]{2,1,0:T(8,128)}, u32[]{:S(2)}) copy-start(f32[32,16,128]{2,1,0:T(8,128)} %source.1) | copy-start | bytes 786436
  2.5 0.9 %copy-start.4 = (f32[32,16,16]{0,2,1:T(8,128)S(1)}, f32[32,16,16]{0,2,1:T(8,128)}, u32[]{:S(2)}) copy-start(f32[32,16,16]{0,2,1:T(8,128)} %param.6) | copy-start | bytes 98308
  3.4 0.9 %copy-start.5 = (f32[32,16,16]{0,2,1:T(8,128)S(1)}, f32[32,16,16]{0,2,1:T(8,128)}, u32[]{:S(2)}) copy-start(f32[32,16,16]{0,2,1:T(8,128)} %param.7) | copy-start | bytes 98308
  4.3 42.4 %copy-start.2 = (f32[32,16,128]{2,1,0:T(8,128)S(1)}, f32[32,16,128]{2,1,0:T(8,128)}, u32[]{:S(2)}) copy-start(f32[32,16,128]{2,1,0:T(8,128)} %guess.5) | copy-start | bytes 786436
  5.1 6.0 %collective-permute-start = (f32[200,128]{1,0:T(8,128)S(1)}, f32[200,128]{1,0:T(8,128)S(1)}, u32[]{:S(2)}, u32[]{:S(2)}) collective-permute-start(f32[200,128]{1,0:T(8,128)S(1)} %get-tuple-element.16), channel_id=1, source_target_pairs={{0,8},{8,0},{16,24},{24,16},{1,9},{9,1},{17,25},{25,17},{2,10},{10... | collective-permute-start | bytes 307208 | tf_op jit(solution)/shard_map/ppermute | solution.py:473
  8.2 2.9 %collective-permute-start.1 = (f32[200,128]{1,0:T(8,128)S(1)}, f32[200,128]{1,0:T(8,128)S(1)}, u32[]{:S(2)}, u32[]{:S(2)}) collective-permute-start(f32[200,128]{1,0:T(8,128)S(1)} %get-tuple-element.17), channel_id=1, source_target_pairs={{8,16},{16,8},{9,17},{17,9},{10,18},{18,10},{11,19},{19,11},{12,20... | collective-permute-start | bytes 307208 | tf_op jit(solution)/shard_map/ppermute | solution.py:473
  11.1 1.0 %copy-start.1 = (f32[32,16,128]{2,1,0:T(8,128)S(1)}, f32[32,16,128]{2,1,0:T(8,128)}, u32[]{:S(2)}) copy-start(f32[32,16,128]{2,1,0:T(8,128)} %guess.5) | copy-start | bytes 786436
  12.3 1.6 %collective-permute-start.2 = (f32[536,128]{1,0:T(8,128)S(1)}, f32[536,128]{1,0:T(8,128)S(1)}, u32[]{:S(2)}, u32[]{:S(2)}) collective-permute-start(f32[536,128]{1,0:T(8,128)S(1)} %get-tuple-element.21), channel_id=1, source_target_pairs={{0,1},{1,0},{2,3},{3,2},{4,5},{5,4},{6,7},{7,6},{8,9},{9,8},{10,11... | collective-permute-start | bytes 823304 | tf_op jit(solution)/shard_map/ppermute | solution.py:473
  12.4 1.5 %collective-permute-start.3 = (f32[536,128]{1,0:T(8,128)S(1)}, f32[536,128]{1,0:T(8,128)S(1)}, u32[]{:S(2)}, u32[]{:S(2)}) collective-permute-start(f32[536,128]{1,0:T(8,128)S(1)} %get-tuple-element.22), channel_id=1, source_target_pairs={{1,2},{2,1},{3,4},{4,3},{5,6},{6,5},{9,10},{10,9},{11,12},{12,11},... | collective-permute-start | bytes 823304 | tf_op jit(solution)/shard_map/ppermute | solution.py:473

commit v3 on v2

--- a/solution.py
+++ b/solution.py
@@ -16,7 +16,7 @@
 CENTRE = 10.3
 HALF_WIDTH = 9.8
 RIDGE = 0.05
-PANEL = 8
+PANEL = 16
 VMEM_BYTES = 48 * 1024 * 1024
 
 
@@ -75,15 +75,31 @@
     return jnp.stack(out)
 
 
-def begin_kernel(px, guess, source, leaf, absorb, root_o, abs_o, b0_o, send_a, send_b, root, absb):
+def begin_kernel(px, *refs):
+    far, refs = refs[:4], refs[4:]
+    (root_o, abs_o, b0_o, edge_o, face_o, send_a, send_b), refs = refs[:7], refs[7:]
+    guess, source, leaf, absorb, root, absb, sems = refs
+    copies = [
+        pltpu.make_async_copy(there, here, sems.at[i])
+        for i, (there, here) in enumerate(zip(far, (guess, source, leaf, absorb)))
+    ]
+    for i in (2, 3, 0, 1):
+        copies[i].start()
     nx, ny, _ = guess.shape
     depth = leaf.shape[1]
+    copies[2].wait()
+    copies[3].wait()
     turned = jnp.transpose(leaf[...].reshape(ny * depth, nx))
     root_o[...] = jnp.sqrt(PEAK_COND / (1.0 + turned))
     abs_o[...] = jnp.transpose(absorb[...].reshape(ny * depth, nx))
     for part, wide in ((root_o, root), (abs_o, absb)):
         for y in range(0, ny, NRHS):
             wide[:, y : y + NRHS, :] = spread(part[:, y * depth : (y + NRHS) * depth])
+    copies[0].wait()
+    copies[1].wait()
+    for at, col, face in ((0, 0, 0), (1, ny - 1, nx - 1)):
+        edge_o[at] = guess[:, col, :]
+        face_o[at] = guess[face]
     zero = jnp.zeros((ny, LANES), jnp.float32)
 
     def pair(x, field):
@@ -133,15 +149,16 @@
 
 
 def widen_kernel(
-    px, py, recv_a, recv_b, guess, root, absb, b0, rootx, absx, b0x, edge, send_a, send_b, face
+    px, py, recv_a, recv_b, edge_own, face_own, root, absb, b0,
+    rootx, absx, b0x, edge, send_a, send_b, face
 ):
-    nx, ny, _ = guess.shape
+    nx, ny, _ = b0.shape
     wide = nx + 2 * DEEP
     rootx[DEEP : DEEP + nx] = root[...]
     absx[DEEP : DEEP + nx] = absb[...]
     b0x[DEEP : DEEP + nx] = b0[...]
-    for at, col in ((0, 0), (1, ny - 1)):
-        edge[at, DEEP : DEEP + nx] = guess[:, col, :]
+    for at in (0, 1):
+        edge[at, DEEP : DEEP + nx] = edge_own[at]
         edge[at, wide : wide + 8] = jnp.zeros((8, LANES), jnp.float32)
 
     def read(msg, x0, side):
@@ -178,9 +195,9 @@
         ]
         return jnp.concatenate(parts, axis=1)[0]
 
-    for side, out_x, in_x, own in ((0, DEEP - 1, DEEP, 0), (1, DEEP + nx, DEEP + nx - 1, nx - 1)):
+    for side, out_x, in_x in ((0, DEEP - 1, DEEP), (1, DEEP + nx, DEEP + nx - 1)):
         va, ra = face[side], root_line(out_x)
-        vb, rb = guess[own], root_line(in_x)
+        vb, rb = face_own[side], root_line(in_x)
         fix_a = ra * (cross_sum(rb * vb, row_sum_zero) - va * cross_sum(rb, row_sum_zero))
         fix_b = rb * (cross_sum(ra * va, row_sum_zero) - vb * cross_sum(ra, row_sum_zero))
         b0x[out_x] = b0x[out_x] + fix_a
@@ -447,9 +464,9 @@
         rest[at] = out[:, :, LANES:]
 
 
-def call(kernel, ins, outs, scratch=(), scalars=0, kinds=None):
+def call(kernel, ins, outs, scratch=(), scalars=0, kinds=None, space=pltpu.VMEM):
     specs = [pl.BlockSpec(memory_space=pltpu.SMEM)] * scalars
-    specs += [pl.BlockSpec(memory_space=pltpu.VMEM)] * (len(ins) - scalars)
+    specs += [pl.BlockSpec(memory_space=space)] * (len(ins) - scalars)
     result = pl.pallas_call(
         kernel,
         out_shape=[
@@ -505,18 +522,28 @@
     across = ny * depth
     x_rows = DEEP * ny + ny + 2 * DEEP + 8 + 2 * DEEP * (across // lanes)
     y_rows = wide * DEEP + wide + 8 + 2 * wide
-    root, absb, b0, xa, xb = call(
+    sides = ((2, nx, lanes), (2, ny, lanes))
+    root, absb, b0, edge, face, xa, xb = call(
         begin_kernel,
         (px, initial_guess, source, leaf, absorb),
-        ((nx, across), (nx, across), block, (x_rows, lanes), (x_rows, lanes)),
-        scratch=[pltpu.VMEM(block, jnp.float32)] * 2,
+        ((nx, across), (nx, across), block, *sides, (x_rows, lanes), (x_rows, lanes)),
+        scratch=[
+            pltpu.VMEM(block, jnp.float32),
+            pltpu.VMEM(block, jnp.float32),
+            pltpu.VMEM(leaf.shape, jnp.float32),
+            pltpu.VMEM(leaf.shape, jnp.float32),
+            pltpu.VMEM(block, jnp.float32),
+            pltpu.VMEM(block, jnp.float32),
+            pltpu.SemaphoreType.DMA((4,)),
+        ],
         scalars=1,
+        space=pltpu.HBM,
     )
     xa, xb = exchange(xa, xb, "gx")
     broad = (wide, ny, lanes)
     rootx, absx, b0x, edge, ya, yb = call(
         widen_kernel,
-        (px, py, xa, xb, initial_guess, root, absb, b0),
+        (px, py, xa, xb, edge, face, root, absb, b0),
         ((wide, across), (wide, across), broad, (2, wide + 8, lanes), (y_rows, lanes), (y_rows, lanes)),
         scratch=[pltpu.VMEM((2, ny, lanes), jnp.float32)],
         scalars=2,

time: 51.7 us -> 50.8 us (0.983)
  local copies, waits for them, and re-layouts: 4.66 us -> 3.71 us
    unnamed x12 -> x10, local copies, waits for them, and re-layouts: 4.66 us -> 3.71 us
where the time goes in v3:
time: 50.8 us; the launch traced here: 50.6 us
  blocking collectives  25.4 us (50%)
  Pallas kernels  13.2 us (26%)
  starting transfers between devices  4.5 us (9%)
  local copies, waits for them, and re-layouts  3.71 us (7%)
  waiting for transfers between devices  3.07 us (6%)
  between operations  0.71 us (1%)
    all_to_all x1, blocking collectives, totals(): return lax.all_to_all(parts, ('gx', 'gy'), 0, 0)  25.4 us
    pallas_call x4, Pallas kernels, call(): pl.pallas_call(kernel, out_shape=[jax.ShapeDtypeStruct(s, k) for s, k in...  13.2 us
    ppermute x4, starting transfers between devices, exchange(): got.append(lax.ppermute(cells, axis, links))  4.5 us
    unnamed x10, local copies, waits for them, and re-layouts  3.71 us
    ppermute x4, waiting for transfers between devices, exchange(): got.append(lax.ppermute(cells, axis, links))  3.07 us
  transfers between devices with their start and end apart: 4, of which 2 were waited for; matrix products, arithmetic and copies ran while one was open for 0% of the time, Pallas kernels for 0%

profile of v3, /device:TPU:0, one launch (start us, length us, event | category | flops | bytes accessed | tf_op | source)
XLA Modules:
  0.0 50.6 jit_solution(16572916873741269387)
XLA Ops:
  0.6 0.0 copy-start
  0.6 0.9 %copy-done = f32[32,16,128]{2,1,0:T(8,128)S(1)} copy-done((f32[32,16,128]{2,1,0:T(8,128)S(1)}, f32[32,16,128]{2,1,0:T(8,128)}, u32[]{:S(2)}) %copy-start) | copy-done | bytes 262168
  1.6 0.0 copy-start.2
  1.6 0.9 %copy-done.2 = f32[32,16,128]{2,1,0:T(8,128)S(1)} copy-done((f32[32,16,128]{2,1,0:T(8,128)S(1)}, f32[32,16,128]{2,1,0:T(8,128)}, u32[]{:S(2)}) %copy-start.2) | copy-done | bytes 262168
  2.5 0.0 copy-start.3
  2.5 0.9 %copy-done.3 = f32[32,16,16]{0,2,1:T(8,128)S(1)} copy-done((f32[32,16,16]{0,2,1:T(8,128)S(1)}, f32[32,16,16]{0,2,1:T(8,128)}, u32[]{:S(2)}) %copy-start.3) | copy-done | bytes 32792
  3.4 0.0 copy-start.4
  3.4 0.9 %copy-done.4 = f32[32,16,16]{0,2,1:T(8,128)S(1)} copy-done((f32[32,16,16]{0,2,1:T(8,128)S(1)}, f32[32,16,16]{0,2,1:T(8,128)}, u32[]{:S(2)}) %copy-start.4) | copy-done | bytes 32792
  4.3 1.2 %shard_map.59 = (f32[32,256]{1,0:T(8,128)S(1)}, f32[32,256]{1,0:T(8,128)S(1)}, f32[32,16,128]{2,1,0:T(8,128)S(1)}, f32[2,32,128]{2,1,0:T(8,128)S(1)}, f32[2,16,1...) custom-call(s32[1]{0:T(128)} %bitcast.1.px, f32[32,16,128]{2,1,0:T(8,128)S(1)} %copy-done, ...), custom_call_target="tpu_custom_call" | custom-call | tf_op jit(solution)/shard_map/pallas_call | solution.py:470
  5.5 0.0 copy-start.1
  5.5 3.1 %collective-permute-start = (f32[200,128]{1,0:T(8,128)S(1)}, f32[200,128]{1,0:T(8,128)S(1)}, u32[]{:S(2)}, u32[]{:S(2)}) collective-permute-start(f32[200,128]{1,0:T(8,128)S(1)} %get-tuple-element.18), channel_id=1, source_target_pairs={{0,8},{8,0},{16,24},{24,16},{1,9},{9,1},{17,25},{25,17},{2,10},{10... | collective-permute-start | bytes 307208 | tf_op jit(solution)/shard_map/ppermute | solution.py:490
  8.6 0.7 %collective-permute-start.1 = (f32[200,128]{1,0:T(8,128)S(1)}, f32[200,128]{1,0:T(8,128)S(1)}, u32[]{:S(2)}, u32[]{:S(2)}) collective-permute-start(f32[200,128]{1,0:T(8,128)S(1)} %get-tuple-element.19), channel_id=1, source_target_pairs={{8,16},{16,8},{9,17},{17,9},{10,18},{18,10},{11,19},{19,11},{12,20... | collective-permute-start | bytes 307208 | tf_op jit(solution)/shard_map/ppermute | solution.py:490
  9.3 2.2 %collective-permute-done.recv_a = f32[200,128]{1,0:T(8,128)S(1)} collective-permute-done((f32[200,128]{1,0:T(8,128)S(1)}, f32[200,128]{1,0:T(8,128)S(1)}, u32[]{:S(2)}, u32[]{:S(2)}) %collective-permute-start) | collective-permute-done | bytes 102432 | tf_op jit(solution)/shard_map/ppermute | solution.py:490
  11.5 0.0 collective-permute-done.1.recv_b
  11.5 0.3 shard_map.60
  11.8 0.1 collective-permute-start.2
  11.9 0.7 %collective-permute-start.3 = (f32[536,128]{1,0:T(8,128)S(1)}, f32[536,128]{1,0:T(8,128)S(1)}, u32[]{:S(2)}, u32[]{:S(2)}) collective-permute-start(f32[536,128]{1,0:T(8,128)S(1)} %get-tuple-element.26), channel_id=1, source_target_pairs={{1,2},{2,1},{3,4},{4,3},{5,6},{6,5},{9,10},{10,9},{11,12},{12,11},... | collective-permute-start | bytes 823304 | tf_op jit(solution)/shard_map/ppermute | solution.py:490
  12.5 0.9 %collective-permute-done.2.recv_a = f32[536,128]{1,0:T(8,128)S(1)} collective-permute-done((f32[536,128]{1,0:T(8,128)S(1)}, f32[536,128]{1,0:T(8,128)S(1)}, u32[]{:S(2)}, u32[]{:S(2)}) %collective-permute-start.2) | collective-permute-done | bytes 274464 | tf_op jit(solution)/shard_map/ppermute | solution.py:490
  13.4 0.0 collective-permute-done.3.recv_b
  13.4 7.4 %shard_map.61 = (bf16[512,1152]{1,0:T(8,128)(2,1)S(1)}, bf16[512,1152]{1,0:T(8,128)(2,1)S(1)}, f32[32,8,128]{2,1,0:T(8,128)S(1)}) custom-call(s32[1]{0:T(128)} %bitcast.py, f32[536,128]{1,0:T(8,128)S(1)} %collective-permute-done.2.recv_a, f32[536,128]{1,0:T(8,128)S(1)} %collective-permute-done.3.recv_b, f32[48,256]{1,0:T(8,128)S(1)} %get-tuple-element.27.rootx, ...), custom_call_target="tpu_custom_call" | custom-call | tf_op jit(solution)/shard_map/pallas_call | solution.py:470
  20.8 25.4 %all_to_all.5.parts = f32[32,8,128]{2,1,0:T(8,128)S(1)} all-to-all(f32[32,8,128]{2,1,0:T(8,128)S(1)} %get-tuple-element.33), channel_id=1, replica_groups=mesh['gx'=4,'gy'=8] {'gx','gy'}, dimensions={0} | all-to-all | bytes 262144 | tf_op jit(solution)/shard_map/all_to_all | solution.py:508
  46.2 0.0 copy-done.1
  46.2 4.3 %shard_map.62 = (f32[32,16,128]{2,1,0:T(8,128)}, f32[32,16,128]{2,1,0:T(8,128)}) custom-call(f32[32,16,128]{2,1,0:T(8,128)S(1)} %copy-done.1, bf16[512,1152]{1,0:T(8,128)(2,1)S(1)} %get-tuple-element.31.rough, bf16[512,1152]{1,0:T(8,128)(2,1)S(1)} %get-tuple-element.32.fine, f32[32,8,128]{2,1,0:T(8,128)S(1)} %all_to_all.5.parts), custom_call_target="tpu_custom_call" | custom-call | tf_op jit(solution)/shard_map/pallas_call | solution.py:470
Async XLA Ops:
  0.6 1.0 %copy-start = (f32[32,16,128]{2,1,0:T(8,128)S(1)}, f32[32,16,128]{2,1,0:T(8,128)}, u32[]{:S(2)}) copy-start(f32[32,16,128]{2,1,0:T(8,128)} %guess.1) | copy-start | bytes 786436
  1.6 0.9 %copy-start.2 = (f32[32,16,128]{2,1,0:T(8,128)S(1)}, f32[32,16,128]{2,1,0:T(8,128)}, u32[]{:S(2)}) copy-start(f32[32,16,128]{2,1,0:T(8,128)} %refs_1_.1) | copy-start | bytes 786436
  2.5 0.9 %copy-start.3 = (f32[32,16,16]{0,2,1:T(8,128)S(1)}, f32[32,16,16]{0,2,1:T(8,128)}, u32[]{:S(2)}) copy-start(f32[32,16,16]{0,2,1:T(8,128)} %param.6) | copy-start | bytes 98308
  3.4 0.9 %copy-start.4 = (f32[32,16,16]{0,2,1:T(8,128)S(1)}, f32[32,16,16]{0,2,1:T(8,128)}, u32[]{:S(2)}) copy-start(f32[32,16,16]{0,2,1:T(8,128)} %param.7) | copy-start | bytes 98308
  5.5 40.7 %copy-start.1 = (f32[32,16,128]{2,1,0:T(8,128)S(1)}, f32[32,16,128]{2,1,0:T(8,128)}, u32[]{:S(2)}) copy-start(f32[32,16,128]{2,1,0:T(8,128)} %guess.1) | copy-start | bytes 786436
  5.5 6.0 %collective-permute-start = (f32[200,128]{1,0:T(8,128)S(1)}, f32[200,128]{1,0:T(8,128)S(1)}, u32[]{:S(2)}, u32[]{:S(2)}) collective-permute-start(f32[200,128]{1,0:T(8,128)S(1)} %get-tuple-element.18), channel_id=1, source_target_pairs={{0,8},{8,0},{16,24},{24,16},{1,9},{9,1},{17,25},{25,17},{2,10},{10... | collective-permute-start | bytes 307208 | tf_op jit(solution)/shard_map/ppermute | solution.py:490
  8.6 2.9 %collective-permute-start.1 = (f32[200,128]{1,0:T(8,128)S(1)}, f32[200,128]{1,0:T(8,128)S(1)}, u32[]{:S(2)}, u32[]{:S(2)}) collective-permute-start(f32[200,128]{1,0:T(8,128)S(1)} %get-tuple-element.19), channel_id=1, source_target_pairs={{8,16},{16,8},{9,17},{17,9},{10,18},{18,10},{11,19},{19,11},{12,20... | collective-permute-start | bytes 307208 | tf_op jit(solution)/shard_map/ppermute | solution.py:490
  11.8 1.6 %collective-permute-start.2 = (f32[536,128]{1,0:T(8,128)S(1)}, f32[536,128]{1,0:T(8,128)S(1)}, u32[]{:S(2)}, u32[]{:S(2)}) collective-permute-start(f32[536,128]{1,0:T(8,128)S(1)} %get-tuple-element.25), channel_id=1, source_target_pairs={{0,1},{1,0},{2,3},{3,2},{4,5},{5,4},{6,7},{7,6},{8,9},{9,8},{10,11... | collective-permute-start | bytes 823304 | tf_op jit(solution)/shard_map/ppermute | solution.py:490
  11.9 1.5 %collective-permute-start.3 = (f32[536,128]{1,0:T(8,128)S(1)}, f32[536,128]{1,0:T(8,128)S(1)}, u32[]{:S(2)}, u32[]{:S(2)}) collective-permute-start(f32[536,128]{1,0:T(8,128)S(1)} %get-tuple-element.26), channel_id=1, source_target_pairs={{1,2},{2,1},{3,4},{4,3},{5,6},{6,5},{9,10},{10,9},{11,12},{12,11},... | collective-permute-start | bytes 823304 | tf_op jit(solution)/shard_map/ppermute | solution.py:490

commit v4 on v3

--- a/solution.py
+++ b/solution.py
@@ -18,6 +18,7 @@
 RIDGE = 0.05
 PANEL = 16
 VMEM_BYTES = 48 * 1024 * 1024
+BEGIN_BYTES = 55000 * 1024
 
 
 def lanes_of(shape):
@@ -75,9 +76,9 @@
     return jnp.stack(out)
 
 
-def begin_kernel(px, *refs):
+def begin_kernel(px, py, *refs):
     far, refs = refs[:4], refs[4:]
-    (root_o, abs_o, b0_o, edge_o, face_o, send_a, send_b), refs = refs[:7], refs[7:]
+    (root_o, abs_o, b0_o, edge_o, face_o, send_a, send_b, side_a, side_b), refs = refs[:9], refs[9:]
     guess, source, leaf, absorb, root, absb, sems = refs
     copies = [
         pltpu.make_async_copy(there, here, sems.at[i])
@@ -147,6 +148,25 @@
         write(send_b, nx - DEEP, nx - 1, nx - DEEP - 1)
         write(send_a, 0, 0, DEEP)
 
+    def write_side(out, y0, at):
+        n = (nx - 2) * DEEP
+        out[0:n] = b0_o[1 : nx - 1, y0 : y0 + DEEP, :].reshape(n, LANES)
+        out[n : n + nx] = edge_o[at]
+        n += nx
+        for part in (root_o, abs_o):
+            out[n : n + nx] = part[:, y0 * depth : (y0 + DEEP) * depth]
+            n += nx
+
+    @pl.when(py[0] == 0)
+    def _():
+        write_side(side_a, ny - DEEP, 1)
+        write_side(side_b, 0, 0)
+
+    @pl.when(py[0] == 1)
+    def _():
+        write_side(side_b, ny - DEEP, 1)
+        write_side(side_a, 0, 0)
+
 
 def widen_kernel(
     px, py, recv_a, recv_b, edge_own, face_own, root, absb, b0,
@@ -204,14 +224,19 @@
         b0x[in_x] = b0x[in_x] + fix_b
 
     def write(out, y0, at):
-        n = wide * DEEP
-        out[0:n] = b0x[:, y0 : y0 + DEEP, :].reshape(n, LANES)
-        out[n : n + wide + 8] = edge[at]
-        n += wide + 8
+        n = 0
+        for x0 in (0, DEEP + nx - 1):
+            m = (DEEP + 1) * DEEP
+            out[n : n + m] = b0x[x0 : x0 + DEEP + 1, y0 : y0 + DEEP, :].reshape(m, LANES)
+            n += m
         first = y0 * (LANES // NRHS)
-        for part in (rootx, absx):
-            out[n : n + wide] = part[:, first : first + LANES]
-            n += wide
+        for x0 in (0, DEEP + nx):
+            out[n : n + DEEP] = edge[at, x0 : x0 + DEEP]
+            n += DEEP
+            for part in (rootx, absx):
+                out[n : n + DEEP] = part[x0 : x0 + DEEP, first : first + LANES]
+                n += DEEP
+        out[n : n + 8] = edge[at, wide : wide + 8]
 
     @pl.when(py[0] == 0)
     def _():
@@ -230,7 +255,8 @@
 
 
 def basis_kernel(
-    py, recv_a, recv_b, rootx, absx, b0x, edge, rough, fine, moments, root, diag, far, f0, f1, f2
+    py, side_a, side_b, recv_a, recv_b, rootx, absx, b0x, edge,
+    rough, fine, moments, root, diag, far, f0, f1, f2
 ):
     wide, ny, _ = b0x.shape
     nx = wide - 2 * DEEP
@@ -242,24 +268,38 @@
             out[:, DEEP + y : 2 * DEEP + y, :] = spread(part[:, first : first + LANES])
     f0[:, DEEP : DEEP + ny, :] = b0x[...]
 
-    def read(msg, y0, side):
-        n = wide * DEEP
-        f0[:, y0 : y0 + DEEP, :] = msg[0:n].reshape(wide, DEEP, LANES)
-        far[side] = msg[n : n + wide + 8]
-        n += wide + 8
+    def read(inner, outer, y0, side):
+        n = (nx - 2) * DEEP
+        f0[DEEP + 1 : DEEP + nx - 1, y0 : y0 + DEEP, :] = inner[0:n].reshape(nx - 2, DEEP, LANES)
+        far[side, DEEP : DEEP + nx] = inner[n : n + nx]
+        n += nx
         for out in (root, diag):
-            out[:, y0 : y0 + DEEP, :] = spread(msg[n : n + wide])
-            n += wide
+            out[DEEP : DEEP + nx, y0 : y0 + DEEP, :] = spread(inner[n : n + nx])
+            n += nx
+        n = 0
+        for x0 in (0, DEEP + nx - 1):
+            m = (DEEP + 1) * DEEP
+            f0[x0 : x0 + DEEP + 1, y0 : y0 + DEEP, :] = outer[n : n + m].reshape(
+                DEEP + 1, DEEP, LANES
+            )
+            n += m
+        for x0 in (0, DEEP + nx):
+            far[side, x0 : x0 + DEEP] = outer[n : n + DEEP]
+            n += DEEP
+            for out in (root, diag):
+                out[x0 : x0 + DEEP, y0 : y0 + DEEP, :] = spread(outer[n : n + DEEP])
+                n += DEEP
+        far[side, wide : wide + 8] = outer[n : n + 8]
 
     @pl.when(py[0] == 0)
     def _():
-        read(recv_b, 0, 0)
-        read(recv_a, DEEP + ny, 1)
+        read(side_b, recv_b, 0, 0)
+        read(side_a, recv_a, DEEP + ny, 1)
 
     @pl.when(py[0] == 1)
     def _():
-        read(recv_a, 0, 0)
-        read(recv_b, DEEP + ny, 1)
+        read(side_a, recv_a, 0, 0)
+        read(side_b, recv_b, DEEP + ny, 1)
 
     row = lax.broadcasted_iota(jnp.int32, (wide, LANES), 0)
 
@@ -464,7 +504,7 @@
         rest[at] = out[:, :, LANES:]
 
 
-def call(kernel, ins, outs, scratch=(), scalars=0, kinds=None, space=pltpu.VMEM):
+def call(kernel, ins, outs, scratch=(), scalars=0, kinds=None, space=pltpu.VMEM, limit=VMEM_BYTES):
     specs = [pl.BlockSpec(memory_space=pltpu.SMEM)] * scalars
     specs += [pl.BlockSpec(memory_space=space)] * (len(ins) - scalars)
     result = pl.pallas_call(
@@ -475,7 +515,7 @@
         in_specs=specs,
         out_specs=[pl.BlockSpec(memory_space=pltpu.VMEM)] * len(outs),
         scratch_shapes=list(scratch),
-        compiler_params=pltpu.CompilerParams(vmem_limit_bytes=VMEM_BYTES),
+        compiler_params=pltpu.CompilerParams(vmem_limit_bytes=limit),
     )(*ins)
     return result
 
@@ -521,12 +561,15 @@
     block = (nx, ny, lanes)
     across = ny * depth
     x_rows = DEEP * ny + ny + 2 * DEEP + 8 + 2 * DEEP * (across // lanes)
-    y_rows = wide * DEEP + wide + 8 + 2 * wide
+    side_rows = (nx - 2) * DEEP + 3 * nx
+    y_rows = 2 * (DEEP + 1) * DEEP + 6 * DEEP + 8
     sides = ((2, nx, lanes), (2, ny, lanes))
-    root, absb, b0, edge, face, xa, xb = call(
+    root, absb, b0, edge, face, xa, xb, sa, sb = call(
         begin_kernel,
-        (px, initial_guess, source, leaf, absorb),
-        ((nx, across), (nx, across), block, *sides, (x_rows, lanes), (x_rows, lanes)),
+        (px, py, initial_guess, source, leaf, absorb),
+        ((nx, across), (nx, across), block, *sides)
+        + ((x_rows, lanes),) * 2
+        + ((side_rows, lanes),) * 2,
         scratch=[
             pltpu.VMEM(block, jnp.float32),
             pltpu.VMEM(block, jnp.float32),
@@ -536,10 +579,12 @@
             pltpu.VMEM(block, jnp.float32),
             pltpu.SemaphoreType.DMA((4,)),
         ],
-        scalars=1,
+        scalars=2,
         space=pltpu.HBM,
+        limit=BEGIN_BYTES,
     )
     xa, xb = exchange(xa, xb, "gx")
+    sa, sb = exchange(sa, sb, "gy")
     broad = (wide, ny, lanes)
     rootx, absx, b0x, edge, ya, yb = call(
         widen_kernel,
@@ -555,7 +600,7 @@
     cells = nx * ny
     rough, fine, moments = call(
         basis_kernel,
-        (py, ya, yb, rootx, absx, b0x, edge),
+        (py, sa, sb, ya, yb, rootx, absx, b0x, edge),
         ((cells, (S + 1) * lanes), (cells, (S + 1) * lanes), (count, NRHS, lanes)),
         scratch=[frame, frame, pltpu.VMEM((2, wide + 8, lanes), jnp.float32), frame, frame, frame],
         scalars=1,

time: 50.8 us -> 46.1 us (0.907)
  blocking collectives: 25.4 us -> 21.2 us
  local copies, waits for them, and re-layouts: 3.71 us -> 0.96 us
  starting transfers between devices: 4.5 us -> 6.61 us
  Pallas kernels: 13.2 us -> 14.6 us
  waiting for transfers between devices: 3.07 us -> 1.74 us
    all_to_all x1, blocking collectives: 25.4 us -> 21.2 us  [totals(): return lax.all_to_all(parts, ('gx', 'gy'), 0, 0)]
    unnamed x10 -> x4, local copies, waits for them, and re-layouts: 3.71 us -> 0.96 us
    ppermute x4 -> x6, starting transfers between devices: 4.5 us -> 6.61 us  [exchange(): got.append(lax.ppermute(cells, axis, links))]
    pallas_call x4, Pallas kernels: 13.2 us -> 14.6 us  [call(): pl.pallas_call(kernel, out_shape=[jax.ShapeDtypeStruct(s, k) for s, k in...]
    ppermute x4 -> x6, waiting for transfers between devices: 3.07 us -> 1.74 us  [exchange(): got.append(lax.ppermute(cells, axis, links))]
  transfers between devices with their start and end apart: 4 -> 6, of which waited for: 2 -> 2; matrix products, arithmetic and copies ran while one was open for 0% -> 0% of each run, Pallas kernels for 0% -> 1%
where the time goes in v4:
time: 46.1 us; the launch traced here: 45.8 us
  blocking collectives  21.2 us (46%)
  Pallas kernels  14.6 us (32%)
  starting transfers between devices  6.61 us (14%)
  waiting for transfers between devices  1.74 us (4%)
  local copies, waits for them, and re-layouts  0.96 us (2%)
  between operations  0.72 us (2%)
    all_to_all x1, blocking collectives, totals(): return lax.all_to_all(parts, ('gx', 'gy'), 0, 0)  21.2 us
    pallas_call x4, Pallas kernels, call(): pl.pallas_call(kernel, out_shape=[jax.ShapeDtypeStruct(s, k) for s, k in...  14.6 us
    ppermute x6, starting transfers between devices, exchange(): got.append(lax.ppermute(cells, axis, links))  6.61 us
    ppermute x6, waiting for transfers between devices, exchange(): got.append(lax.ppermute(cells, axis, links))  1.74 us
    unnamed x4, local copies, waits for them, and re-layouts  0.96 us
  transfers between devices with their start and end apart: 6, of which 2 were waited for; matrix products, arithmetic and copies ran while one was open for 0% of the time, Pallas kernels for 1%

profile of v4, /device:TPU:0, one launch (start us, length us, event | category | flops | bytes accessed | tf_op | source)
XLA Modules:
  0.0 45.8 jit_solution(2433923339504286015)
XLA Ops:
  0.6 2.7 %shard_map.59 = (f32[32,256]{1,0:T(8,128)S(1)}, f32[32,256]{1,0:T(8,128)S(1)}, f32[32,16,128]{2,1,0:T(8,128)}, f32[2,32,128]{2,1,0:T(8,128)S(1)}, f32[2,16,128]{...) custom-call(s32[1]{0:T(128)} %bitcast.1.px, ...), custom_call_target="tpu_custom_call" | custom-call | tf_op jit(solution)/shard_map/pallas_call | solution.py:510
  3.3 0.0 copy-start
  3.3 3.1 %collective-permute-start.2 = (f32[200,128]{1,0:T(8,128)S(1)}, f32[200,128]{1,0:T(8,128)S(1)}, u32[]{:S(2)}, u32[]{:S(2)}) collective-permute-start(f32[200,128]{1,0:T(8,128)S(1)} %get-tuple-element.22), channel_id=1, source_target_pairs={{0,8},{8,0},{16,24},{24,16},{1,9},{9,1},{17,25},{25,17},{2,10},{10... | collective-permute-start | bytes 307208 | tf_op jit(solution)/shard_map/ppermute | solution.py:530
  6.4 0.7 %collective-permute-start.3 = (f32[200,128]{1,0:T(8,128)}, f32[200,128]{1,0:T(8,128)S(1)}, u32[]{:S(2)}, u32[]{:S(2)}) collective-permute-start(f32[200,128]{1,0:T(8,128)} %get-tuple-element.23), channel_id=1, source_target_pairs={{8,16},{16,8},{9,17},{17,9},{10,18},{18,10},{11,19},{19,11},{12,20... | collective-permute-start | bytes 307208 | tf_op jit(solution)/shard_map/ppermute | solution.py:530
  7.1 0.1 collective-permute-start
  7.2 0.7 %collective-permute-start.1 = (f32[336,128]{1,0:T(8,128)}, f32[336,128]{1,0:T(8,128)S(1)}, u32[]{:S(2)}, u32[]{:S(2)}) collective-permute-start(f32[336,128]{1,0:T(8,128)} %get-tuple-element.21), channel_id=1, source_target_pairs={{1,2},{2,1},{3,4},{4,3},{5,6},{6,5},{9,10},{10,9},{11,12},{12,11},... | collective-permute-start | bytes 516104 | tf_op jit(solution)/shard_map/ppermute | solution.py:530
  7.8 1.5 %collective-permute-done.2.recv_a = f32[200,128]{1,0:T(8,128)S(1)} collective-permute-done((f32[200,128]{1,0:T(8,128)S(1)}, f32[200,128]{1,0:T(8,128)S(1)}, u32[]{:S(2)}, u32[]{:S(2)}) %collective-permute-start.2) | collective-permute-done | bytes 102432 | tf_op jit(solution)/shard_map/ppermute | solution.py:530
  9.3 0.0 collective-permute-done.3.recv_b
  9.3 0.0 copy-start.1
  9.3 0.9 %copy-done.1 = f32[32,16,128]{2,1,0:T(8,128)S(1)} copy-done((f32[32,16,128]{2,1,0:T(8,128)S(1)}, f32[32,16,128]{2,1,0:T(8,128)}, u32[]{:S(2)}) %copy-start.1) | copy-done | bytes 262168
  10.3 0.2 shard_map.60
  10.5 1.5 %collective-permute-start.4 = (f32[200,128]{1,0:T(8,128)S(1)}, f32[200,128]{1,0:T(8,128)S(1)}, u32[]{:S(2)}, u32[]{:S(2)}) collective-permute-start(f32[200,128]{1,0:T(8,128)S(1)} %get-tuple-element.29), channel_id=1, source_target_pairs={{0,1},{1,0},{2,3},{3,2},{4,5},{5,4},{6,7},{7,6},{8,9},{9,8},{10,11... | collective-permute-start | bytes 307208 | tf_op jit(solution)/shard_map/ppermute | solution.py:530
  12.0 0.7 %collective-permute-start.5 = (f32[200,128]{1,0:T(8,128)S(1)}, f32[200,128]{1,0:T(8,128)S(1)}, u32[]{:S(2)}, u32[]{:S(2)}) collective-permute-start(f32[200,128]{1,0:T(8,128)S(1)} %get-tuple-element.30), channel_id=1, source_target_pairs={{1,2},{2,1},{3,4},{4,3},{5,6},{6,5},{9,10},{10,9},{11,12},{12,11},... | collective-permute-start | bytes 307208 | tf_op jit(solution)/shard_map/ppermute | solution.py:530
  12.6 0.0 collective-permute-done.side_a
  12.6 0.0 collective-permute-done.1.side_b
  12.7 0.3 collective-permute-done.4.recv_a
  12.9 0.0 collective-permute-done.5.recv_b
  12.9 7.4 %shard_map.61 = (bf16[512,1152]{1,0:T(8,128)(2,1)S(1)}, bf16[512,1152]{1,0:T(8,128)(2,1)S(1)}, f32[32,8,128]{2,1,0:T(8,128)S(1)}) custom-call(s32[1]{0:T(128)} %bitcast.py, f32[336,128]{1,0:T(8,128)S(1)} %collective-permute-done.side_a, f32[336,128]{1,0:T(8,128)S(1)} %collective-permute-done.1.side_b, f32[200,128]{1,0:T(8,128)S(1)} %collective-permute-done.4.recv_a, ...), custom_call_target="tpu_custom_call" | custom-call | tf_op jit(solution)/shard_map/pallas_call | solution.py:510
  20.3 21.2 %all_to_all.5.parts = f32[32,8,128]{2,1,0:T(8,128)S(1)} all-to-all(f32[32,8,128]{2,1,0:T(8,128)S(1)} %get-tuple-element.37), channel_id=1, replica_groups=mesh['gx'=4,'gy'=8] {'gx','gy'}, dimensions={0} | all-to-all | bytes 262144 | tf_op jit(solution)/shard_map/all_to_all | solution.py:548
  41.5 0.0 copy-done
  41.5 4.3 %shard_map.62 = (f32[32,16,128]{2,1,0:T(8,128)}, f32[32,16,128]{2,1,0:T(8,128)}) custom-call(f32[32,16,128]{2,1,0:T(8,128)S(1)} %copy-done, bf16[512,1152]{1,0:T(8,128)(2,1)S(1)} %get-tuple-element.35.rough, bf16[512,1152]{1,0:T(8,128)(2,1)S(1)} %get-tuple-element.36.fine, f32[32,8,128]{2,1,0:T(8,128)S(1)} %all_to_all.5.parts), custom_call_target="tpu_custom_call" | custom-call | tf_op jit(solution)/shard_map/pallas_call | solution.py:510
Async XLA Ops:
  3.3 38.2 %copy-start = (f32[32,16,128]{2,1,0:T(8,128)S(1)}, f32[32,16,128]{2,1,0:T(8,128)}, u32[]{:S(2)}) copy-start(f32[32,16,128]{2,1,0:T(8,128)} %guess.1) | copy-start | bytes 786436
  3.3 6.0 %collective-permute-start.2 = (f32[200,128]{1,0:T(8,128)S(1)}, f32[200,128]{1,0:T(8,128)S(1)}, u32[]{:S(2)}, u32[]{:S(2)}) collective-permute-start(f32[200,128]{1,0:T(8,128)S(1)} %get-tuple-element.22), channel_id=1, source_target_pairs={{0,8},{8,0},{16,24},{24,16},{1,9},{9,1},{17,25},{25,17},{2,10},{10... | collective-permute-start | bytes 307208 | tf_op jit(solution)/shard_map/ppermute | solution.py:530
  6.4 2.9 %collective-permute-start.3 = (f32[200,128]{1,0:T(8,128)}, f32[200,128]{1,0:T(8,128)S(1)}, u32[]{:S(2)}, u32[]{:S(2)}) collective-permute-start(f32[200,128]{1,0:T(8,128)} %get-tuple-element.23), channel_id=1, source_target_pairs={{8,16},{16,8},{9,17},{17,9},{10,18},{18,10},{11,19},{19,11},{12,20... | collective-permute-start | bytes 307208 | tf_op jit(solution)/shard_map/ppermute | solution.py:530
  7.1 5.6 %collective-permute-start = (f32[336,128]{1,0:T(8,128)}, f32[336,128]{1,0:T(8,128)S(1)}, u32[]{:S(2)}, u32[]{:S(2)}) collective-permute-start(f32[336,128]{1,0:T(8,128)} %get-tuple-element.20), channel_id=1, source_target_pairs={{0,1},{1,0},{2,3},{3,2},{4,5},{5,4},{6,7},{7,6},{8,9},{9,8},{10,11... | collective-permute-start | bytes 516104 | tf_op jit(solution)/shard_map/ppermute | solution.py:530
  7.2 5.5 %collective-permute-start.1 = (f32[336,128]{1,0:T(8,128)}, f32[336,128]{1,0:T(8,128)S(1)}, u32[]{:S(2)}, u32[]{:S(2)}) collective-permute-start(f32[336,128]{1,0:T(8,128)} %get-tuple-element.21), channel_id=1, source_target_pairs={{1,2},{2,1},{3,4},{4,3},{5,6},{6,5},{9,10},{10,9},{11,12},{12,11},... | collective-permute-start | bytes 516104 | tf_op jit(solution)/shard_map/ppermute | solution.py:530
  9.3 1.0 %copy-start.1 = (f32[32,16,128]{2,1,0:T(8,128)S(1)}, f32[32,16,128]{2,1,0:T(8,128)}, u32[]{:S(2)}) copy-start(f32[32,16,128]{2,1,0:T(8,128)} %get-tuple-element.28.b0) | copy-start | bytes 786436
  10.5 2.4 %collective-permute-start.4 = (f32[200,128]{1,0:T(8,128)S(1)}, f32[200,128]{1,0:T(8,128)S(1)}, u32[]{:S(2)}, u32[]{:S(2)}) collective-permute-start(f32[200,128]{1,0:T(8,128)S(1)} %get-tuple-element.29), channel_id=1, source_target_pairs={{0,1},{1,0},{2,3},{3,2},{4,5},{5,4},{6,7},{7,6},{8,9},{9,8},{10,11... | collective-permute-start | bytes 307208 | tf_op jit(solution)/shard_map/ppermute | solution.py:530
  12.0 1.0 %collective-permute-start.5 = (f32[200,128]{1,0:T(8,128)S(1)}, f32[200,128]{1,0:T(8,128)S(1)}, u32[]{:S(2)}, u32[]{:S(2)}) collective-permute-start(f32[200,128]{1,0:T(8,128)S(1)} %get-tuple-element.30), channel_id=1, source_target_pairs={{1,2},{2,1},{3,4},{4,3},{5,6},{6,5},{9,10},{10,9},{11,12},{12,11},... | collective-permute-start | bytes 307208 | tf_op jit(solution)/shard_map/ppermute | solution.py:530

commit v5 on v4

--- a/solution.py
+++ b/solution.py
@@ -17,8 +17,8 @@
 HALF_WIDTH = 9.8
 RIDGE = 0.05
 PANEL = 16
-VMEM_BYTES = 48 * 1024 * 1024
-BEGIN_BYTES = 55000 * 1024
+VMEM_BYTES = 24 * 1024 * 1024
+BEGIN_BYTES = 54300 * 1024
 
 
 def lanes_of(shape):
@@ -77,22 +77,22 @@
 
 
 def begin_kernel(px, py, *refs):
-    far, refs = refs[:4], refs[4:]
-    (root_o, abs_o, b0_o, edge_o, face_o, send_a, send_b, side_a, side_b), refs = refs[:9], refs[9:]
-    guess, source, leaf, absorb, root, absb, sems = refs
+    far, refs = refs[:3], refs[3:]
+    (root_o, abs_o, b0_o, rim_o, edge_o, face_o), refs = refs[:6], refs[6:]
+    (send_a, send_b, side_a, side_b), refs = refs[:4], refs[4:]
+    guess, source, pair_in, root, absb, sems = refs
     copies = [
         pltpu.make_async_copy(there, here, sems.at[i])
-        for i, (there, here) in enumerate(zip(far, (guess, source, leaf, absorb)))
+        for i, (there, here) in enumerate(zip(far, (guess, source, pair_in)))
     ]
-    for i in (2, 3, 0, 1):
+    for i in (2, 0, 1):
         copies[i].start()
     nx, ny, _ = guess.shape
-    depth = leaf.shape[1]
+    depth = pair_in.shape[2]
     copies[2].wait()
-    copies[3].wait()
-    turned = jnp.transpose(leaf[...].reshape(ny * depth, nx))
+    turned = jnp.transpose(pair_in[0].reshape(ny * depth, nx))
     root_o[...] = jnp.sqrt(PEAK_COND / (1.0 + turned))
-    abs_o[...] = jnp.transpose(absorb[...].reshape(ny * depth, nx))
+    abs_o[...] = jnp.transpose(pair_in[1].reshape(ny * depth, nx))
     for part, wide in ((root_o, root), (abs_o, absb)):
         for y in range(0, ny, NRHS):
             wide[:, y : y + NRHS, :] = spread(part[:, y * depth : (y + NRHS) * depth])
@@ -119,6 +119,9 @@
         moving, still = moving[1:], still[1:]
         v = guess[x]
         b0_o[x] = source[x] - absb[x] * v + root[x] * (wu - v * wr)
+
+    rim_o[0] = b0_o[0]
+    rim_o[1] = b0_o[nx - 1]
 
     def write(out, x0, face, beyond):
         n = DEEP * ny
@@ -169,21 +172,18 @@
 
 
 def widen_kernel(
-    px, py, recv_a, recv_b, edge_own, face_own, root, absb, b0,
-    rootx, absx, b0x, edge, send_a, send_b, face
+    px, py, recv_a, recv_b, edge_own, face_own, root, absb, rim,
+    root_h, abs_h, band, edge, send_a, send_b, face
 ):
-    nx, ny, _ = b0.shape
+    nx, ny = edge_own.shape[1], face_own.shape[1]
     wide = nx + 2 * DEEP
-    rootx[DEEP : DEEP + nx] = root[...]
-    absx[DEEP : DEEP + nx] = absb[...]
-    b0x[DEEP : DEEP + nx] = b0[...]
     for at in (0, 1):
         edge[at, DEEP : DEEP + nx] = edge_own[at]
         edge[at, wide : wide + 8] = jnp.zeros((8, LANES), jnp.float32)
 
     def read(msg, x0, side):
         n = DEEP * ny
-        b0x[x0 : x0 + DEEP] = msg[0:n].reshape(DEEP, ny, LANES)
+        band[side, side : side + DEEP] = msg[0:n].reshape(DEEP, ny, LANES)
         face[side] = msg[n : n + ny]
         n += ny
         for at in (0, 1):
@@ -193,9 +193,9 @@
             edge[at, wide + side : wide + side + 1] = msg[n + at : n + at + 1]
             edge[at, wide + 2 + side : wide + 3 + side] = msg[n + 2 + at : n + 3 + at]
         n += 8
-        for out in (rootx, absx):
-            for first in range(0, out.shape[1], LANES):
-                out[x0 : x0 + DEEP, first : first + LANES] = msg[n : n + DEEP]
+        for out in (root_h, abs_h):
+            for first in range(0, out.shape[2], LANES):
+                out[side, :, first : first + LANES] = msg[n : n + DEEP]
                 n += DEEP
 
     @pl.when(px[0] == 0)
@@ -208,33 +208,33 @@
         read(recv_a, 0, 0)
         read(recv_b, DEEP + nx, 1)
 
-    def root_line(x):
-        parts = [
-            spread(rootx[x : x + 1, first : first + LANES])
-            for first in range(0, rootx.shape[1], LANES)
-        ]
+    def line(rows):
+        parts = [spread(rows[:, at : at + LANES]) for at in range(0, rows.shape[1], LANES)]
         return jnp.concatenate(parts, axis=1)[0]
 
-    for side, out_x, in_x in ((0, DEEP - 1, DEEP), (1, DEEP + nx, DEEP + nx - 1)):
-        va, ra = face[side], root_line(out_x)
-        vb, rb = face_own[side], root_line(in_x)
+    for side, out_x, in_x, far_x, near_x in (
+        (0, DEEP - 1, DEEP, DEEP - 1, 0),
+        (1, 1, 0, 0, nx - 1),
+    ):
+        va, ra = face[side], line(root_h[side, far_x : far_x + 1])
+        vb, rb = face_own[side], line(root[near_x : near_x + 1])
         fix_a = ra * (cross_sum(rb * vb, row_sum_zero) - va * cross_sum(rb, row_sum_zero))
         fix_b = rb * (cross_sum(ra * va, row_sum_zero) - vb * cross_sum(ra, row_sum_zero))
-        b0x[out_x] = b0x[out_x] + fix_a
-        b0x[in_x] = b0x[in_x] + fix_b
+        band[side, out_x] = band[side, out_x] + fix_a
+        band[side, in_x] = rim[side] + fix_b
 
     def write(out, y0, at):
         n = 0
-        for x0 in (0, DEEP + nx - 1):
+        for side in (0, 1):
             m = (DEEP + 1) * DEEP
-            out[n : n + m] = b0x[x0 : x0 + DEEP + 1, y0 : y0 + DEEP, :].reshape(m, LANES)
+            out[n : n + m] = band[side, :, y0 : y0 + DEEP, :].reshape(m, LANES)
             n += m
         first = y0 * (LANES // NRHS)
-        for x0 in (0, DEEP + nx):
+        for side, x0 in ((0, 0), (1, DEEP + nx)):
             out[n : n + DEEP] = edge[at, x0 : x0 + DEEP]
             n += DEEP
-            for part in (rootx, absx):
-                out[n : n + DEEP] = part[x0 : x0 + DEEP, first : first + LANES]
+            for part in (root_h, abs_h):
+                out[n : n + DEEP] = part[side, :, first : first + LANES]
                 n += DEEP
         out[n : n + 8] = edge[at, wide : wide + 8]
 
@@ -254,52 +254,123 @@
     return high, (a - high.astype(jnp.float32)).astype(jnp.bfloat16)
 
 
-def basis_kernel(
-    py, side_a, side_b, recv_a, recv_b, rootx, absx, b0x, edge,
-    rough, fine, moments, root, diag, far, f0, f1, f2
-):
-    wide, ny, _ = b0x.shape
-    nx = wide - 2 * DEEP
-    tall = ny + 2 * DEEP
-    depth = LANES // NRHS
-    for part, out in ((rootx, root), (absx, diag)):
+def sweep(root, field, lo, hi, put):
+    def pair(x):
+        u = root(x) if field is None else root(x) * field(x)
+        return (u, z_sum(u))
+
+    first, second = pair(lo - 1), pair(lo)
+    for x in range(lo, hi):
+        third = pair(x + 1)
+        put(x, slab_sum(first, second, third, row_sum))
+        first, second = second, third
+
+
+def final_diag(raw, root, total):
+    return (raw + root * total - CENTRE) * (2.0 / HALF_WIDTH)
+
+
+def next_basis(j, diag, root, here, total, before):
+    new = diag * here - (2.0 / HALF_WIDTH) * root * total
+    return 0.5 * new if j == 1 else new - before
+
+
+def inner_kernel(py, side_a, side_b, root_own, abs_own, b0, edge, root, diag, frames, far):
+    nx, ny, _ = b0.shape
+    for part, out in ((root_own, root), (abs_own, diag)):
         for y in range(0, ny, DEEP):
-            first = y * depth
+            first = y * (LANES // NRHS)
             out[:, DEEP + y : 2 * DEEP + y, :] = spread(part[:, first : first + LANES])
-    f0[:, DEEP : DEEP + ny, :] = b0x[...]
-
-    def read(inner, outer, y0, side):
+    inner = slice(1, nx - 1)
+    frames[0, inner, DEEP : DEEP + ny, :] = b0[inner]
+
+    def read(msg, y0, side):
         n = (nx - 2) * DEEP
-        f0[DEEP + 1 : DEEP + nx - 1, y0 : y0 + DEEP, :] = inner[0:n].reshape(nx - 2, DEEP, LANES)
-        far[side, DEEP : DEEP + nx] = inner[n : n + nx]
+        frames[0, inner, y0 : y0 + DEEP, :] = msg[0:n].reshape(nx - 2, DEEP, LANES)
+        far[side] = msg[n : n + nx]
         n += nx
         for out in (root, diag):
-            out[DEEP : DEEP + nx, y0 : y0 + DEEP, :] = spread(inner[n : n + nx])
+            out[:, y0 : y0 + DEEP, :] = spread(msg[n : n + nx])
             n += nx
+
+    @pl.when(py[0] == 0)
+    def _():
+        read(side_b, 0, 0)
+        read(side_a, DEEP + ny, 1)
+
+    @pl.when(py[0] == 1)
+    def _():
+        read(side_a, 0, 0)
+        read(side_b, DEEP + ny, 1)
+
+    def column(v, y):
+        r = root[:, y, :]
+        return v, r, cross_sum(r * v, row_sum), cross_sum(r, row_sum)
+
+    for side, out_y, in_y in ((0, DEEP - 1, DEEP), (1, DEEP + ny, DEEP + ny - 1)):
+        va, ra, ua, wa = column(far[side], out_y)
+        vb, rb, ub, wb = column(edge[side], in_y)
+        for y, fix in ((out_y, ra * (ub - va * wb)), (in_y, rb * (ua - vb * wa))):
+            frames[0, inner, y, :] = frames[0, inner, y, :] + fix[inner]
+
+    def put_diag(x, total):
+        diag[x] = final_diag(diag[x], root[x], total)
+
+    sweep(lambda x: root[x], None, 1, nx - 1, put_diag)
+    for j in range(1, S + 1):
+
+        def put(x, total):
+            before = frames[j - 2, x] if j > 1 else None
+            frames[j, x] = next_basis(j, diag[x], root[x], frames[j - 1, x], total, before)
+
+        sweep(lambda x: root[x], lambda x: frames[j - 1, x], 1 + j, nx - 1 - j, put)
+
+
+def basis_kernel(
+    py, recv_a, recv_b, root_h, abs_h, band, edge, root_i, diag_i, frames, far_own,
+    rough, fine, moments, root_o, diag_o, far, f0, f1, f2
+):
+    _, nx, tall, _ = frames.shape
+    ny = tall - 2 * DEEP
+    wide = nx + 2 * DEEP
+    low, high_x = DEEP + 1, DEEP + nx - 1
+    for side in (0, 1):
+        rows = slice(side * DEEP, (side + 1) * DEEP)
+        for y in range(0, ny, DEEP):
+            first = y * (LANES // NRHS)
+            for part, out in ((root_h, root_o), (abs_h, diag_o)):
+                out[rows, DEEP + y : 2 * DEEP + y, :] = spread(
+                    part[side, :, first : first + LANES]
+                )
+        far[side, DEEP : DEEP + nx] = far_own[side]
+    f0[0:low, DEEP : DEEP + ny, :] = band[0]
+    f0[high_x:wide, DEEP : DEEP + ny, :] = band[1]
+
+    def read(msg, y0, side):
         n = 0
-        for x0 in (0, DEEP + nx - 1):
+        for x0 in (0, high_x):
             m = (DEEP + 1) * DEEP
-            f0[x0 : x0 + DEEP + 1, y0 : y0 + DEEP, :] = outer[n : n + m].reshape(
+            f0[x0 : x0 + DEEP + 1, y0 : y0 + DEEP, :] = msg[n : n + m].reshape(
                 DEEP + 1, DEEP, LANES
             )
             n += m
-        for x0 in (0, DEEP + nx):
-            far[side, x0 : x0 + DEEP] = outer[n : n + DEEP]
+        for at, x0 in ((0, 0), (DEEP, DEEP + nx)):
+            far[side, x0 : x0 + DEEP] = msg[n : n + DEEP]
             n += DEEP
-            for out in (root, diag):
-                out[x0 : x0 + DEEP, y0 : y0 + DEEP, :] = spread(outer[n : n + DEEP])
+            for out in (root_o, diag_o):
+                out[at : at + DEEP, y0 : y0 + DEEP, :] = spread(msg[n : n + DEEP])
                 n += DEEP
-        far[side, wide : wide + 8] = outer[n : n + 8]
+        far[side, wide : wide + 8] = msg[n : n + 8]
 
     @pl.when(py[0] == 0)
     def _():
-        read(side_b, recv_b, 0, 0)
-        read(side_a, recv_a, DEEP + ny, 1)
+        read(recv_b, 0, 0)
+        read(recv_a, DEEP + ny, 1)
 
     @pl.when(py[0] == 1)
     def _():
-        read(side_a, recv_a, 0, 0)
-        read(side_b, recv_b, DEEP + ny, 1)
+        read(recv_a, 0, 0)
+        read(recv_b, DEEP + ny, 1)
 
     row = lax.broadcasted_iota(jnp.int32, (wide, LANES), 0)
 
@@ -315,31 +386,51 @@
     def column(ref, at, y):
         v = ref[at, 0:wide]
         ends = ref[at, wide : wide + 8]
-        r = root[:, y, :]
+        r = jnp.concatenate([root_o[0:DEEP, y, :], root_i[:, y, :], root_o[DEEP:, y, :]], axis=0)
         r0, r1 = ends[2:3], ends[3:4]
         return v, r, across(r * v, r0 * ends[0:1], r1 * ends[1:2]), across(r, r0, r1)
 
     for side, out_y, in_y in ((0, DEEP - 1, DEEP), (1, DEEP + ny, DEEP + ny - 1)):
         va, ra, ua, wa = column(far, side, out_y)
         vb, rb, ub, wb = column(edge, side, in_y)
-        f0[:, out_y, :] = f0[:, out_y, :] + ra * (ub - va * wb)
-        f0[:, in_y, :] = f0[:, in_y, :] + rb * (ua - vb * wa)
-
-    def pair(src, x):
-        u = root[x] if src is None else root[x] * src[x]
-        return (u, z_sum(u))
-
-    def sweep(src, lo, hi, put):
-        first, second = pair(src, lo - 1), pair(src, lo)
-        for x in range(lo, hi):
-            third = pair(src, x + 1)
-            put(x, slab_sum(first, second, third, row_sum))
-            first, second = second, third
+        for y, fix in ((out_y, ra * (ub - va * wb)), (in_y, rb * (ua - vb * wa))):
+            f0[0:low, y, :] = f0[0:low, y, :] + fix[0:low]
+            f0[high_x:wide, y, :] = f0[high_x:wide, y, :] + fix[high_x:wide]
+
+    outer = [f0, f1, f2]
+
+    def root(x):
+        if DEEP <= x < DEEP + nx:
+            return root_i[x - DEEP]
+        return root_o[x if x < DEEP else x - nx]
+
+    def field(j):
+        def at(x):
+            if low + j <= x < high_x - j:
+                return frames[j, x - DEEP]
+            return outer[j % 3][x]
+
+        return at
+
+    edges = {}
+
+    def diag(x):
+        if low <= x < high_x:
+            return diag_i[x - DEEP]
+        if x in (DEEP, DEEP + nx - 1):
+            return diag_e[0 if x == DEEP else 1]
+        return diag_o[x if x < DEEP else x - nx]
 
     def put_diag(x, total):
-        diag[x] = (diag[x] + root[x] * total - CENTRE) * (2.0 / HALF_WIDTH)
-
-    sweep(None, 1, wide - 1, put_diag)
+        if DEEP <= x < DEEP + nx:
+            edges[x] = final_diag(diag_i[x - DEEP], root(x), total)
+        else:
+            at = x if x < DEEP else x - nx
+            diag_o[at] = final_diag(diag_o[at], root(x), total)
+
+    for lo, hi in ((1, low), (high_x, wide - 1)):
+        sweep(root, None, lo, hi, put_diag)
+    diag_e = (edges[DEEP], edges[DEEP + nx - 1])
 
     level = lanes_of((NRHS, LANES)) // NRHS
     depth = LANES // NRHS
@@ -353,31 +444,39 @@
             f = jnp.where(level == z, block[z * NRHS : (z + 1) * NRHS], f)
         folded[n] = f
 
-    frames = [f0, f1, f2]
     old = None
     for j in range(S + 1):
-        now = frames[j % 3]
+        now = outer[j % 3]
         if j > 0:
-            src, prev = frames[(j - 1) % 3], frames[(j - 2) % 3]
+            here, before = field(j - 1), field(j - 2)
 
             def put(x, total):
-                new = diag[x] * src[x] - (2.0 / HALF_WIDTH) * root[x] * total
-                now[x] = 0.5 * new if j == 1 else new - prev[x]
-
-            sweep(src, j, wide - j, put)
-        own = now[DEEP : DEEP + nx, DEEP : DEEP + ny, :]
-        high, low = halves(own.reshape(nx * ny, LANES))
+                past = before(x) if j > 1 else None
+                now[x] = next_basis(j, diag(x), root(x), here(x), total, past)
+
+            for lo, hi in ((j, low + j), (high_x - j, wide - j)):
+                sweep(root, here, lo, hi, put)
+        columns = slice(DEEP, DEEP + ny)
+        own = jnp.concatenate(
+            [
+                now[DEEP : low + j, columns, :],
+                frames[j, 1 + j : nx - 1 - j, columns, :],
+                now[high_x - j : DEEP + nx, columns, :],
+            ],
+            axis=0,
+        )
+        high, rest = halves(own.reshape(nx * ny, LANES))
         rough[:, j * LANES : (j + 1) * LANES] = high
-        fine[:, j * LANES : (j + 1) * LANES] = low
+        fine[:, j * LANES : (j + 1) * LANES] = rest
         turned = high.T
-        both = jnp.concatenate([high, low], axis=1)
+        both = jnp.concatenate([high, rest], axis=1)
         left = turned if j == 0 else jnp.concatenate([turned, old[0]], axis=0)
         got = jnp.dot(left, both, preferred_element_type=jnp.float32)
         note(2 * j, got[:LANES, :LANES] + 2.0 * got[:LANES, LANES:])
         if j > 0:
-            rest = jnp.dot(turned, old[1], preferred_element_type=jnp.float32)
-            note(2 * j - 1, got[LANES:, :LANES] + got[LANES:, LANES:] + rest)
-        old = (turned, low)
+            more = jnp.dot(turned, old[1], preferred_element_type=jnp.float32)
+            note(2 * j - 1, got[LANES:, :LANES] + got[LANES:, LANES:] + more)
+        old = (turned, rest)
     every = jnp.concatenate(folded, axis=0)
     shift = LANES // 2
     while shift >= NRHS:
@@ -551,9 +650,8 @@
 
 def body(initial_guess, source, leaf_density, absorption):
     nx, ny, lanes = initial_guess.shape
-    leaf = jnp.transpose(leaf_density, (1, 2, 0))
-    absorb = jnp.transpose(absorption, (1, 2, 0))
-    depth = leaf.shape[1]
+    cells = jnp.transpose(jnp.stack([leaf_density, absorption]), (0, 2, 3, 1))
+    depth = cells.shape[2]
     px = lax.rem(lax.axis_index("gx"), 2).astype(jnp.int32).reshape(1)
     py = lax.rem(lax.axis_index("gy"), 2).astype(jnp.int32).reshape(1)
     wide = nx + 2 * DEEP
@@ -564,20 +662,19 @@
     side_rows = (nx - 2) * DEEP + 3 * nx
     y_rows = 2 * (DEEP + 1) * DEEP + 6 * DEEP + 8
     sides = ((2, nx, lanes), (2, ny, lanes))
-    root, absb, b0, edge, face, xa, xb, sa, sb = call(
+    root, absb, b0, rim, edge, face, xa, xb, sa, sb = call(
         begin_kernel,
-        (px, py, initial_guess, source, leaf, absorb),
-        ((nx, across), (nx, across), block, *sides)
+        (px, py, initial_guess, source, cells),
+        ((nx, across), (nx, across), block, sides[1], *sides)
         + ((x_rows, lanes),) * 2
         + ((side_rows, lanes),) * 2,
         scratch=[
             pltpu.VMEM(block, jnp.float32),
             pltpu.VMEM(block, jnp.float32),
-            pltpu.VMEM(leaf.shape, jnp.float32),
-            pltpu.VMEM(leaf.shape, jnp.float32),
+            pltpu.VMEM(cells.shape, jnp.float32),
             pltpu.VMEM(block, jnp.float32),
             pltpu.VMEM(block, jnp.float32),
-            pltpu.SemaphoreType.DMA((4,)),
+            pltpu.SemaphoreType.DMA((3,)),
         ],
         scalars=2,
         space=pltpu.HBM,
@@ -585,24 +682,33 @@
     )
     xa, xb = exchange(xa, xb, "gx")
     sa, sb = exchange(sa, sb, "gy")
-    broad = (wide, ny, lanes)
-    rootx, absx, b0x, edge, ya, yb = call(
+    root_h, abs_h, band, edges, ya, yb = call(
         widen_kernel,
-        (px, py, xa, xb, edge, face, root, absb, b0),
-        ((wide, across), (wide, across), broad, (2, wide + 8, lanes), (y_rows, lanes), (y_rows, lanes)),
+        (px, py, xa, xb, edge, face, root, absb, rim),
+        ((2, DEEP, across),) * 2
+        + ((2, DEEP + 1, ny, lanes), (2, wide + 8, lanes))
+        + ((y_rows, lanes),) * 2,
         scratch=[pltpu.VMEM((2, ny, lanes), jnp.float32)],
         scalars=2,
     )
     ya, yb = exchange(ya, yb, "gy")
+    inner = (nx, tall, lanes)
+    root_i, diag_i, frames, far = call(
+        inner_kernel,
+        (py, sa, sb, root, absb, b0, edge),
+        (inner, inner, (S + 1, *inner), sides[0]),
+        scalars=1,
+    )
     frame = pltpu.VMEM((wide, tall, lanes), jnp.float32)
+    halo = pltpu.VMEM((2 * DEEP, tall, lanes), jnp.float32)
     count = lax.axis_size("gx") * lax.axis_size("gy")
     count = count if count <= 64 else 1
     cells = nx * ny
     rough, fine, moments = call(
         basis_kernel,
-        (py, sa, sb, ya, yb, rootx, absx, b0x, edge),
+        (py, ya, yb, root_h, abs_h, band, edges, root_i, diag_i, frames, far),
         ((cells, (S + 1) * lanes), (cells, (S + 1) * lanes), (count, NRHS, lanes)),
-        scratch=[frame, frame, pltpu.VMEM((2, wide + 8, lanes), jnp.float32), frame, frame, frame],
+        scratch=[halo, halo, pltpu.VMEM((2, wide + 8, lanes), jnp.float32), frame, frame, frame],
         scalars=1,
         kinds=(jnp.bfloat16, jnp.bfloat16, jnp.float32),
     )

time: 46.1 us -> 44.3 us (0.961)
  blocking collectives: 21.2 us -> 18.8 us
  other arithmetic: 0 us -> 1.69 us
  local copies, waits for them, and re-layouts: 0.96 us -> 0.01 us
    all_to_all x1, blocking collectives: 21.2 us -> 18.8 us  [totals(): return lax.all_to_all(parts, ('gx', 'gy'), 0, 0)]
    transpose x0 -> x1, other arithmetic: none -> 1.69 us  [body(): cells = jnp.transpose(jnp.stack([leaf_density, absorption]), (0, 2, 3, 1))]
    unnamed x4 -> x2, local copies, waits for them, and re-layouts: 0.96 us -> 0.01 us
    pallas_call x4 -> x5, Pallas kernels: 14.6 us -> 14.8 us  [call(): pl.pallas_call(kernel, out_shape=[jax.ShapeDtypeStruct(s, k) for s, k in...]
  transfers between devices with their start and end apart: 6 -> 6, of which waited for: 2 -> 1; matrix products, arithmetic and copies ran while one was open for 0% -> 0% of each run, Pallas kernels for 1% -> 8%
where the time goes in v5:
time: 44.3 us; the launch traced here: 44.1 us
  blocking collectives  18.8 us (42%)
  Pallas kernels  14.8 us (33%)
  starting transfers between devices  6.62 us (15%)
  other arithmetic  1.69 us (4%)
  waiting for transfers between devices  1.47 us (3%)
  between operations  0.74 us (2%)
    all_to_all x1, blocking collectives, totals(): return lax.all_to_all(parts, ('gx', 'gy'), 0, 0)  18.8 us
    pallas_call x5, Pallas kernels, call(): pl.pallas_call(kernel, out_shape=[jax.ShapeDtypeStruct(s, k) for s, k in...  14.8 us
    ppermute x6, starting transfers between devices, exchange(): got.append(lax.ppermute(cells, axis, links))  6.62 us
    transpose x1, other arithmetic, body(): cells = jnp.transpose(jnp.stack([leaf_density, absorption]), (0, 2, 3, 1))  1.69 us
    ppermute x6, waiting for transfers between devices, exchange(): got.append(lax.ppermute(cells, axis, links))  1.47 us
  transfers between devices with their start and end apart: 6, of which 1 were waited for; matrix products, arithmetic and copies ran while one was open for 0% of the time, Pallas kernels for 8%

profile of v5, /device:TPU:0, one launch (start us, length us, event | category | flops | bytes accessed | tf_op | source)
XLA Modules:
  0.0 44.1 jit_solution(17098336266442330490)
XLA Ops:
  0.6 1.7 %maximum_bitcast_fusion.refs_2_ = f32[2,16,16,32]{3,2,1,0:T(8,128)} fusion(f32[1,32,16,16]{1,3,2,0:T(8,128)} %bitcast.6, f32[1,32,16,16]{1,3,2,0:T(8,128)} %bitcast.7), kind=kLoop, calls=%fused_computation | loop fusion | flops 16384 | bytes 131072 | tf_op jit(solution)/shard_map/transpose | solution.py:653
  2.3 1.8 %shard_map.59 = (f32[32,256]{1,0:T(8,128)S(1)}, f32[32,256]{1,0:T(8,128)S(1)}, f32[32,16,128]{2,1,0:T(8,128)S(1)}, f32[2,16,128]{2,1,0:T(8,128)S(1)}, f32[2,32,1...) custom-call(s32[1]{0:T(128)} %bitcast.1.px, ...), custom_call_target="tpu_custom_call" | custom-call | tf_op jit(solution)/shard_map/pallas_call | solution.py:609
  4.1 3.1 %collective-permute-start = (f32[200,128]{1,0:T(8,128)S(1)}, f32[200,128]{1,0:T(8,128)S(1)}, u32[]{:S(2)}, u32[]{:S(2)}) collective-permute-start(f32[200,128]{1,0:T(8,128)S(1)} %get-tuple-element.25), channel_id=1, source_target_pairs={{0,8},{8,0},{16,24},{24,16},{1,9},{9,1},{17,25},{25,17},{2,10},{10... | collective-permute-start | bytes 307208 | tf_op jit(solution)/shard_map/ppermute | solution.py:629
  7.2 0.7 %collective-permute-start.1 = (f32[200,128]{1,0:T(8,128)S(1)}, f32[200,128]{1,0:T(8,128)S(1)}, u32[]{:S(2)}, u32[]{:S(2)}) collective-permute-start(f32[200,128]{1,0:T(8,128)S(1)} %get-tuple-element.26), channel_id=1, source_target_pairs={{8,16},{16,8},{9,17},{17,9},{10,18},{18,10},{11,19},{19,11},{12,20... | collective-permute-start | bytes 307208 | tf_op jit(solution)/shard_map/ppermute | solution.py:629
  7.9 0.1 collective-permute-start.4
  8.0 0.7 %collective-permute-start.5 = (f32[336,128]{1,0:T(8,128)S(1)}, f32[336,128]{1,0:T(8,128)S(1)}, u32[]{:S(2)}, u32[]{:S(2)}) collective-permute-start(f32[336,128]{1,0:T(8,128)S(1)} %get-tuple-element.39), channel_id=1, source_target_pairs={{1,2},{2,1},{3,4},{4,3},{5,6},{6,5},{9,10},{10,9},{11,12},{12,11},... | collective-permute-start | bytes 516104 | tf_op jit(solution)/shard_map/ppermute | solution.py:629
  8.6 1.5 %collective-permute-done.recv_a = f32[200,128]{1,0:T(8,128)S(1)} collective-permute-done((f32[200,128]{1,0:T(8,128)S(1)}, f32[200,128]{1,0:T(8,128)S(1)}, u32[]{:S(2)}, u32[]{:S(2)}) %collective-permute-start) | collective-permute-done | bytes 102432 | tf_op jit(solution)/shard_map/ppermute | solution.py:629
  10.1 0.0 collective-permute-done.1.recv_b
  10.1 0.2 shard_map.60
  10.3 1.5 %collective-permute-start.2 = (f32[200,128]{1,0:T(8,128)S(1)}, f32[200,128]{1,0:T(8,128)S(1)}, u32[]{:S(2)}, u32[]{:S(2)}) collective-permute-start(f32[200,128]{1,0:T(8,128)S(1)} %get-tuple-element.32), channel_id=1, source_target_pairs={{0,1},{1,0},{2,3},{3,2},{4,5},{5,4},{6,7},{7,6},{8,9},{9,8},{10,11... | collective-permute-start | bytes 307208 | tf_op jit(solution)/shard_map/ppermute | solution.py:629
  11.8 0.7 %collective-permute-start.3 = (f32[200,128]{1,0:T(8,128)S(1)}, f32[200,128]{1,0:T(8,128)S(1)}, u32[]{:S(2)}, u32[]{:S(2)}) collective-permute-start(f32[200,128]{1,0:T(8,128)S(1)} %get-tuple-element.33), channel_id=1, source_target_pairs={{1,2},{2,1},{3,4},{4,3},{5,6},{6,5},{9,10},{10,9},{11,12},{12,11},... | collective-permute-start | bytes 307208 | tf_op jit(solution)/shard_map/ppermute | solution.py:629
  12.5 0.0 collective-permute-done.4.side_a
  12.5 0.0 collective-permute-done.5.side_b
  12.5 3.5 %shard_map.61 = (f32[32,32,128]{2,1,0:T(8,128)S(1)}, f32[32,32,128]{2,1,0:T(8,128)S(1)}, f32[9,32,32,128]{3,2,1,0:T(8,128)S(1)}, f32[2,32,128]{2,1,0:T(8,128)S(1)}) custom-call(s32[1]{0:T(128)} %bitcast.py, f32[336,128]{1,0:T(8,128)S(1)} %collective-permute-done.4.side_a, f32[336,128]{1,0:T(8,128)S(1)} %collective-permute-done.5.side_b, ...), custom_call_target="tpu_custom_call" | custom-call | tf_op jit(solution)/shard_map/pallas_call | solution.py:609
  16.0 0.0 collective-permute-done.2.recv_a
  16.0 0.0 collective-permute-done.3.recv_b
  16.0 0.0 copy-start
  16.0 5.0 %shard_map.62 = (bf16[512,1152]{1,0:T(8,128)(2,1)S(1)}, bf16[512,1152]{1,0:T(8,128)(2,1)S(1)}, f32[32,8,128]{2,1,0:T(8,128)S(1)}) custom-call(s32[1]{0:T(128)} %bitcast.py, f32[200,128]{1,0:T(8,128)S(1)} %collective-permute-done.2.recv_a, f32[200,128]{1,0:T(8,128)S(1)} %collective-permute-done.3.recv_b, f32[2,8,256]{2,1,0:T(8,128)S(1)} %get-tuple-element.34.root_h, ...), custom_call_target="tpu_custom_call" | custom-call | tf_op jit(solution)/shard_map/pallas_call | solution.py:609
  21.0 18.8 %all_to_all.5.parts = f32[32,8,128]{2,1,0:T(8,128)S(1)} all-to-all(f32[32,8,128]{2,1,0:T(8,128)S(1)} %get-tuple-element.47), channel_id=1, replica_groups=mesh['gx'=4,'gy'=8] {'gx','gy'}, dimensions={0} | all-to-all | bytes 262144 | tf_op jit(solution)/shard_map/all_to_all | solution.py:647
  39.8 0.0 copy-done
  39.8 4.3 %shard_map.63 = (f32[32,16,128]{2,1,0:T(8,128)}, f32[32,16,128]{2,1,0:T(8,128)}) custom-call(f32[32,16,128]{2,1,0:T(8,128)S(1)} %copy-done, bf16[512,1152]{1,0:T(8,128)(2,1)S(1)} %get-tuple-element.45.rough, bf16[512,1152]{1,0:T(8,128)(2,1)S(1)} %get-tuple-element.46.fine, f32[32,8,128]{2,1,0:T(8,128)S(1)} %all_to_all.5.parts), custom_call_target="tpu_custom_call" | custom-call | tf_op jit(solution)/shard_map/pallas_call | solution.py:609
Async XLA Ops:
  4.1 6.0 %collective-permute-start = (f32[200,128]{1,0:T(8,128)S(1)}, f32[200,128]{1,0:T(8,128)S(1)}, u32[]{:S(2)}, u32[]{:S(2)}) collective-permute-start(f32[200,128]{1,0:T(8,128)S(1)} %get-tuple-element.25), channel_id=1, source_target_pairs={{0,8},{8,0},{16,24},{24,16},{1,9},{9,1},{17,25},{25,17},{2,10},{10... | collective-permute-start | bytes 307208 | tf_op jit(solution)/shard_map/ppermute | solution.py:629
  7.2 2.9 %collective-permute-start.1 = (f32[200,128]{1,0:T(8,128)S(1)}, f32[200,128]{1,0:T(8,128)S(1)}, u32[]{:S(2)}, u32[]{:S(2)}) collective-permute-start(f32[200,128]{1,0:T(8,128)S(1)} %get-tuple-element.26), channel_id=1, source_target_pairs={{8,16},{16,8},{9,17},{17,9},{10,18},{18,10},{11,19},{19,11},{12,20... | collective-permute-start | bytes 307208 | tf_op jit(solution)/shard_map/ppermute | solution.py:629
  7.9 4.6 %collective-permute-start.4 = (f32[336,128]{1,0:T(8,128)S(1)}, f32[336,128]{1,0:T(8,128)S(1)}, u32[]{:S(2)}, u32[]{:S(2)}) collective-permute-start(f32[336,128]{1,0:T(8,128)S(1)} %get-tuple-element.38), channel_id=1, source_target_pairs={{0,1},{1,0},{2,3},{3,2},{4,5},{5,4},{6,7},{7,6},{8,9},{9,8},{10,11... | collective-permute-start | bytes 516104 | tf_op jit(solution)/shard_map/ppermute | solution.py:629
  8.0 4.5 %collective-permute-start.5 = (f32[336,128]{1,0:T(8,128)S(1)}, f32[336,128]{1,0:T(8,128)S(1)}, u32[]{:S(2)}, u32[]{:S(2)}) collective-permute-start(f32[336,128]{1,0:T(8,128)S(1)} %get-tuple-element.39), channel_id=1, source_target_pairs={{1,2},{2,1},{3,4},{4,3},{5,6},{6,5},{9,10},{10,9},{11,12},{12,11},... | collective-permute-start | bytes 516104 | tf_op jit(solution)/shard_map/ppermute | solution.py:629
  10.3 5.6 %collective-permute-start.2 = (f32[200,128]{1,0:T(8,128)S(1)}, f32[200,128]{1,0:T(8,128)S(1)}, u32[]{:S(2)}, u32[]{:S(2)}) collective-permute-start(f32[200,128]{1,0:T(8,128)S(1)} %get-tuple-element.32), channel_id=1, source_target_pairs={{0,1},{1,0},{2,3},{3,2},{4,5},{5,4},{6,7},{7,6},{8,9},{9,8},{10,11... | collective-permute-start | bytes 307208 | tf_op jit(solution)/shard_map/ppermute | solution.py:629
  11.8 4.2 %collective-permute-start.3 = (f32[200,128]{1,0:T(8,128)S(1)}, f32[200,128]{1,0:T(8,128)S(1)}, u32[]{:S(2)}, u32[]{:S(2)}) collective-permute-start(f32[200,128]{1,0:T(8,128)S(1)} %get-tuple-element.33), channel_id=1, source_target_pairs={{1,2},{2,1},{3,4},{4,3},{5,6},{6,5},{9,10},{10,9},{11,12},{12,11},... | collective-permute-start | bytes 307208 | tf_op jit(solution)/shard_map/ppermute | solution.py:629
  16.0 23.8 %copy-start = (f32[32,16,128]{2,1,0:T(8,128)S(1)}, f32[32,16,128]{2,1,0:T(8,128)}, u32[]{:S(2)}) copy-start(f32[32,16,128]{2,1,0:T(8,128)} %guess.1) | copy-start | bytes 786436

commit v6 on v5

--- a/solution.py
+++ b/solution.py
@@ -17,6 +17,7 @@
 HALF_WIDTH = 9.8
 RIDGE = 0.05
 PANEL = 16
+ROOT_SCALE = (2.0 / HALF_WIDTH) ** 0.5
 VMEM_BYTES = 24 * 1024 * 1024
 BEGIN_BYTES = 54300 * 1024
 
@@ -267,20 +268,21 @@
 
 
 def final_diag(raw, root, total):
-    return (raw + root * total - CENTRE) * (2.0 / HALF_WIDTH)
+    return (raw - CENTRE) * (2.0 / HALF_WIDTH) + root * total
 
 
 def next_basis(j, diag, root, here, total, before):
-    new = diag * here - (2.0 / HALF_WIDTH) * root * total
+    new = diag * here - root * total
     return 0.5 * new if j == 1 else new - before
 
 
 def inner_kernel(py, side_a, side_b, root_own, abs_own, b0, edge, root, diag, frames, far):
     nx, ny, _ = b0.shape
-    for part, out in ((root_own, root), (abs_own, diag)):
+    for part, out, factor in ((root_own, root, ROOT_SCALE), (abs_own, diag, 1.0)):
         for y in range(0, ny, DEEP):
             first = y * (LANES // NRHS)
-            out[:, DEEP + y : 2 * DEEP + y, :] = spread(part[:, first : first + LANES])
+            some = factor * part[:, first : first + LANES]
+            out[:, DEEP + y : 2 * DEEP + y, :] = spread(some)
     inner = slice(1, nx - 1)
     frames[0, inner, DEEP : DEEP + ny, :] = b0[inner]
 
@@ -289,8 +291,8 @@
         frames[0, inner, y0 : y0 + DEEP, :] = msg[0:n].reshape(nx - 2, DEEP, LANES)
         far[side] = msg[n : n + nx]
         n += nx
-        for out in (root, diag):
-            out[:, y0 : y0 + DEEP, :] = spread(msg[n : n + nx])
+        for out, factor in ((root, ROOT_SCALE), (diag, 1.0)):
+            out[:, y0 : y0 + DEEP, :] = spread(factor * msg[n : n + nx])
             n += nx
 
     @pl.when(py[0] == 0)
@@ -311,6 +313,7 @@
         va, ra, ua, wa = column(far[side], out_y)
         vb, rb, ub, wb = column(edge[side], in_y)
         for y, fix in ((out_y, ra * (ub - va * wb)), (in_y, rb * (ua - vb * wa))):
+            fix = fix * (HALF_WIDTH / 2)
             frames[0, inner, y, :] = frames[0, inner, y, :] + fix[inner]
 
     def put_diag(x, total):
@@ -321,7 +324,11 @@
 
         def put(x, total):
             before = frames[j - 2, x] if j > 1 else None
-            frames[j, x] = next_basis(j, diag[x], root[x], frames[j - 1, x], total, before)
+            new = next_basis(j, diag[x], root[x], frames[j - 1, x], total, before)
+            if j < S:
+                frames[j, x] = new
+            else:
+                frames[j, x, DEEP : DEEP + ny] = new[DEEP : DEEP + ny]
 
         sweep(lambda x: root[x], lambda x: frames[j - 1, x], 1 + j, nx - 1 - j, put)
 
@@ -338,10 +345,9 @@
         rows = slice(side * DEEP, (side + 1) * DEEP)
         for y in range(0, ny, DEEP):
             first = y * (LANES // NRHS)
-            for part, out in ((root_h, root_o), (abs_h, diag_o)):
-                out[rows, DEEP + y : 2 * DEEP + y, :] = spread(
-                    part[side, :, first : first + LANES]
-                )
+            for part, out, factor in ((root_h, root_o, ROOT_SCALE), (abs_h, diag_o, 1.0)):
+                some = factor * part[side, :, first : first + LANES]
+                out[rows, DEEP + y : 2 * DEEP + y, :] = spread(some)
         far[side, DEEP : DEEP + nx] = far_own[side]
     f0[0:low, DEEP : DEEP + ny, :] = band[0]
     f0[high_x:wide, DEEP : DEEP + ny, :] = band[1]
@@ -357,8 +363,8 @@
         for at, x0 in ((0, 0), (DEEP, DEEP + nx)):
             far[side, x0 : x0 + DEEP] = msg[n : n + DEEP]
             n += DEEP
-            for out in (root_o, diag_o):
-                out[at : at + DEEP, y0 : y0 + DEEP, :] = spread(msg[n : n + DEEP])
+            for out, factor in ((root_o, ROOT_SCALE), (diag_o, 1.0)):
+                out[at : at + DEEP, y0 : y0 + DEEP, :] = spread(factor * msg[n : n + DEEP])
                 n += DEEP
         far[side, wide : wide + 8] = msg[n : n + 8]
 
@@ -387,13 +393,14 @@
         v = ref[at, 0:wide]
         ends = ref[at, wide : wide + 8]
         r = jnp.concatenate([root_o[0:DEEP, y, :], root_i[:, y, :], root_o[DEEP:, y, :]], axis=0)
-        r0, r1 = ends[2:3], ends[3:4]
+        r0, r1 = ROOT_SCALE * ends[2:3], ROOT_SCALE * ends[3:4]
         return v, r, across(r * v, r0 * ends[0:1], r1 * ends[1:2]), across(r, r0, r1)
 
     for side, out_y, in_y in ((0, DEEP - 1, DEEP), (1, DEEP + ny, DEEP + ny - 1)):
         va, ra, ua, wa = column(far, side, out_y)
         vb, rb, ub, wb = column(edge, side, in_y)
         for y, fix in ((out_y, ra * (ub - va * wb)), (in_y, rb * (ua - vb * wa))):
+            fix = fix * (HALF_WIDTH / 2)
             f0[0:low, y, :] = f0[0:low, y, :] + fix[0:low]
             f0[high_x:wide, y, :] = f0[high_x:wide, y, :] + fix[high_x:wide]
 
@@ -452,7 +459,11 @@
 
             def put(x, total):
                 past = before(x) if j > 1 else None
-                now[x] = next_basis(j, diag(x), root(x), here(x), total, past)
+                new = next_basis(j, diag(x), root(x), here(x), total, past)
+                if j < S:
+                    now[x] = new
+                elif DEEP <= x < DEEP + nx:
+                    now[x, DEEP : DEEP + ny] = new[DEEP : DEEP + ny]
 
             for lo, hi in ((j, low + j), (high_x - j, wide - j)):
                 sweep(root, here, lo, hi, put)

time: 44.3 us -> 44.1 us (level)
  no operation moved by 1% of the time
where the time goes in v6:
time: 44.1 us; the launch traced here: 43.9 us
  blocking collectives  18.8 us (43%)
  Pallas kernels  14.6 us (33%)
  starting transfers between devices  6.62 us (15%)
  other arithmetic  1.69 us (4%)
  waiting for transfers between devices  1.47 us (3%)
  between operations  0.74 us (2%)
    all_to_all x1, blocking collectives, totals(): return lax.all_to_all(parts, ('gx', 'gy'), 0, 0)  18.8 us
    pallas_call x5, Pallas kernels, call(): pl.pallas_call(kernel, out_shape=[jax.ShapeDtypeStruct(s, k) for s, k in...  14.6 us
    ppermute x6, starting transfers between devices, exchange(): got.append(lax.ppermute(cells, axis, links))  6.62 us
    transpose x1, other arithmetic, body(): cells = jnp.transpose(jnp.stack([leaf_density, absorption]), (0, 2, 3, 1))  1.69 us
    ppermute x6, waiting for transfers between devices, exchange(): got.append(lax.ppermute(cells, axis, links))  1.47 us
  transfers between devices with their start and end apart: 6, of which 1 were waited for; matrix products, arithmetic and copies ran while one was open for 0% of the time, Pallas kernels for 8%

profile of v6, /device:TPU:0, one launch (start us, length us, event | category | flops | bytes accessed | tf_op | source)
XLA Modules:
  0.0 43.9 jit_solution(16868831104947626976)
XLA Ops:
  0.6 1.7 %maximum_bitcast_fusion.refs_2_ = f32[2,16,16,32]{3,2,1,0:T(8,128)} fusion(f32[1,32,16,16]{1,3,2,0:T(8,128)} %bitcast.6, f32[1,32,16,16]{1,3,2,0:T(8,128)} %bitcast.7), kind=kLoop, calls=%fused_computation | loop fusion | flops 16384 | bytes 131072 | tf_op jit(solution)/shard_map/transpose | solution.py:664
  2.3 1.8 %shard_map.59 = (f32[32,256]{1,0:T(8,128)S(1)}, f32[32,256]{1,0:T(8,128)S(1)}, f32[32,16,128]{2,1,0:T(8,128)S(1)}, f32[2,16,128]{2,1,0:T(8,128)S(1)}, f32[2,32,1...) custom-call(s32[1]{0:T(128)} %bitcast.1.px, ...), custom_call_target="tpu_custom_call" | custom-call | tf_op jit(solution)/shard_map/pallas_call | solution.py:620
  4.1 3.1 %collective-permute-start = (f32[200,128]{1,0:T(8,128)S(1)}, f32[200,128]{1,0:T(8,128)S(1)}, u32[]{:S(2)}, u32[]{:S(2)}) collective-permute-start(f32[200,128]{1,0:T(8,128)S(1)} %get-tuple-element.25), channel_id=1, source_target_pairs={{0,8},{8,0},{16,24},{24,16},{1,9},{9,1},{17,25},{25,17},{2,10},{10... | collective-permute-start | bytes 307208 | tf_op jit(solution)/shard_map/ppermute | solution.py:640
  7.2 0.7 %collective-permute-start.1 = (f32[200,128]{1,0:T(8,128)S(1)}, f32[200,128]{1,0:T(8,128)S(1)}, u32[]{:S(2)}, u32[]{:S(2)}) collective-permute-start(f32[200,128]{1,0:T(8,128)S(1)} %get-tuple-element.26), channel_id=1, source_target_pairs={{8,16},{16,8},{9,17},{17,9},{10,18},{18,10},{11,19},{19,11},{12,20... | collective-permute-start | bytes 307208 | tf_op jit(solution)/shard_map/ppermute | solution.py:640
  7.9 0.1 collective-permute-start.4
  8.0 0.7 %collective-permute-start.5 = (f32[336,128]{1,0:T(8,128)S(1)}, f32[336,128]{1,0:T(8,128)S(1)}, u32[]{:S(2)}, u32[]{:S(2)}) collective-permute-start(f32[336,128]{1,0:T(8,128)S(1)} %get-tuple-element.39), channel_id=1, source_target_pairs={{1,2},{2,1},{3,4},{4,3},{5,6},{6,5},{9,10},{10,9},{11,12},{12,11},... | collective-permute-start | bytes 516104 | tf_op jit(solution)/shard_map/ppermute | solution.py:640
  8.6 1.5 %collective-permute-done.recv_a = f32[200,128]{1,0:T(8,128)S(1)} collective-permute-done((f32[200,128]{1,0:T(8,128)S(1)}, f32[200,128]{1,0:T(8,128)S(1)}, u32[]{:S(2)}, u32[]{:S(2)}) %collective-permute-start) | collective-permute-done | bytes 102432 | tf_op jit(solution)/shard_map/ppermute | solution.py:640
  10.1 0.0 collective-permute-done.1.recv_b
  10.1 0.2 shard_map.60
  10.3 1.5 %collective-permute-start.2 = (f32[200,128]{1,0:T(8,128)S(1)}, f32[200,128]{1,0:T(8,128)S(1)}, u32[]{:S(2)}, u32[]{:S(2)}) collective-permute-start(f32[200,128]{1,0:T(8,128)S(1)} %get-tuple-element.32), channel_id=1, source_target_pairs={{0,1},{1,0},{2,3},{3,2},{4,5},{5,4},{6,7},{7,6},{8,9},{9,8},{10,11... | collective-permute-start | bytes 307208 | tf_op jit(solution)/shard_map/ppermute | solution.py:640
  11.8 0.7 %collective-permute-start.3 = (f32[200,128]{1,0:T(8,128)S(1)}, f32[200,128]{1,0:T(8,128)S(1)}, u32[]{:S(2)}, u32[]{:S(2)}) collective-permute-start(f32[200,128]{1,0:T(8,128)S(1)} %get-tuple-element.33), channel_id=1, source_target_pairs={{1,2},{2,1},{3,4},{4,3},{5,6},{6,5},{9,10},{10,9},{11,12},{12,11},... | collective-permute-start | bytes 307208 | tf_op jit(solution)/shard_map/ppermute | solution.py:640
  12.5 0.0 collective-permute-done.4.side_a
  12.5 0.0 collective-permute-done.5.side_b
  12.5 3.3 %shard_map.61 = (f32[32,32,128]{2,1,0:T(8,128)S(1)}, f32[32,32,128]{2,1,0:T(8,128)S(1)}, f32[9,32,32,128]{3,2,1,0:T(8,128)S(1)}, f32[2,32,128]{2,1,0:T(8,128)S(1)}) custom-call(s32[1]{0:T(128)} %bitcast.py, f32[336,128]{1,0:T(8,128)S(1)} %collective-permute-done.4.side_a, f32[336,128]{1,0:T(8,128)S(1)} %collective-permute-done.5.side_b, ...), custom_call_target="tpu_custom_call" | custom-call | tf_op jit(solution)/shard_map/pallas_call | solution.py:620
  15.8 0.0 collective-permute-done.2.recv_a
  15.8 0.0 collective-permute-done.3.recv_b
  15.9 0.0 copy-start
  15.9 4.9 %shard_map.62 = (bf16[512,1152]{1,0:T(8,128)(2,1)S(1)}, bf16[512,1152]{1,0:T(8,128)(2,1)S(1)}, f32[32,8,128]{2,1,0:T(8,128)S(1)}) custom-call(s32[1]{0:T(128)} %bitcast.py, f32[200,128]{1,0:T(8,128)S(1)} %collective-permute-done.2.recv_a, f32[200,128]{1,0:T(8,128)S(1)} %collective-permute-done.3.recv_b, f32[2,8,256]{2,1,0:T(8,128)S(1)} %get-tuple-element.34.root_h, ...), custom_call_target="tpu_custom_call" | custom-call | tf_op jit(solution)/shard_map/pallas_call | solution.py:620
  20.8 18.8 %all_to_all.5.parts = f32[32,8,128]{2,1,0:T(8,128)S(1)} all-to-all(f32[32,8,128]{2,1,0:T(8,128)S(1)} %get-tuple-element.47), channel_id=1, replica_groups=mesh['gx'=4,'gy'=8] {'gx','gy'}, dimensions={0} | all-to-all | bytes 262144 | tf_op jit(solution)/shard_map/all_to_all | solution.py:658
  39.5 0.0 copy-done
  39.5 4.3 %shard_map.63 = (f32[32,16,128]{2,1,0:T(8,128)}, f32[32,16,128]{2,1,0:T(8,128)}) custom-call(f32[32,16,128]{2,1,0:T(8,128)S(1)} %copy-done, bf16[512,1152]{1,0:T(8,128)(2,1)S(1)} %get-tuple-element.45.rough, bf16[512,1152]{1,0:T(8,128)(2,1)S(1)} %get-tuple-element.46.fine, f32[32,8,128]{2,1,0:T(8,128)S(1)} %all_to_all.5.parts), custom_call_target="tpu_custom_call" | custom-call | tf_op jit(solution)/shard_map/pallas_call | solution.py:620
Async XLA Ops:
  4.1 6.0 %collective-permute-start = (f32[200,128]{1,0:T(8,128)S(1)}, f32[200,128]{1,0:T(8,128)S(1)}, u32[]{:S(2)}, u32[]{:S(2)}) collective-permute-start(f32[200,128]{1,0:T(8,128)S(1)} %get-tuple-element.25), channel_id=1, source_target_pairs={{0,8},{8,0},{16,24},{24,16},{1,9},{9,1},{17,25},{25,17},{2,10},{10... | collective-permute-start | bytes 307208 | tf_op jit(solution)/shard_map/ppermute | solution.py:640
  7.2 2.9 %collective-permute-start.1 = (f32[200,128]{1,0:T(8,128)S(1)}, f32[200,128]{1,0:T(8,128)S(1)}, u32[]{:S(2)}, u32[]{:S(2)}) collective-permute-start(f32[200,128]{1,0:T(8,128)S(1)} %get-tuple-element.26), channel_id=1, source_target_pairs={{8,16},{16,8},{9,17},{17,9},{10,18},{18,10},{11,19},{19,11},{12,20... | collective-permute-start | bytes 307208 | tf_op jit(solution)/shard_map/ppermute | solution.py:640
  7.9 4.6 %collective-permute-start.4 = (f32[336,128]{1,0:T(8,128)S(1)}, f32[336,128]{1,0:T(8,128)S(1)}, u32[]{:S(2)}, u32[]{:S(2)}) collective-permute-start(f32[336,128]{1,0:T(8,128)S(1)} %get-tuple-element.38), channel_id=1, source_target_pairs={{0,1},{1,0},{2,3},{3,2},{4,5},{5,4},{6,7},{7,6},{8,9},{9,8},{10,11... | collective-permute-start | bytes 516104 | tf_op jit(solution)/shard_map/ppermute | solution.py:640
  8.0 4.5 %collective-permute-start.5 = (f32[336,128]{1,0:T(8,128)S(1)}, f32[336,128]{1,0:T(8,128)S(1)}, u32[]{:S(2)}, u32[]{:S(2)}) collective-permute-start(f32[336,128]{1,0:T(8,128)S(1)} %get-tuple-element.39), channel_id=1, source_target_pairs={{1,2},{2,1},{3,4},{4,3},{5,6},{6,5},{9,10},{10,9},{11,12},{12,11},... | collective-permute-start | bytes 516104 | tf_op jit(solution)/shard_map/ppermute | solution.py:640
  10.3 5.5 %collective-permute-start.2 = (f32[200,128]{1,0:T(8,128)S(1)}, f32[200,128]{1,0:T(8,128)S(1)}, u32[]{:S(2)}, u32[]{:S(2)}) collective-permute-start(f32[200,128]{1,0:T(8,128)S(1)} %get-tuple-element.32), channel_id=1, source_target_pairs={{0,1},{1,0},{2,3},{3,2},{4,5},{5,4},{6,7},{7,6},{8,9},{9,8},{10,11... | collective-permute-start | bytes 307208 | tf_op jit(solution)/shard_map/ppermute | solution.py:640
  11.8 4.0 %collective-permute-start.3 = (f32[200,128]{1,0:T(8,128)S(1)}, f32[200,128]{1,0:T(8,128)S(1)}, u32[]{:S(2)}, u32[]{:S(2)}) collective-permute-start(f32[200,128]{1,0:T(8,128)S(1)} %get-tuple-element.33), channel_id=1, source_target_pairs={{1,2},{2,1},{3,4},{4,3},{5,6},{6,5},{9,10},{10,9},{11,12},{12,11},... | collective-permute-start | bytes 307208 | tf_op jit(solution)/shard_map/ppermute | solution.py:640
  15.9 23.7 %copy-start = (f32[32,16,128]{2,1,0:T(8,128)S(1)}, f32[32,16,128]{2,1,0:T(8,128)}, u32[]{:S(2)}) copy-start(f32[32,16,128]{2,1,0:T(8,128)} %guess.1) | copy-start | bytes 786436

commit v7 on v6

--- a/solution.py
+++ b/solution.py
@@ -633,12 +633,13 @@
 def exchange(first, second, axis):
     count = lax.axis_size(axis)
     got = []
-    for cells, start in ((first, 0), (second, 1)):
+    order = ((first, 0), (second, 1))
+    for cells, start in order[::-1] if axis == "gx" else order:
         links = []
         for i in range(start, count - 1, 2):
             links += [(i, i + 1), (i + 1, i)]
         got.append(lax.ppermute(cells, axis, links))
-    return got
+    return got[::-1] if axis == "gx" else got
 
 
 def total_of(x, axis):

time: 44.1 us -> 44.1 us (level)
  no operation moved by 1% of the time
where the time goes in v7:
time: 44.1 us; the launch traced here: 43.9 us
  blocking collectives  18.8 us (43%)
  Pallas kernels  14.6 us (33%)
  starting transfers between devices  6.62 us (15%)
  other arithmetic  1.69 us (4%)
  waiting for transfers between devices  1.47 us (3%)
  between operations  0.74 us (2%)
    all_to_all x1, blocking collectives, totals(): return lax.all_to_all(parts, ('gx', 'gy'), 0, 0)  18.8 us
    pallas_call x5, Pallas kernels, call(): pl.pallas_call(kernel, out_shape=[jax.ShapeDtypeStruct(s, k) for s, k in...  14.6 us
    ppermute x6, starting transfers between devices, exchange(): got.append(lax.ppermute(cells, axis, links))  6.62 us
    transpose x1, other arithmetic, body(): cells = jnp.transpose(jnp.stack([leaf_density, absorption]), (0, 2, 3, 1))  1.69 us
    ppermute x6, waiting for transfers between devices, exchange(): got.append(lax.ppermute(cells, axis, links))  1.47 us
  transfers between devices with their start and end apart: 6, of which 1 were waited for; matrix products, arithmetic and copies ran while one was open for 0% of the time, Pallas kernels for 8%

profile of v7, /device:TPU:0, one launch (start us, length us, event | category | flops | bytes accessed | tf_op | source)
XLA Modules:
  0.0 43.9 jit_solution(16868831104947626976)
XLA Ops:
  0.6 1.7 %maximum_bitcast_fusion.refs_2_ = f32[2,16,16,32]{3,2,1,0:T(8,128)} fusion(f32[1,32,16,16]{1,3,2,0:T(8,128)} %bitcast.6, f32[1,32,16,16]{1,3,2,0:T(8,128)} %bitcast.7), kind=kLoop, calls=%fused_computation | loop fusion | flops 16384 | bytes 131072 | tf_op jit(solution)/shard_map/transpose | solution.py:665
  2.3 1.8 %shard_map.59 = (f32[32,256]{1,0:T(8,128)S(1)}, f32[32,256]{1,0:T(8,128)S(1)}, f32[32,16,128]{2,1,0:T(8,128)S(1)}, f32[2,16,128]{2,1,0:T(8,128)S(1)}, f32[2,32,1...) custom-call(s32[1]{0:T(128)} %bitcast.1.px, ...), custom_call_target="tpu_custom_call" | custom-call | tf_op jit(solution)/shard_map/pallas_call | solution.py:620
  4.1 3.1 %collective-permute-start = (f32[200,128]{1,0:T(8,128)S(1)}, f32[200,128]{1,0:T(8,128)S(1)}, u32[]{:S(2)}, u32[]{:S(2)}) collective-permute-start(f32[200,128]{1,0:T(8,128)S(1)} %get-tuple-element.25), channel_id=1, source_target_pairs={{0,8},{8,0},{16,24},{24,16},{1,9},{9,1},{17,25},{25,17},{2,10},{10... | collective-permute-start | bytes 307208 | tf_op jit(solution)/shard_map/ppermute | solution.py:641
  7.2 0.7 %collective-permute-start.1 = (f32[200,128]{1,0:T(8,128)S(1)}, f32[200,128]{1,0:T(8,128)S(1)}, u32[]{:S(2)}, u32[]{:S(2)}) collective-permute-start(f32[200,128]{1,0:T(8,128)S(1)} %get-tuple-element.26), channel_id=1, source_target_pairs={{8,16},{16,8},{9,17},{17,9},{10,18},{18,10},{11,19},{19,11},{12,20... | collective-permute-start | bytes 307208 | tf_op jit(solution)/shard_map/ppermute | solution.py:641
  7.9 0.1 collective-permute-start.4
  8.0 0.7 %collective-permute-start.5 = (f32[336,128]{1,0:T(8,128)S(1)}, f32[336,128]{1,0:T(8,128)S(1)}, u32[]{:S(2)}, u32[]{:S(2)}) collective-permute-start(f32[336,128]{1,0:T(8,128)S(1)} %get-tuple-element.39), channel_id=1, source_target_pairs={{1,2},{2,1},{3,4},{4,3},{5,6},{6,5},{9,10},{10,9},{11,12},{12,11},... | collective-permute-start | bytes 516104 | tf_op jit(solution)/shard_map/ppermute | solution.py:641
  8.6 1.5 %collective-permute-done.recv_a = f32[200,128]{1,0:T(8,128)S(1)} collective-permute-done((f32[200,128]{1,0:T(8,128)S(1)}, f32[200,128]{1,0:T(8,128)S(1)}, u32[]{:S(2)}, u32[]{:S(2)}) %collective-permute-start) | collective-permute-done | bytes 102432 | tf_op jit(solution)/shard_map/ppermute | solution.py:641
  10.1 0.0 collective-permute-done.1.recv_b
  10.1 0.2 shard_map.60
  10.3 1.5 %collective-permute-start.2 = (f32[200,128]{1,0:T(8,128)S(1)}, f32[200,128]{1,0:T(8,128)S(1)}, u32[]{:S(2)}, u32[]{:S(2)}) collective-permute-start(f32[200,128]{1,0:T(8,128)S(1)} %get-tuple-element.32), channel_id=1, source_target_pairs={{0,1},{1,0},{2,3},{3,2},{4,5},{5,4},{6,7},{7,6},{8,9},{9,8},{10,11... | collective-permute-start | bytes 307208 | tf_op jit(solution)/shard_map/ppermute | solution.py:641
  11.8 0.7 %collective-permute-start.3 = (f32[200,128]{1,0:T(8,128)S(1)}, f32[200,128]{1,0:T(8,128)S(1)}, u32[]{:S(2)}, u32[]{:S(2)}) collective-permute-start(f32[200,128]{1,0:T(8,128)S(1)} %get-tuple-element.33), channel_id=1, source_target_pairs={{1,2},{2,1},{3,4},{4,3},{5,6},{6,5},{9,10},{10,9},{11,12},{12,11},... | collective-permute-start | bytes 307208 | tf_op jit(solution)/shard_map/ppermute | solution.py:641
  12.5 0.0 collective-permute-done.4.side_a
  12.5 0.0 collective-permute-done.5.side_b
  12.5 3.3 %shard_map.61 = (f32[32,32,128]{2,1,0:T(8,128)S(1)}, f32[32,32,128]{2,1,0:T(8,128)S(1)}, f32[9,32,32,128]{3,2,1,0:T(8,128)S(1)}, f32[2,32,128]{2,1,0:T(8,128)S(1)}) custom-call(s32[1]{0:T(128)} %bitcast.py, f32[336,128]{1,0:T(8,128)S(1)} %collective-permute-done.4.side_a, f32[336,128]{1,0:T(8,128)S(1)} %collective-permute-done.5.side_b, ...), custom_call_target="tpu_custom_call" | custom-call | tf_op jit(solution)/shard_map/pallas_call | solution.py:620
  15.8 0.0 collective-permute-done.2.recv_a
  15.8 0.0 collective-permute-done.3.recv_b
  15.9 0.0 copy-start
  15.9 4.9 %shard_map.62 = (bf16[512,1152]{1,0:T(8,128)(2,1)S(1)}, bf16[512,1152]{1,0:T(8,128)(2,1)S(1)}, f32[32,8,128]{2,1,0:T(8,128)S(1)}) custom-call(s32[1]{0:T(128)} %bitcast.py, f32[200,128]{1,0:T(8,128)S(1)} %collective-permute-done.2.recv_a, f32[200,128]{1,0:T(8,128)S(1)} %collective-permute-done.3.recv_b, f32[2,8,256]{2,1,0:T(8,128)S(1)} %get-tuple-element.34.root_h, ...), custom_call_target="tpu_custom_call" | custom-call | tf_op jit(solution)/shard_map/pallas_call | solution.py:620
  20.8 18.8 %all_to_all.5.parts = f32[32,8,128]{2,1,0:T(8,128)S(1)} all-to-all(f32[32,8,128]{2,1,0:T(8,128)S(1)} %get-tuple-element.47), channel_id=1, replica_groups=mesh['gx'=4,'gy'=8] {'gx','gy'}, dimensions={0} | all-to-all | bytes 262144 | tf_op jit(solution)/shard_map/all_to_all | solution.py:659
  39.5 0.0 copy-done
  39.5 4.3 %shard_map.63 = (f32[32,16,128]{2,1,0:T(8,128)}, f32[32,16,128]{2,1,0:T(8,128)}) custom-call(f32[32,16,128]{2,1,0:T(8,128)S(1)} %copy-done, bf16[512,1152]{1,0:T(8,128)(2,1)S(1)} %get-tuple-element.45.rough, bf16[512,1152]{1,0:T(8,128)(2,1)S(1)} %get-tuple-element.46.fine, f32[32,8,128]{2,1,0:T(8,128)S(1)} %all_to_all.5.parts), custom_call_target="tpu_custom_call" | custom-call | tf_op jit(solution)/shard_map/pallas_call | solution.py:620
Async XLA Ops:
  4.1 6.0 %collective-permute-start = (f32[200,128]{1,0:T(8,128)S(1)}, f32[200,128]{1,0:T(8,128)S(1)}, u32[]{:S(2)}, u32[]{:S(2)}) collective-permute-start(f32[200,128]{1,0:T(8,128)S(1)} %get-tuple-element.25), channel_id=1, source_target_pairs={{0,8},{8,0},{16,24},{24,16},{1,9},{9,1},{17,25},{25,17},{2,10},{10... | collective-permute-start | bytes 307208 | tf_op jit(solution)/shard_map/ppermute | solution.py:641
  7.2 2.9 %collective-permute-start.1 = (f32[200,128]{1,0:T(8,128)S(1)}, f32[200,128]{1,0:T(8,128)S(1)}, u32[]{:S(2)}, u32[]{:S(2)}) collective-permute-start(f32[200,128]{1,0:T(8,128)S(1)} %get-tuple-element.26), channel_id=1, source_target_pairs={{8,16},{16,8},{9,17},{17,9},{10,18},{18,10},{11,19},{19,11},{12,20... | collective-permute-start | bytes 307208 | tf_op jit(solution)/shard_map/ppermute | solution.py:641
  7.9 4.6 %collective-permute-start.4 = (f32[336,128]{1,0:T(8,128)S(1)}, f32[336,128]{1,0:T(8,128)S(1)}, u32[]{:S(2)}, u32[]{:S(2)}) collective-permute-start(f32[336,128]{1,0:T(8,128)S(1)} %get-tuple-element.38), channel_id=1, source_target_pairs={{0,1},{1,0},{2,3},{3,2},{4,5},{5,4},{6,7},{7,6},{8,9},{9,8},{10,11... | collective-permute-start | bytes 516104 | tf_op jit(solution)/shard_map/ppermute | solution.py:641
  8.0 4.5 %collective-permute-start.5 = (f32[336,128]{1,0:T(8,128)S(1)}, f32[336,128]{1,0:T(8,128)S(1)}, u32[]{:S(2)}, u32[]{:S(2)}) collective-permute-start(f32[336,128]{1,0:T(8,128)S(1)} %get-tuple-element.39), channel_id=1, source_target_pairs={{1,2},{2,1},{3,4},{4,3},{5,6},{6,5},{9,10},{10,9},{11,12},{12,11},... | collective-permute-start | bytes 516104 | tf_op jit(solution)/shard_map/ppermute | solution.py:641
  10.3 5.5 %collective-permute-start.2 = (f32[200,128]{1,0:T(8,128)S(1)}, f32[200,128]{1,0:T(8,128)S(1)}, u32[]{:S(2)}, u32[]{:S(2)}) collective-permute-start(f32[200,128]{1,0:T(8,128)S(1)} %get-tuple-element.32), channel_id=1, source_target_pairs={{0,1},{1,0},{2,3},{3,2},{4,5},{5,4},{6,7},{7,6},{8,9},{9,8},{10,11... | collective-permute-start | bytes 307208 | tf_op jit(solution)/shard_map/ppermute | solution.py:641
  11.8 4.0 %collective-permute-start.3 = (f32[200,128]{1,0:T(8,128)S(1)}, f32[200,128]{1,0:T(8,128)S(1)}, u32[]{:S(2)}, u32[]{:S(2)}) collective-permute-start(f32[200,128]{1,0:T(8,128)S(1)} %get-tuple-element.33), channel_id=1, source_target_pairs={{1,2},{2,1},{3,4},{4,3},{5,6},{6,5},{9,10},{10,9},{11,12},{12,11},... | collective-permute-start | bytes 307208 | tf_op jit(solution)/shard_map/ppermute | solution.py:641
  15.9 23.7 %copy-start = (f32[32,16,128]{2,1,0:T(8,128)S(1)}, f32[32,16,128]{2,1,0:T(8,128)}, u32[]{:S(2)}) copy-start(f32[32,16,128]{2,1,0:T(8,128)} %guess.1) | copy-start | bytes 786436
